TPU v7x, 32 devices: a whole 2x2x4 slice. The times are simulated.
32 devices in a mesh: rep: 4 (over y, core), fsdp: 8 (over z, x).
Axes of the slice: x: 2, y: 2, z: 4, core: 2. Of those that a mesh axis runs over, the one named last changes fastest.
Arguments:
- tokens: bfloat16 [64, 512, 768], P(('rep', 'fsdp')), may hold values from -6 to 6
- encoder_states: bfloat16 [64, 512, 768], P(('rep', 'fsdp')), may hold values from -6 to 6
- cotangent: bfloat16 [64, 512, 768], P(('rep', 'fsdp')), may hold values from -6 to 6
- qkv_weight: bfloat16 [1, 2, 3, 768, 768], P(None, None, None, 'fsdp'), may hold values from -0.109375 to 0.109375
- out_weight: bfloat16 [1, 2, 768, 768], P(None, None, 'fsdp'), may hold values from -0.625 to 0.625
- ffin_weight: bfloat16 [1, 2, 768, 2048], P(None, None, 'fsdp'), may hold values from -0.21875 to 0.21875
- ffout_weight: bfloat16 [1, 2048, 768], P(None, 'fsdp'), may hold values from -0.125 to 0.125
- norm_gains: bfloat16 [1, 3, 768], P(None, None, 'fsdp'), may hold values from 0.3984375 to 1.59375
- bias_table: bfloat16 [32, 12], P('fsdp'), may hold values from -4 to 4
- lengths: int32 [64], P(('rep', 'fsdp')), may hold values from 65 to 512, as said below
- enc_lengths: int32 [64], P(('rep', 'fsdp')), may hold values from 65 to 512, as said below
Outputs:
- output_state: float32 [64, 512, 768], P(('rep', 'fsdp'))
- token_grad: float32 [64, 512, 768], P(('rep', 'fsdp'))
- encoder_grad: float32 [64, 512, 768], P(('rep', 'fsdp'))
- qkv_grad: float32 [1, 2, 3, 768, 768], P(None, None, None, 'fsdp')
- out_grad: float32 [1, 2, 768, 768], P(None, None, 'fsdp')
- ffin_grad: float32 [1, 2, 768, 2048], P(None, None, 'fsdp')
- ffout_grad: float32 [1, 2048, 768], P(None, 'fsdp')
- gain_grad: float32 [1, 3, 768], P(None, None, 'fsdp')
- table_grad: float32 [32, 12], P('fsdp')
Inputs may be any that keep to these rules, and one draw needn't show every extreme that they name: `lengths`: some sequence has exactly 512 live tokens. `enc_lengths`: some sequence has exactly 512 live encoder states.
All inputs are finite; a program needn't handle non-finite values.
Results may differ from a plain program's by a relative error of at most 0.024.
The roundings to bfloat16 on the way count: a program that leaves them out, or rounds other values in their place, can miss the bound.
Values may be sent and summed in bfloat16 or wider, within the bound.
No kernel may reach another device: no remote copies, remote signals or barrier semaphores. Data moves between devices by JAX's collectives and lax.ppermute only.
A program may use at most 256 MiB of HBM per device.

v0:
```python
import jax
import jax.numpy as jnp
from jax import lax
from jax.sharding import PartitionSpec as P

H = 12
NB = 32
DECODER_LAYERS = 1


EPS = 1e-06
NEGATIVE = -1e30
STEPS = (19, 21, 24, 27, 31, 35, 40, 46, 52, 59, 67, 77, 87, 99, 113)


def buckets(extent):
    position = jnp.arange(extent, dtype=jnp.int32)
    distance = jnp.maximum(position[:, None] - position[None, :], 0)
    far_bucket = 16 + sum(((distance >= border).astype(jnp.int32) for border in STEPS))
    return jnp.where(distance < 16, distance, far_bucket)


def rms_scale(values, factor):
    return values * lax.rsqrt(jnp.mean(values * values, axis=-1, keepdims=True) + EPS) * factor


def rms_back(values, factor, grad_out):
    pullback = jax.vjp(rms_scale, values, factor)[1]
    return pullback(grad_out)


def geglu(gate_in, upward_in):
    return jax.nn.gelu(gate_in, approximate=True) * upward_in


def project(left_operand, right_operand):
    return jnp.einsum(
        "vgq,qy->vgy", left_operand, right_operand, preferred_element_type=jnp.float32
    )


def project_back(left_operand, right_operand):
    return jnp.einsum(
        "gjr,fr->gjf", left_operand, right_operand, preferred_element_type=jnp.float32
    )


def weight_grad(left_operand, right_operand):
    return jnp.einsum(
        "nou,noi->ui", left_operand, right_operand, preferred_element_type=jnp.float32
    )


def split_heads(values):
    return values.reshape(values.shape[0], values.shape[1], H, values.shape[2] // H)


def merge_heads(values):
    return values.reshape(values.shape[0], values.shape[1], values.shape[2] * values.shape[3])


def attention_scores(queries, key_heads, extra_bias, allowed):
    scores = (
        jnp.einsum(
            "sqhd,skhd->shqk",
            split_heads(queries),
            split_heads(key_heads),
            preferred_element_type=jnp.float32,
        )
        + extra_bias
    )
    return jnp.where(allowed[:, None], scores, NEGATIVE)


def attend_forward(query_in, key_in, matrices, extra_bias, allowed):
    w_query, w_key, w_value, w_output = matrices
    queries = project(query_in, w_query).astype(jnp.bfloat16)
    key_heads = project(key_in, w_key).astype(jnp.bfloat16)
    value_heads = project(key_in, w_value).astype(jnp.bfloat16)
    scores = attention_scores(queries, key_heads, extra_bias, allowed)
    top_score = jnp.max(scores, axis=-1, keepdims=True)
    expanded = jnp.exp(scores - top_score)
    totals = jnp.sum(expanded, axis=-1, keepdims=True)
    chances = (expanded / totals).astype(jnp.bfloat16)
    mixture = jnp.einsum(
        "shqk,skhd->sqhd", chances, split_heads(value_heads), preferred_element_type=jnp.float32
    )
    mixture = merge_heads(mixture).astype(jnp.bfloat16)
    branch = project(mixture, w_output)
    log_total = top_score + jnp.log(totals)
    return (branch, (queries, key_heads, value_heads, mixture, log_total))


def attend_backward(branch_gradient, query_in, key_in, matrices, kept, extra_bias, allowed):
    w_query, w_key, w_value, w_output = matrices
    queries, key_heads, value_heads, mixture, log_total = kept
    grad_low = branch_gradient.astype(jnp.bfloat16)
    grad_output_w = weight_grad(mixture, grad_low)
    grad_mixture = project_back(grad_low, w_output).astype(jnp.bfloat16)
    scores = attention_scores(queries, key_heads, extra_bias, allowed)
    chances = jnp.exp(scores - log_total)
    grad_chances = jnp.einsum(
        "sqhd,skhd->shqk",
        split_heads(grad_mixture),
        split_heads(value_heads),
        preferred_element_type=jnp.float32,
    )
    grad_values = jnp.einsum(
        "shqk,sqhd->skhd",
        chances.astype(jnp.bfloat16),
        split_heads(grad_mixture),
        preferred_element_type=jnp.float32,
    )
    grad_values = merge_heads(grad_values).astype(jnp.bfloat16)
    grad_scores = chances * (grad_chances - jnp.sum(chances * grad_chances, axis=-1, keepdims=True))
    grad_scores = grad_scores.astype(jnp.bfloat16)
    grad_queries = jnp.einsum(
        "shqk,skhd->sqhd", grad_scores, split_heads(key_heads), preferred_element_type=jnp.float32
    )
    grad_queries = merge_heads(grad_queries).astype(jnp.bfloat16)
    grad_keys = jnp.einsum(
        "shqk,sqhd->skhd", grad_scores, split_heads(queries), preferred_element_type=jnp.float32
    )
    grad_keys = merge_heads(grad_keys).astype(jnp.bfloat16)
    grad_query_in = project_back(grad_queries, w_query)
    grad_key_in = project_back(grad_keys, w_key) + project_back(grad_values, w_value)
    matrix_grads = (
        weight_grad(query_in, grad_queries),
        weight_grad(key_in, grad_keys),
        weight_grad(key_in, grad_values),
        grad_output_w,
    )
    return (grad_query_in, grad_key_in, matrix_grads, grad_scores)


def layer_forward(stream, encoder_in, layer_weights, extra_bias, causal, visible):
    qkv_full, out_full, ffin_full, ffout_full, gains_full = layer_weights
    gains_wide = gains_full.astype(jnp.float32)
    normed_self = rms_scale(stream, gains_wide[0]).astype(jnp.bfloat16)
    branch, kept_self = attend_forward(
        normed_self,
        normed_self,
        (qkv_full[0, 0], qkv_full[0, 1], qkv_full[0, 2], out_full[0]),
        extra_bias,
        causal,
    )
    middle = stream + branch
    normed_cross = rms_scale(middle, gains_wide[1]).astype(jnp.bfloat16)
    branch, kept_cross = attend_forward(
        normed_cross,
        encoder_in,
        (qkv_full[1, 0], qkv_full[1, 1], qkv_full[1, 2], out_full[1]),
        0.0,
        visible,
    )
    later = middle + branch
    normed_feed = rms_scale(later, gains_wide[2]).astype(jnp.bfloat16)
    gate = project(normed_feed, ffin_full[0])
    upward = project(normed_feed, ffin_full[1])
    product = geglu(gate, upward).astype(jnp.bfloat16)
    result = later + project(product, ffout_full)
    kept = (
        stream,
        middle,
        later,
        normed_self,
        normed_cross,
        normed_feed,
        kept_self,
        kept_cross,
        gate,
        upward,
        product,
    )
    return (result, kept)


def layer_backward(
    grad_stream, encoder_in, layer_weights, kept, extra_bias, causal, visible, table_hot
):
    qkv_full, out_full, ffin_full, ffout_full, gains_full = layer_weights
    gains_wide = gains_full.astype(jnp.float32)
    (
        stream,
        middle,
        later,
        normed_self,
        normed_cross,
        normed_feed,
        kept_self,
        kept_cross,
        gate,
        upward,
        product,
    ) = kept
    grad_low = grad_stream.astype(jnp.bfloat16)
    grad_ffout = weight_grad(product, grad_low)
    grad_product = project_back(grad_low, ffout_full)
    grad_gate, grad_upward = jax.vjp(geglu, gate, upward)[1](grad_product)
    grad_gate = grad_gate.astype(jnp.bfloat16)
    grad_upward = grad_upward.astype(jnp.bfloat16)
    grad_ffin = jnp.stack(
        [weight_grad(normed_feed, grad_gate), weight_grad(normed_feed, grad_upward)]
    )
    grad_normed = project_back(grad_gate, ffin_full[0]) + project_back(grad_upward, ffin_full[1])
    grad_later_norm, grad_gain_feed = rms_back(later, gains_wide[2], grad_normed)
    grad_later = grad_stream + grad_later_norm
    cross_in, encoder_part, cross_grads, discarded_scores = attend_backward(
        grad_later,
        normed_cross,
        encoder_in,
        (qkv_full[1, 0], qkv_full[1, 1], qkv_full[1, 2], out_full[1]),
        kept_cross,
        0.0,
        visible,
    )
    grad_middle_norm, grad_gain_cross = rms_back(middle, gains_wide[1], cross_in)
    grad_middle = grad_later + grad_middle_norm
    self_attention_query, self_key, self_grads, grad_scores = attend_backward(
        grad_middle,
        normed_self,
        normed_self,
        (qkv_full[0, 0], qkv_full[0, 1], qkv_full[0, 2], out_full[0]),
        kept_self,
        extra_bias,
        causal,
    )
    grad_stream_norm, grad_gain_self = rms_back(
        stream, gains_wide[0], self_attention_query + self_key
    )
    grad_input = grad_middle + grad_stream_norm
    grad_table = jnp.einsum(
        "shqk,qkb->bh", grad_scores, table_hot, preferred_element_type=jnp.float32
    )
    grad_qkv = jnp.stack([jnp.stack(self_grads[:3]), jnp.stack(cross_grads[:3])])
    grad_out = jnp.stack([self_grads[3], cross_grads[3]])
    grad_gains = jnp.stack([grad_gain_self, grad_gain_cross, grad_gain_feed])
    return (
        grad_input,
        encoder_part,
        (grad_qkv, grad_out, grad_ffin, grad_ffout, grad_gains),
        grad_table,
    )


def per_device(
    tokens,
    encoder_states,
    cotangent,
    qkv_weight,
    out_weight,
    ffin_weight,
    ffout_weight,
    norm_gains,
    bias_table,
    lengths,
    enc_lengths,
):
    seq_count, seq_len = (tokens.shape[0], tokens.shape[1])
    enc_len = encoder_states.shape[1]
    position = jnp.arange(seq_len, dtype=jnp.int32)
    enc_position = jnp.arange(enc_len, dtype=jnp.int32)
    causal = (position[None, :] <= position[:, None])[None] & (
        position[None, None, :] < lengths[:, None, None]
    )
    visible = jnp.broadcast_to(
        enc_position[None, None, :] < enc_lengths[:, None, None], (seq_count, seq_len, enc_len)
    )
    live = (position[None, :] < lengths[:, None]).astype(jnp.float32)[:, :, None]
    bucket_index_grid = buckets(seq_len)
    table_wide = (
        bucket_index_grid[:, :, None] == jnp.arange(NB, dtype=jnp.int32)[None, None, :]
    ).astype(jnp.float32)
    table_hot = table_wide.astype(jnp.bfloat16)
    gathered = (
        lax.all_gather(qkv_weight, "fsdp", axis=3, tiled=True),
        lax.all_gather(out_weight, "fsdp", axis=2, tiled=True),
        lax.all_gather(ffin_weight, "fsdp", axis=2, tiled=True),
        lax.all_gather(ffout_weight, "fsdp", axis=1, tiled=True),
        lax.all_gather(norm_gains, "fsdp", axis=2, tiled=True),
        lax.all_gather(bias_table, "fsdp", axis=0, tiled=True),
    )
    extra_bias = jnp.einsum(
        "qkb,bh->hqk", table_wide, gathered[5].astype(jnp.float32), precision=lax.Precision.HIGHEST
    )
    stream = tokens.astype(jnp.float32)
    layer_index = 0
    layer_weights = tuple((member[layer_index] for member in gathered[:5]))
    stream, kept = layer_forward(stream, encoder_states, layer_weights, extra_bias, causal, visible)
    saved_layer_states = [kept]
    output_state = stream * live
    grad_stream = cotangent.astype(jnp.float32) * live
    grad_encoder = jnp.zeros(encoder_states.shape, jnp.float32)
    grad_table = jnp.zeros((NB, H), jnp.float32)
    layer_grads = [None] * DECODER_LAYERS
    for layer_index in reversed(range(DECODER_LAYERS)):
        layer_weights = (
            lax.all_gather(qkv_weight[layer_index], "fsdp", axis=2, tiled=True),
            lax.all_gather(out_weight[layer_index], "fsdp", axis=1, tiled=True),
            lax.all_gather(ffin_weight[layer_index], "fsdp", axis=1, tiled=True),
            lax.all_gather(ffout_weight[layer_index], "fsdp", axis=0, tiled=True),
            lax.all_gather(norm_gains[layer_index], "fsdp", axis=1, tiled=True),
        )
        grad_stream, encoder_part, matrix_grads, table_part = layer_backward(
            grad_stream,
            encoder_states,
            layer_weights,
            saved_layer_states[layer_index],
            extra_bias,
            causal,
            visible,
            table_hot,
        )
        grad_encoder = encoder_part
        grad_table = table_part
        layer_grads[layer_index] = matrix_grads
    stacked = tuple((jnp.stack([layer_grads[0][member_index]]) for member_index in range(5)))
    sharded = (
        lax.psum_scatter(stacked[0], "fsdp", scatter_dimension=3, tiled=True),
        lax.psum_scatter(stacked[1], "fsdp", scatter_dimension=2, tiled=True),
        lax.psum_scatter(stacked[2], "fsdp", scatter_dimension=2, tiled=True),
        lax.psum_scatter(stacked[3], "fsdp", scatter_dimension=1, tiled=True),
        lax.psum_scatter(stacked[4], "fsdp", scatter_dimension=2, tiled=True),
        lax.psum_scatter(grad_table, "fsdp", scatter_dimension=0, tiled=True),
    )
    summed = lax.psum(
        (sharded[0], sharded[1], sharded[2], sharded[3], sharded[4], sharded[5]), "rep"
    )
    qkv_grad, out_grad, ffin_grad, ffout_grad, gain_grad, table_grad = summed
    return (
        output_state,
        grad_stream,
        grad_encoder,
        qkv_grad,
        out_grad,
        ffin_grad,
        ffout_grad,
        gain_grad,
        table_grad,
    )


def solution(mesh):
    in_specs = (
        P(("rep", "fsdp"), None, None),
        P(("rep", "fsdp"), None, None),
        P(("rep", "fsdp"), None, None),
        P(None, None, None, "fsdp", None),
        P(None, None, "fsdp", None),
        P(None, None, "fsdp", None),
        P(None, "fsdp", None),
        P(None, None, "fsdp"),
        P("fsdp", None),
        P(("rep", "fsdp")),
        P(("rep", "fsdp")),
    )
    out_specs = (
        P(("rep", "fsdp"), None, None),
        P(("rep", "fsdp"), None, None),
        P(("rep", "fsdp"), None, None),
        P(None, None, None, "fsdp", None),
        P(None, None, "fsdp", None),
        P(None, None, "fsdp", None),
        P(None, "fsdp", None),
        P(None, None, "fsdp"),
        P("fsdp", None),
    )
    return jax.shard_map(
        per_device, mesh=mesh, in_specs=in_specs, out_specs=out_specs, check_vma=False
    )
```

profile of v0, /device:TPU:0, one launch (start us, length us, event | category | flops | bytes accessed | tf_op | source)
XLA Modules:
  0.0 1260.9 jit_solution(2233513824844103040)
XLA Ops:
  12.9 22.5 %all-gather.5 = bf16[8,4,12]{2,1,0:T(4,128)(2,1)S(1)} all-gather(bf16[1,4,12]{2,1,0:T(4,128)(2,1)S(1)} %bitcast.275), channel_id=1, replica_groups=mesh['rep'=4,'fsdp'=8] {'fsdp'}, dimensions={0}, use_global_device_ids=true | all-gather | bytes 864 | tf_op jit(solution)/shard_map/all_gather | solution.py:281
  35.5 32.3 %all_gather.33 = bf16[1,3,768]{1,0,2:T(2,128)(2,1)S(1)} all-gather(bf16[1,3,96]{1,0,2:T(2,128)(2,1)S(1)} %copy.150), channel_id=1, replica_groups=mesh['rep'=4,'fsdp'=8] {'fsdp'}, dimensions={2}, use_global_device_ids=true | all-gather | bytes 5184 | tf_op jit(solution)/shard_map/all_gather | solution.py:280
  85.8 46.2 %copy.154 = pred[512,512,32]{1,2,0:T(32,128)(4,1)} copy(pred[512,512,32]{0,2,1:T(32,128)(4,1)} %iota_compare_fusion) | data formatting | bytes 16777216 | tf_op jit(solution)/shard_map/eq | solution.py:272
  132.0 13.4 %convolution_bitcast_fusion = f32[12,512,512]{2,0,1:T(8,128)} fusion(pred[512,512,32]{1,2,0:T(32,128)(4,1)} %copy.154, bf16[32,12,1]{1,0,2:T(8,128)(2,1)S(1)} %bitcast.274), kind=kOutput, calls=%fused_computation.33 | convolution fusion | flops 201326592 | bytes 20972288 | tf_op jit(solution)/shard_map/qkb,bh->hqk/dot_general | solution.py:283
  145.4 18.1 %copy.156 = f32[12,512,512]{1,2,0:T(8,128)} copy(f32[12,512,512]{2,0,1:T(8,128)} %convolution_bitcast_fusion) | data formatting | bytes 25165824 | tf_op jit(solution)/shard_map/qkb,bh->hqk/dot_general | solution.py:283
  190.8 13.9 %fusion.92 = (f32[2,12,512]{2,1,0:T(8,128)S(1)}, f32[2,12,512,512]{2,3,1,0:T(8,128)}) fusion(f32[12,512,512]{1,2,0:T(8,128)} %copy.156, bf16[2,512,12,64]{1,3,2,0:T(8,128)(2,1)} %bitcast.238, bf16[2,512,12,64]{1,3,2,0:T(8,128)(2,1)S(1)} %bitcast.232, pred[2,512,512]{1,2,0:T(8,128)(4,1)} %broadcast_and_fusion), kind=kOutput, calls=%fused_computation.175 | convolution fusion | flops 824168448 | bytes 41467904 | tf_op jit(solution)/shard_map/sqhd,skhd->shqk/dot_general | solution.py:64
  215.6 12.9 %fusion.45 = bf16[2,12,64,512]{3,2,1,0:T(8,128)(2,1)} fusion(bf16[2,512,12,64]{1,3,2,0:T(8,128)(2,1)S(1)} %bitcast.245, f32[2,12,512,512]{2,3,1,0:T(8,128)} %get-tuple-element.32, f32[2,12,512]{2,1,0:T(8,128)S(1)} %fusion, f32[2,12,512]{2,1,0:T(8,128)S(1)} %get-tuple-element.31), kind=kOutput, calls=%fused_computation.94 | convolution fusion | flops 824967168 | bytes 28409856 | tf_op jit(solution)/shard_map/shqk,skhd->sqhd/dot_general | solution.py:85
  240.2 12.2 select_reduce_fusion
  263.5 11.6 fusion.44
  294.9 43.6 %all-gather.17.cloned.1.call-done = bf16[1,2048,768]{2,1,0:T(8,128)(2,1)} async-done(((bf16[1,256,768]{2,1,0:T(8,128)(2,1)}), bf16[1,2048,768]{2,1,0:T(8,128)(2,1)}) %all-gather.17.cloned.1.call-update) | async-done | bytes 3145744 | tf_op jit(solution)/shard_map/all_gather | solution.py:279
  338.5 16.0 %multiply_convert_fusion.2 = (bf16[2,512,2048]{2,1,0:T(8,128)(2,1)}, bf16[2,512,2048]{2,1,0:T(8,128)(2,1)S(1)}, bf16[2,512,2048]{2,1,0:T(8,128)(2,1)}) fusion(f32[2,512,2048]{2,1,0:T(8,128)} %fusion.38, f32[2,512,2048]{2,1,0:T(8,128)} %fusion.40, bf16[1,2048,768]{2,1,0:T(8,128)(2,1)} %all-gather.17.cloned.1.call-done, bf16[2,512,768]{2,1,0:T(8,128)(2,1)} %param.13, ...), kind=kOutput, calls=%fused_computation.41 | convolution fusion | flops 3278110720 | bytes 34082816 | tf_op jit(solution)/shard_map/gjr,fr->gjf/dot_general | solution.py:43
  378.2 18.2 %multiply_reduce_fusion.1 = (f32[2,12,512]{2,1,0:T(8,128)S(1)}, f32[2,12,512,512]{2,3,1,0:T(8,128)}) fusion(f32[2,12,512,512]{2,3,1,0:T(8,128)} %get-tuple-element.36, f32[2,12,512]{2,1,0:T(8,128)S(1)} %log_add_fusion.1, pred[2,512]{1,0:T(4,128)(4,1)S(1)} %iota_compare_fusion.2, bf16[2,512,12,64]{1,3,2,0:T(8,128)(2,1)} %bitcast.242, ...), kind=kOutput, calls=%fused_computation.7 | convolution fusion | flops 830459904 | bytes 53576704 | tf_op jit(solution)/shard_map/sqhd,skhd->shqk/dot_general | solution.py:102
  396.3 17.2 %multiply_convert_fusion.1 = bf16[2,12,512,512]{2,3,1,0:T(8,128)(2,1)S(1)} fusion(f32[2,12,512,512]{2,3,1,0:T(8,128)} %get-tuple-element.41, f32[2,12,512,512]{2,3,1,0:T(8,128)} %get-tuple-element.36, f32[2,12,512]{2,1,0:T(8,128)S(1)} %get-tuple-element.40, f32[2,12,512]{2,1,0:T(8,128)S(1)} %log_add_fusion.1, pred[2,512]{1,0:T(4,128)(4,1)S(1)} %iota_compare_fusion.2), kind=kLoop, calls=%fused_computation.6 | loop fusion | flops 31457280 | bytes 63013888 | tf_op jit(solution)/shard_map/convert_element_type | solution.py:116
  454.0 11.6 maximum_bitcast_fusion.1
  472.7 11.3 fusion.46
  498.5 12.0 fusion.49
  515.4 16.4 %multiply_reduce_fusion = (f32[2,12,512]{2,1,0:T(8,128)S(1)}, f32[2,12,512,512]{2,3,1,0:T(8,128)}) fusion(f32[2,12,512,512]{2,3,1,0:T(8,128)} %get-tuple-element.32, f32[2,12,512]{2,1,0:T(8,128)S(1)} %log_add_fusion, bf16[2,512,12,64]{1,3,2,0:T(8,128)(2,1)S(1)} %bitcast.237, bf16[2,512,12,64]{1,3,2,0:T(8,128)(2,1)} %bitcast.244), kind=kOutput, calls=%fused_computation.4 | convolution fusion | flops 824168448 | bytes 53575680 | tf_op jit(solution)/shard_map/sqhd,skhd->shqk/dot_general | solution.py:102
  531.8 26.7 %convert_reduce_fusion = (bf16[12,512,512]{1,2,0:T(8,128)(2,1)}, bf16[2,12,512,512]{2,3,1,0:T(8,128)(2,1)}) fusion(f32[2,12,512,512]{2,3,1,0:T(8,128)} %get-tuple-element.44, f32[2,12,512]{2,1,0:T(8,128)S(1)} %get-tuple-element.43, f32[2,12,512,512]{2,3,1,0:T(8,128)} %get-tuple-element.32, f32[2,12,512]{2,1,0:T(8,128)S(1)} %log_add_fusion), kind=kLoop, calls=%fused_computation.2 | loop fusion | flops 34603008 | bytes 69304320 | tf_op jit(solution)/shard_map/shqk,qkb->bh/reduce_sum | solution.py:232
  587.2 12.0 maximum_bitcast_fusion
  629.4 37.6 %all-reduce = f32[32,12]{1,0:T(8,128)S(1)} all-reduce(f32[32,12]{1,0:T(8,128)S(1)} %fusion.54), channel_id=7, replica_groups=mesh['rep'=4,'fsdp'=8] {'fsdp'}, use_global_device_ids=true, to_apply=%region_26.27.clone | all-reduce | flops 384 | bytes 3072
  667.0 188.4 %reduce-scatter.12.cloned.1.call-done = f32[1,2,96,2048]{3,2,1,0:T(8,128)} async-done(((f32[1,2,768,2048]{3,2,1,0:T(8,128)}), f32[1,2,96,2048]{3,2,1,0:T(8,128)}) %reduce-scatter.12.cloned.1.call-update) | async-done | bytes 1572880 | tf_op jit(solution)/shard_map/reduce_scatter | solution.py:321
  855.4 232.0 %reduce-scatter.8.cloned.1.call-done = f32[1,2,3,96,768]{4,3,2,1,0:T(8,128)} async-done(((f32[1,2,3,768,768]{4,3,2,1,0:T(8,128)}), f32[1,2,3,96,768]{4,3,2,1,0:T(8,128)}) %reduce-scatter.8.cloned.1.call-update) | async-done | bytes 1769488 | tf_op jit(solution)/shard_map/reduce_scatter | solution.py:319
  1103.8 48.0 %reduce-scatter.16.cloned.1.call-done = f32[96,3]{1,0:T(8,128)} async-done(((f32[768,3]{1,0:T(8,128)}), f32[96,3]{1,0:T(8,128)}) %reduce-scatter.16.cloned.1.call-update) | async-done | bytes 1168
  1159.0 88.8 %all-reduce.5.cloned.1.call-done = (f32[1,2,3,96,768]{4,3,2,1,0:T(8,128)}, f32[1,2,96,768]{3,2,1,0:T(8,128)}, f32[1,2,96,2048]{3,2,1,0:T(8,128)}, f32[1,256,768]{2,1,0:T(8,128)}) async-done(((f32[1,2,3,96,768]{4,3,2,1,0:T(8,128)}, f32[1,2,96,768]{3,2,1,0:T(8,128)}, f32[1,2,96,2048]{3,2,1,0:T(8,128)}, f32[1,256,768]{2,1,0:T(8,128)}), (f32[1,2,3,96,768]{4,3,2,1,0:T(8,128)}, f32[1,2,96,768]{3,2,1,0:T(8,128)}, ...) | async-done | bytes 4718608 | tf_op jit(solution)/shard_map/psum | solution.py:326
  (279 shorter events, 281.9 us)
Async XLA Ops:
  7.2 166.6 %copy-start = (bf16[2,512,768]{2,1,0:T(8,128)(2,1)S(1)}, bf16[2,512,768]{2,1,0:T(8,128)(2,1)}, u32[]{:S(2)}) copy-start(bf16[2,512,768]{2,1,0:T(8,128)(2,1)} %param.12) | copy-start | bytes 4718596
  7.2 28.1 %copy-start.72 = (bf16[1,3,96]{2,1,0:T(4,128)(2,1)S(1)}, bf16[1,3,96]{2,1,0:T(4,128)(2,1)}, u32[]{:S(2)}) copy-start(bf16[1,3,96]{2,1,0:T(4,128)(2,1)} %param.18) | copy-start | bytes 1732
  7.2 157.3 %all-gather.11.cloned.1.call-start = ((), (), s32[]{:S(2)}) async-start(), calls=%async_computation.5 | async-start | bytes 7962624 | tf_op jit(solution)/shard_map/all_gather | solution.py:276
  8.0 220.5 %all-gather.13.cloned.1.call-start = ((), (), s32[]{:S(2)}) async-start(), calls=%async_computation.6 | async-start | bytes 2654208 | tf_op jit(solution)/shard_map/all_gather | solution.py:277
  8.7 271.2 %all-gather.15.cloned.1.call-start = ((), (), s32[]{:S(2)}) async-start(), calls=%async_computation.7 | async-start | bytes 7077888 | tf_op jit(solution)/shard_map/all_gather | solution.py:278
  9.5 329.0 %all-gather.17.cloned.1.call-start = ((), (), s32[]{:S(2)}) async-start(), calls=%async_computation.8 | async-start | bytes 3538944 | tf_op jit(solution)/shard_map/all_gather | solution.py:279
  10.0 657.0 %reduce-scatter.10.cloned.1.call-start = ((), (), s32[]{:S(2)}) async-start(), calls=%async_computation.10 | async-start | bytes 5308416 | tf_op jit(solution)/shard_map/reduce_scatter | solution.py:320
  12.2 158.9 %copy-start.58 = (f32[2,512]{1,0:T(2,128)}, f32[2,512]{1,0:T(2,128)S(1)}, u32[]{:S(2)}) copy-start(f32[2,512]{1,0:T(2,128)S(1)} %fusion.80) | copy-start | bytes 12292
  76.0 95.2 %copy-start.56 = (f32[768]{0:T(1024)}, f32[768]{0:T(1024)S(1)}, u32[]{:S(2)}) copy-start(f32[768]{0:T(1024)S(1)} %get-tuple-element.17) | copy-start | bytes 9220
  76.0 156.0 %copy-start.62 = (f32[768]{0:T(1024)}, f32[768]{0:T(1024)S(1)}, u32[]{:S(2)}) copy-start(f32[768]{0:T(1024)S(1)} %get-tuple-element.16) | copy-start | bytes 9220
  215.6 12.9 %copy-start.9 = (bf16[2,512,768]{2,1,0:T(8,128)(2,1)S(1)}, bf16[2,512,768]{2,1,0:T(8,128)(2,1)}, u32[]{:S(2)}) copy-start(bf16[2,512,768]{2,1,0:T(8,128)(2,1)} %param.11) | copy-start | bytes 4718596
  263.5 11.7 copy-start.18
  263.5 11.7 copy-start.52
  289.1 49.3 %copy-start.66 = (f32[2,512]{1,0:T(2,128)S(1)}, f32[2,512]{1,0:T(2,128)}, u32[]{:S(2)}) copy-start(f32[2,512]{1,0:T(2,128)} %get-tuple-element.29) | copy-start | bytes 12292
  429.6 237.4 %reduce-scatter.14.cloned.1.call-start = ((), (), s32[]{:S(2)}) async-start(), calls=%async_computation.12 | async-start | bytes 7077888 | tf_op jit(solution)/shard_map/reduce_scatter | solution.py:322
  439.5 415.9 %reduce-scatter.12.cloned.1.call-start = ((), (), s32[]{:S(2)}) async-start(), calls=%async_computation.11 | async-start | bytes 14155776 | tf_op jit(solution)/shard_map/reduce_scatter | solution.py:321
  465.6 621.7 %reduce-scatter.8.cloned.1.call-start = ((), (), s32[]{:S(2)}) async-start(), calls=%async_computation.9 | async-start | bytes 15925248 | tf_op jit(solution)/shard_map/reduce_scatter | solution.py:319
  498.5 12.0 copy-start.57
  498.5 12.0 copy-start.59
  558.5 14.3 %slice-start = ((s8[12582912]{0:T(1024)(128)(4,1)}), s8[4194304]{0:T(1024)(128)(4,1)S(1)}, s32[]{:S(2)}) async-start(s8[12582912]{0:T(1024)(128)(4,1)} %bitcast.230), calls=%async_computation.15 | async-start | bytes 8388608
  558.5 14.3 %slice-start.1 = ((s8[12582912]{0:T(1024)(128)(4,1)}), s8[4194304]{0:T(1024)(128)(4,1)S(1)}, s32[]{:S(2)}) async-start(s8[12582912]{0:T(1024)(128)(4,1)} %bitcast.230), calls=%async_computation.16 | async-start | bytes 8388608
  599.2 552.5 %reduce-scatter.16.cloned.1.call-start = ((), (), s32[]{:S(2)}) async-start(), calls=%async_computation.13 | async-start | bytes 442368
  624.2 623.6 %all-reduce.5.cloned.1.call-start = ((), (), s32[]{:S(2)}) async-start(), calls=%async_computation.14 | async-start | bytes 9437184 | tf_op jit(solution)/shard_map/psum | solution.py:326
  629.4 458.0 %copy-start.61 = (f32[2,512]{1,0:T(2,128)S(1)}, f32[2,512]{1,0:T(2,128)}, u32[]{:S(2)}) copy-start(f32[2,512]{1,0:T(2,128)} %copy-done.60) | copy-start | bytes 12292
  (69 other events, 278.4 us)
Sparse Core Ops, SparseCore 0:
  10.3 114.8 all-gather.10
  127.3 50.6 all-gather.12
  180.2 97.5 all-gather.14
  279.8 58.6 all-gather.16
  429.8 94.0 reduce-scatter.9
  527.3 117.9 reduce-scatter.13
  648.9 206.4 reduce-scatter.11
  859.0 228.2 reduce-scatter.7
  1091.2 60.4 reduce-scatter.15
  1154.1 93.6 all-reduce.4
where the time goes:
time: 1270 us; the launch traced here: 1260 us
  waiting for transfers between devices  603 us (47%)
  matrix products  302 us (24%)
  local copies, waits for them, and re-layouts  122 us (10%)
  other arithmetic  117 us (9%)
  blocking collectives  98.7 us (8%)
  between operations  16.2 us (1%)
    reduce_scatter x1, waiting for transfers between devices, per_device(): lax.psum_scatter(stacked[0], 'fsdp', scatter_dimension=3, tiled=True)  232 us
    reduce_scatter x1, waiting for transfers between devices, per_device(): lax.psum_scatter(stacked[2], 'fsdp', scatter_dimension=2, tiled=True)  188 us
    psum x1, waiting for transfers between devices, per_device(): lax.psum((sharded[0], sharded[1], sharded[2], sharded[3], sharded[4], sha...  88.8 us
    dot_general x11, matrix products, project_back(): jnp.einsum('gjr,fr->gjf', left_operand, right_operand, preferred_element_...  62.6 us
    unnamed x11, waiting for transfers between devices  50.7 us
    eq x1, local copies, waits for them, and re-layouts, per_device(): bucket_index_grid[:, :, None]  46.2 us
    dot_general x11, matrix products, weight_grad(): jnp.einsum('nou,noi->ui', left_operand, right_operand, preferred_element_...  43.6 us
    all_gather x1, waiting for transfers between devices, per_device(): lax.all_gather(ffout_weight, 'fsdp', axis=1, tiled=True)  43.6 us
  transfers between devices with their start and end apart: 10, of which 5 were waited for; matrix products, arithmetic and copies ran while one was open for 34% of the time, Pallas kernels for 0%

commit v1 on v0

v1 whole, which is shorter than its diff:
```python
import functools

import jax
import jax.numpy as jnp
from jax import lax
from jax.experimental import pallas as pl
from jax.experimental.pallas import tpu as pltpu
from jax.sharding import PartitionSpec as P

EPS = 1e-06
STEPS = (19, 21, 24, 27, 31, 35, 40, 46, 52, 59, 67, 77, 87, 99, 113)


Z = 4


class Place:
    def __init__(self, rep, fsdp):
        self.rep, self.fsdp = rep, fsdp
        self.nx = fsdp // Z
        r = lax.axis_index("rep")
        f = lax.axis_index("fsdp")
        self.c, self.y = r % 2, (r // 2) % 2
        self.z, self.x = f // self.nx, f % self.nx
        self.q = 2 * self.y + self.c

    def core(self, v):
        return lax.ppermute(v, "rep", [(i, i ^ 1) for i in range(self.rep)])

    def across(self, v, bit):
        return lax.ppermute(v, "rep", [(i, i ^ bit) for i in range(self.rep)])

    def along_x(self, v, d):
        nx = self.nx
        return lax.ppermute(
            v, "fsdp", [(i, i // nx * nx + (i % nx + d) % nx) for i in range(self.fsdp)]
        )

    def along_z(self, v, d):
        return lax.ppermute(
            v, "fsdp", [(i, (i + d * self.nx) % self.fsdp) for i in range(self.fsdp)]
        )


def low(v):
    return v.astype(jnp.bfloat16)


def wide(v):
    return v.astype(jnp.float32)


def pick(v, i, axis=0):
    return lax.dynamic_index_in_dim(v, i, axis, keepdims=False)


def assemble_kernel(where_ref, *refs, parts, nx, kind):
    out = refs[-1]
    c, y, z, x = (where_ref[i] for i in range(4))
    for ref, (dc, dy, dx) in zip(refs, parts):
        core = c ^ dc
        row = y ^ dy
        col = lax.rem(x - dx + nx, nx)
        width = ref.shape[-1]
        for k in range(Z):
            f = lax.rem(z - k + Z, Z) * nx + col
            if kind == "matrix":
                out[2 * row + core, f] = ref[k]
            elif kind == "columns":
                out[row, f, :, pl.ds(pl.multiple_of(core * width, width), width)] = ref[k]
            else:
                out[f, core, :, pl.ds(pl.multiple_of(row * width, width), width)] = ref[k]


def gather_stage(place, piece, kind, y_last):
    rows, cols = piece.shape
    nx, fsdp = place.nx, place.fsdp
    stack = jnp.stack([piece] + [place.along_z(piece, d) for d in range(1, Z)])
    held = {(0, 0): stack}
    if y_last:
        for d in range(1, nx):
            held[0, d] = place.along_x(stack, d)
        for d in range(nx):
            held[1, d] = place.across(held[0, d], 2)
    else:
        held[1, 0] = place.across(stack, 2)
        for d in range(1, nx):
            for e in range(2):
                held[e, d] = place.along_x(held[e, 0], d)
    parts, arrays = [], []
    for (e, d), value in held.items():
        parts += [(0, e, d), (1, e, d)]
        arrays += [value, place.across(value, 1)]
    shape = {
        "matrix": (4, fsdp, rows, cols),
        "columns": (2, fsdp, rows, 2 * cols),
        "corners": (fsdp, 2, rows, 2 * cols),
    }[kind]
    where = jnp.stack([place.c, place.y, place.z, place.x]).astype(jnp.int32)
    return pl.pallas_call(
        functools.partial(assemble_kernel, parts=tuple(parts), nx=nx, kind=kind),
        out_shape=jax.ShapeDtypeStruct(shape, piece.dtype),
        in_specs=[pl.BlockSpec(memory_space=pltpu.SMEM)]
        + [pl.BlockSpec(memory_space=pltpu.VMEM)] * len(arrays),
        out_specs=pl.BlockSpec(memory_space=pltpu.VMEM),
        name="assemble_" + kind,
        compiler_params=pltpu.CompilerParams(vmem_limit_bytes=40 * 1024 * 1024),
        cost_estimate=pl.CostEstimate(
            flops=0, bytes_accessed=2 * 4 * fsdp * rows * cols * 2, transcendentals=0
        ),
    )(where, *arrays)


def gather_small(place, piece):
    nx = place.nx
    near = [piece] + [place.along_x(piece, nx - d) for d in range(1, nx)]
    near = jnp.roll(jnp.stack(near), place.x, axis=0)
    far = [near] + [place.along_z(near, Z - d) for d in range(1, Z)]
    return jnp.roll(jnp.stack(far), place.z, axis=0).reshape((place.fsdp,) + piece.shape)


def over_z(place, acc):
    total = pick(acc, place.z)
    for d in range(1, Z):
        total = total + wide(place.along_z(low(pick(acc, (place.z + d) % Z)), d))
    return total


def reduce_stage(place, sent, kept, y_first):
    nx = place.nx
    shape = (Z, nx) + sent[0].shape[1:]
    acc = [k + wide(place.across(s, 1)) for s, k in zip(sent, kept)]
    acc = [a.reshape(shape) for a in acc]
    own_y = place.y == 0
    if y_first:
        part = jnp.where(own_y, acc[0], acc[1])
        part = part + wide(place.across(low(jnp.where(own_y, acc[1], acc[0])), 2))
        total = pick(part, place.x, 1)
        for d in range(1, nx):
            total = total + wide(place.along_x(low(pick(part, (place.x + d) % nx, 1)), d))
    else:
        part = jnp.stack([pick(a, place.x, 1) for a in acc])
        for d in range(1, nx):
            away = (place.x + d) % nx
            part = part + wide(place.along_x(jnp.stack([low(pick(a, away, 1)) for a in acc]), d))
        total = pick(part, place.y) + wide(place.across(low(pick(part, 1 - place.y)), 2))
    total = over_z(place, total)
    bit = 4
    while bit < place.rep:
        total = total + place.across(total, bit)
        bit *= 2
    other = place.across(total, 2)
    pair = jnp.stack([jnp.where(own_y, total, other), jnp.where(own_y, other, total)])
    mate = place.across(pair, 1)
    by_core = (jnp.where(place.c == 0, pair, mate), jnp.where(place.c == 0, mate, pair))
    return [[by_core[c][y] for c in range(2)] for y in range(2)]


def reduce_small(place, partial):
    total = partial
    bit = 1
    while bit < place.rep:
        total = total + place.across(total, bit)
        bit *= 2
    total = total.reshape(Z, place.nx, -1)
    near = pick(total, place.x, 1)
    for d in range(1, place.nx):
        near = near + place.along_x(pick(total, (place.x + d) % place.nx, 1), d)
    mine = pick(near, place.z)
    for d in range(1, Z):
        mine = mine + place.along_z(pick(near, (place.z + d) % Z), d)
    return mine


NEGATIVE = -1e30
TILE = 256
PAIR = 128


def dot(a, b, dims):
    return lax.dot_general(a, b, (dims, ((), ())), preferred_element_type=jnp.float32)


NT = ((1,), (1,))
NN = ((1,), (0,))


def turned(v):
    return v.astype(jnp.float32).T


def half_mask(j):
    return lax.broadcasted_iota(jnp.int32, (1, PAIR), 1) // (PAIR // 2) == j


def masked_scores(k, qm, toe, length, t, causal):
    scores = dot(k, qm, NT)
    rows = scores.shape[0]
    key = lax.broadcasted_iota(jnp.int32, (rows, TILE), 0)
    if causal:
        bias = toe[:, :TILE]
        if t:
            bias = jnp.concatenate([toe[:, TILE:], bias], axis=0)
        scores = scores + bias
        query = lax.broadcasted_iota(jnp.int32, (rows, TILE), 1) + t * TILE
        allowed = key <= jnp.minimum(query, length - 1)
    else:
        allowed = key < length
    return jnp.where(allowed, scores, NEGATIVE)


def spread(row_ref, toe_ref):
    for j in range(2):
        row = jnp.broadcast_to(row_ref[0, j : j + 1, :], (TILE, 2 * TILE))
        toe_ref[j] = pltpu.roll(row, 0, 1, stride=1, stride_axis=0)


def forward_kernel(causal, len_ref, *refs):
    if causal:
        q_ref, k_ref, v_ref, row_ref, o_ref, lse_ref, toe_ref = refs
    else:
        q_ref, k_ref, v_ref, o_ref, lse_ref = refs
        toe_ref = None
    s = pl.program_id(1)
    length = len_ref[s]
    if causal:

        @pl.when(s == 0)
        def _():
            spread(row_ref, toe_ref)

    q, k, v = q_ref[0], k_ref[0], v_ref[0]
    v_turned = turned(v).astype(jnp.bfloat16)
    for t in range(q.shape[0] // TILE):
        seen = (t + 1) * TILE if causal else k.shape[0]
        here = slice(t * TILE, (t + 1) * TILE)
        outs = []
        for j in range(2):
            qm = jnp.where(half_mask(j), q[here], 0)
            scores = masked_scores(k[:seen], qm, toe_ref[j] if causal else None, length, t, causal)
            top = jnp.max(scores, axis=0, keepdims=True)
            grown = jnp.exp(scores - top)
            total = jnp.sum(grown, axis=0, keepdims=True)
            chances = (grown * (1.0 / total)).astype(jnp.bfloat16)
            lse_ref[0, 0, j : j + 1, here] = top + jnp.log(total)
            outs.append(dot(v_turned[j * 64 : (j + 1) * 64, :seen], chances, NN))
        o_ref[0, here, :] = turned(jnp.concatenate(outs, axis=0)).astype(jnp.bfloat16)


def diagonal_sums(v):
    width = v.shape[1]
    groups = v[:8]
    for a in range(8, v.shape[0], 8):
        groups = groups + pltpu.roll(v[a : a + 8], width - a, 1)
    total = groups[:1]
    for b in range(1, 8):
        total = total + pltpu.roll(groups[b : b + 1], width - b, 1)
    return total


def backward_kernel(causal, len_ref, *refs):
    if causal:
        q_ref, k_ref, v_ref, do_ref, lse_ref, row_ref = refs[:6]
        dq_ref, dk_ref, dv_ref, diag_ref, toe_ref, sum_ref = refs[6:]
    else:
        q_ref, k_ref, v_ref, do_ref, lse_ref = refs[:5]
        dq_ref, dk_ref, dv_ref = refs[5:]
        toe_ref = None
    s = pl.program_id(1)
    length = len_ref[s]
    if causal:

        @pl.when(s == 0)
        def _():
            spread(row_ref, toe_ref)
            sum_ref[...] = jnp.zeros_like(sum_ref)

    q, k, v, do = q_ref[0], k_ref[0], v_ref[0], do_ref[0]
    k_turned = turned(k).astype(jnp.bfloat16)
    tiles = q.shape[0] // TILE
    dk = [None] * tiles
    dv = [None] * tiles

    def add(held, value):
        return value if held is None else held + value

    for t in range(tiles):
        seen = (t + 1) * TILE if causal else k.shape[0]
        here = slice(t * TILE, (t + 1) * TILE)
        outs = []
        for j in range(2):
            qm = jnp.where(half_mask(j), q[here], 0)
            dom = jnp.where(half_mask(j), do[here], 0)
            scores = masked_scores(k[:seen], qm, toe_ref[j] if causal else None, length, t, causal)
            chances = jnp.exp(scores - lse_ref[0, 0, j : j + 1, here])
            d_chances = dot(v[:seen], dom, NT)
            delta = jnp.sum(chances * d_chances, axis=0, keepdims=True)
            d_scores = (chances * (d_chances - delta)).astype(jnp.bfloat16)
            outs.append(dot(k_turned[j * 64 : (j + 1) * 64, :seen], d_scores, NN))
            dv_part = dot(chances.astype(jnp.bfloat16), dom, NN)
            dk_part = dot(d_scores, qm, NN)
            for b in range(seen // TILE):
                rows = slice(b * TILE, (b + 1) * TILE)
                dv[b] = add(dv[b], dv_part[rows])
                dk[b] = add(dk[b], dk_part[rows])
            if causal:
                if t:
                    sum_ref[j, :, TILE:] += d_scores[: t * TILE].astype(jnp.float32)
                sum_ref[j, :, :TILE] += d_scores[t * TILE :].astype(jnp.float32)
        dq_ref[0, here, :] = turned(jnp.concatenate(outs, axis=0)).astype(jnp.bfloat16)
    for b in range(tiles):
        rows = slice(b * TILE, (b + 1) * TILE)
        dk_ref[0, rows, :] = dk[b].astype(jnp.bfloat16)
        dv_ref[0, rows, :] = dv[b].astype(jnp.bfloat16)
    if causal:

        @pl.when(s == pl.num_programs(1) - 1)
        def _():
            for j in range(2):
                diag_ref[0, j : j + 1, :] = diagonal_sums(sum_ref[j])


def attend(kind, q, k, v, lengths, row=None, do=None, lse=None):
    count, slots, width = q.shape
    pairs = width // PAIR
    assert slots == 2 * TILE and k.shape[1] == 2 * TILE
    block = pl.BlockSpec((1, slots, PAIR), lambda p, s: (s, 0, p))
    lse_block = pl.BlockSpec((1, 1, 2, slots), lambda p, s: (s, p, 0, 0))
    row_block = pl.BlockSpec((1, 2, slots), lambda p, s: (p, 0, 0))
    state = jax.ShapeDtypeStruct(q.shape, jnp.bfloat16)
    causal = row is not None
    ins, specs = [lengths, q, k, v], [pl.BlockSpec(memory_space=pltpu.SMEM), block, block, block]
    if kind == "forward":
        body = forward_kernel
        outs = [state, jax.ShapeDtypeStruct((count, pairs, 2, slots), jnp.float32)]
        out_specs = [block, lse_block]
        dots = 2
    else:
        body = backward_kernel
        ins += [do, lse]
        specs += [block, lse_block]
        outs = [state] * 3
        out_specs = [block] * 3
        dots = 5
    scratch = []
    if causal:
        ins.append(row)
        specs.append(row_block)
        scratch.append(pltpu.VMEM((2, TILE, 2 * TILE), jnp.float32))
        if kind == "backward":
            outs.append(jax.ShapeDtypeStruct(row.shape, jnp.float32))
            out_specs.append(row_block)
            scratch.append(pltpu.VMEM((2, TILE, 2 * TILE), jnp.float32))
    work = count * slots * slots * width
    return pl.pallas_call(
        functools.partial(body, causal),
        grid=(pairs, count),
        in_specs=specs,
        out_specs=out_specs,
        out_shape=outs,
        scratch_shapes=scratch,
        name=("self_" if causal else "cross_") + kind,
        compiler_params=pltpu.CompilerParams(vmem_limit_bytes=40 * 1024 * 1024),
        cost_estimate=pl.CostEstimate(
            flops=4 * dots * work, bytes_accessed=2 * q.size * 10, transcendentals=work // 64
        ),
    )(*ins)


def rms_scale(values, factor):
    return values * lax.rsqrt(jnp.mean(values * values, axis=-1, keepdims=True) + EPS) * factor


def rms_back(values, factor, grad_out):
    return jax.vjp(rms_scale, values, factor)[1](grad_out)


def geglu(gate_in, upward_in):
    return jax.nn.gelu(gate_in, approximate=True) * upward_in


def project(a, w):
    return jnp.einsum("vgq,qy->vgy", a, w, preferred_element_type=jnp.float32)


def project_back(a, w):
    return jnp.einsum("gjr,fr->gjf", a, w, preferred_element_type=jnp.float32)


def weight_grad(a, b):
    return jnp.einsum("nou,noi->ui", a, b, preferred_element_type=jnp.float32)


def bucket_hot(extent, buckets):
    distance = jnp.arange(extent, dtype=jnp.int32)
    far = 16 + sum(((distance >= border).astype(jnp.int32) for border in STEPS))
    bucket = jnp.where(distance < 16, distance, far)
    return (bucket[:, None] == jnp.arange(buckets, dtype=jnp.int32)).astype(jnp.float32)


def per_device(
    rep,
    fsdp,
    tokens,
    encoder_states,
    cotangent,
    qkv_weight,
    out_weight,
    ffin_weight,
    ffout_weight,
    norm_gains,
    bias_table,
    lengths,
    enc_lengths,
):
    place = Place(rep, fsdp)
    seq_len, width = tokens.shape[1:]
    table_rows, heads = bias_table.shape
    shard = qkv_weight.shape[3]
    first = place.c == 0

    def choose(a, b):
        return jnp.where(first, a, b)

    def attention_piece(i):
        return pick(jnp.concatenate([qkv_weight[0, i], out_weight[0, i : i + 1]]), place.q)

    self_w = gather_stage(place, attention_piece(0), "matrix", True)
    small_count = 3 * shard + table_rows * heads
    small = jnp.concatenate([norm_gains.reshape(-1), bias_table.reshape(-1)])
    small = gather_small(place, jnp.pad(small, (0, -small_count % 128)))
    gains = small[:, : 3 * shard].reshape(fsdp, 3, shard)
    gains = wide(jnp.transpose(gains, (1, 0, 2)).reshape(3, width))
    table = wide(small[:, 3 * shard : small_count].reshape(fsdp * table_rows, heads))
    cross_w = gather_stage(place, attention_piece(1), "matrix", False)
    half = ffin_weight.shape[3] // 2
    piece = lax.dynamic_slice(
        ffin_weight[0], (place.y, 0, place.c * half), (1, shard, half)
    )[0]
    ffin = gather_stage(place, piece, "columns", True)
    corner = (ffout_weight.shape[1] // 2, width // 2)
    piece = lax.dynamic_slice(
        ffout_weight[0], (place.c * corner[0], place.y * corner[1]), corner
    )
    ffout = gather_stage(place, piece, "corners", False)
    self_w = self_w.reshape(4, width, width)
    cross_w = cross_w.reshape(4, width, width)
    ffin = ffin.reshape(2, width, 2 * half)
    ffout = ffout.reshape(2 * half, width)

    live = wide(jnp.arange(seq_len, dtype=jnp.int32)[None, :] < lengths[:, None])[:, :, None]
    hot = bucket_hot(seq_len, fsdp * table_rows)
    row = jnp.einsum("nb,bh->hn", hot, table, precision=lax.Precision.HIGHEST)
    row = row.reshape(heads // 2, 2, seq_len)
    stream = wide(tokens)
    normed_self = low(rms_scale(stream, gains[0]))
    q1, k1, v1 = (low(project(normed_self, self_w[i])) for i in range(3))
    o1, lse1 = attend("forward", q1, k1, v1, lengths, row)
    middle = stream + project(o1, self_w[3])
    normed_cross = low(rms_scale(middle, gains[1]))
    q2 = low(project(normed_cross, cross_w[0]))
    k2, v2 = (low(project(encoder_states, cross_w[i])) for i in (1, 2))
    o2, lse2 = attend("forward", q2, k2, v2, enc_lengths)
    later = middle + project(o2, cross_w[3])
    normed_feed = low(rms_scale(later, gains[2]))
    gate = project(normed_feed, ffin[0])
    upward = project(normed_feed, ffin[1])
    product = low(geglu(gate, upward))
    output_state = (later + project(product, ffout)) * live

    grad = wide(cotangent) * live
    grad_low = low(grad)
    grad_product = project_back(grad_low, ffout)
    grad_gate, grad_upward = jax.vjp(geglu, gate, upward)[1](grad_product)
    grad_gate, grad_upward = low(grad_gate), low(grad_upward)
    cells = product.reshape(product.shape[:2] + (fsdp, 2, corner[0]))
    near, far = (cells[:, :, :, c].reshape(product.shape[:2] + (half,)) for c in range(2))

    def ffout_parts(left):
        return [
            weight_grad(left, grad_low[:, :, y * corner[1] : (y + 1) * corner[1]]).reshape(
                (fsdp,) + corner
            )
            for y in range(2)
        ]

    ffout_done = reduce_stage(
        place,
        [low(p) for p in ffout_parts(choose(far, near))],
        ffout_parts(choose(near, far)),
        True,
    )

    def ffin_parts(c_first):
        return [
            weight_grad(
                normed_feed, jnp.where(c_first, g[:, :, :half], g[:, :, half:])
            ).reshape(fsdp, shard, half)
            for g in (grad_gate, grad_upward)
        ]

    ffin_done = reduce_stage(
        place,
        [low(p) for p in ffin_parts(place.c == 1)],
        ffin_parts(first),
        False,
    )
    grad_normed = project_back(grad_gate, ffin[0]) + project_back(grad_upward, ffin[1])
    grad_norm, gain_feed = rms_back(later, gains[2], grad_normed)
    grad_later = grad + grad_norm

    def attention_parts(c_first, y0, y1):
        return [
            weight_grad(
                *(a if a is b else jnp.where(c_first, a, b) for a, b in zip(*both))
            ).reshape(fsdp, shard, width)
            for both in (y0, y1)
        ]

    def attention_reduce(y0, y1, y_first):
        return reduce_stage(
            place,
            [low(p) for p in attention_parts(place.c == 1, y0, y1)],
            attention_parts(first, y0, y1),
            y_first,
        )

    da = low(grad_later)
    do = low(project_back(da, cross_w[3]))
    dq, dk, dv = attend("backward", q2, k2, v2, enc_lengths, None, do, lse2)
    cross_done = attention_reduce(
        ((normed_cross, dq), (encoder_states, dk)), ((encoder_states, dv), (o2, da)), True
    )
    encoder_grad = project_back(dk, cross_w[1]) + project_back(dv, cross_w[2])
    grad_norm, gain_cross = rms_back(middle, gains[1], project_back(dq, cross_w[0]))
    grad_middle = grad_later + grad_norm

    da = low(grad_middle)
    do = low(project_back(da, self_w[3]))
    dq, dk, dv, diagonals = attend("backward", q1, k1, v1, lengths, row, do, lse1)
    self_done = attention_reduce(
        ((normed_self, dq), (normed_self, dk)), ((normed_self, dv), (o1, da)), False
    )
    into = project_back(dq, self_w[0]) + project_back(dk, self_w[1]) + project_back(dv, self_w[2])
    grad_norm, gain_self = rms_back(stream, gains[0], into)
    token_grad = grad_middle + grad_norm
    grad_table = jnp.einsum(
        "nb,hn->bh", hot, diagonals.reshape(heads, seq_len), precision=lax.Precision.HIGHEST
    )

    small = jnp.stack([gain_self, gain_cross, gain_feed]).reshape(3, fsdp, shard)
    small = jnp.concatenate(
        [
            jnp.transpose(small, (1, 0, 2)).reshape(fsdp, 3 * shard),
            grad_table.reshape(fsdp, table_rows * heads),
        ],
        axis=1,
    )
    small = reduce_small(place, jnp.pad(small, ((0, 0), (0, -small_count % 128))))

    done = (self_done, cross_done)
    qkv_grad = jnp.stack([jnp.stack([d[0][0], d[0][1], d[1][0]]) for d in done])[None]
    out_grad = jnp.stack([d[1][1] for d in done])[None]
    ffin_grad = jnp.stack([jnp.concatenate(g, axis=1) for g in ffin_done])[None]
    ffout_grad = jnp.concatenate(
        [jnp.concatenate([ffout_done[0][c], ffout_done[1][c]], axis=1) for c in range(2)]
    )[None]
    return (
        output_state,
        token_grad,
        encoder_grad,
        qkv_grad,
        out_grad,
        ffin_grad,
        ffout_grad,
        small[: 3 * shard].reshape(1, 3, shard),
        small[3 * shard : small_count].reshape(table_rows, heads),
    )


def solution(mesh):
    in_specs = (
        P(("rep", "fsdp"), None, None),
        P(("rep", "fsdp"), None, None),
        P(("rep", "fsdp"), None, None),
        P(None, None, None, "fsdp", None),
        P(None, None, "fsdp", None),
        P(None, None, "fsdp", None),
        P(None, "fsdp", None),
        P(None, None, "fsdp"),
        P("fsdp", None),
        P(("rep", "fsdp")),
        P(("rep", "fsdp")),
    )
    out_specs = (
        P(("rep", "fsdp"), None, None),
        P(("rep", "fsdp"), None, None),
        P(("rep", "fsdp"), None, None),
        P(None, None, None, "fsdp", None),
        P(None, None, "fsdp", None),
        P(None, None, "fsdp", None),
        P(None, "fsdp", None),
        P(None, None, "fsdp"),
        P("fsdp", None),
    )
    return jax.shard_map(
        functools.partial(per_device, mesh.shape["rep"], mesh.shape["fsdp"]),
        mesh=mesh, in_specs=in_specs, out_specs=out_specs, check_vma=False
    )
```

time: 1270 us -> 666 us (0.52)
  waiting for transfers between devices: 603 us -> 206 us
  matrix products: 302 us -> 124 us
  Pallas kernels: 0 us -> 125 us
  blocking collectives: 98.7 us -> 0 us
  other arithmetic: 117 us -> 26.6 us
  starting transfers between devices: 1.48 us -> 78.3 us
  local copies, waits for them, and re-layouts: 122 us -> 96.5 us
  between operations: 16.2 us -> 2.95 us
    reduce_scatter x4 -> x0, waiting for transfers between devices: 420 us -> none  [the longest x1 232 us: per_device(): lax.psum_scatter(stacked[0], 'fsdp', scatter_dimension=3, tiled=True)]
    ppermute x0 -> x86, waiting for transfers between devices: none -> 206 us  [the longest x44 95.6 us: across(): return lax.ppermute(v, 'rep', [(i, i ^ bit) for i in range(self.rep)])]
    dot_general x47 -> x40, matrix products: 302 us -> 124 us  [the longest x16 48.5 us: weight_grad(): return jnp.einsum('nou,noi->ui', a, b, preferred_element_type=jnp.float32)]
    pallas_call x0 -> x8, Pallas kernels: none -> 125 us  [the longest x4 119 us: attend(): pl.pallas_call(functools.partial(body, causal), grid=(pairs, count), in_s...]
    psum x1 -> x0, waiting for transfers between devices: 88.8 us -> none  [per_device(): lax.psum((sharded[0], sharded[1], sharded[2], sharded[3], sharded[4], sha...]
    ppermute x0 -> x86, starting transfers between devices: none -> 78.3 us  [the longest x30 50.4 us: along_z(): lax.ppermute(v, 'fsdp', [(i, (i + d * self.nx) % self.fsdp) for i in rang...]
    all_gather x2 -> x0, blocking collectives: 54.8 us -> none  [the longest x1 32.3 us: per_device(): lax.all_gather(norm_gains, 'fsdp', axis=2, tiled=True)]
    unnamed x11 -> x0, waiting for transfers between devices: 50.7 us -> none
  transfers between devices with their start and end apart: 10 -> 86, of which waited for: 5 -> 30; matrix products, arithmetic and copies ran while one was open for 34% -> 18% of each run, Pallas kernels for 0% -> 9%
where the time goes in v1:
time: 666 us; the launch traced here: 659 us
  waiting for transfers between devices  206 us (31%)
  Pallas kernels  125 us (19%)
  matrix products  124 us (19%)
  local copies, waits for them, and re-layouts  96.5 us (14%)
  starting transfers between devices  78.3 us (12%)
  other arithmetic  26.6 us (4%)
    pallas_call x4, Pallas kernels, attend(): pl.pallas_call(functools.partial(body, causal), grid=(pairs, count), in_s...  119 us
    ppermute x44, waiting for transfers between devices, across(): return lax.ppermute(v, 'rep', [(i, i ^ bit) for i in range(self.rep)])  95.6 us
    ppermute x12, waiting for transfers between devices, along_x(): lax.ppermute(v, 'fsdp', [(i, i // nx * nx + (i % nx + d) % nx) for i in r...  64.4 us
    ppermute x30, starting transfers between devices, along_z(): lax.ppermute(v, 'fsdp', [(i, (i + d * self.nx) % self.fsdp) for i in rang...  50.4 us
    dot_general x16, matrix products, weight_grad(): return jnp.einsum('nou,noi->ui', a, b, preferred_element_type=jnp.float32)  48.5 us
    unnamed x255, local copies, waits for them, and re-layouts  48.1 us
    ppermute x30, waiting for transfers between devices, along_z(): lax.ppermute(v, 'fsdp', [(i, (i + d * self.nx) % self.fsdp) for i in rang...  45.6 us
    dot_general x11, matrix products, project(): return jnp.einsum('vgq,qy->vgy', a, w, preferred_element_type=jnp.float32)  41.4 us
  transfers between devices with their start and end apart: 86, of which 30 were waited for; matrix products, arithmetic and copies ran while one was open for 18% of the time, Pallas kernels for 9%

profile of v1, /device:TPU:0, one launch (start us, length us, event | category | flops | bytes accessed | tf_op | source)
XLA Modules:
  0.0 658.7 jit_solution(14387388971413203907)
XLA Ops:
  37.4 9.5 %collective-permute-done.15 = bf16[96,768]{1,0:T(8,128)(2,1)S(1)} collective-permute-done((bf16[96,768]{1,0:T(8,128)(2,1)S(1)}, bf16[96,768]{1,0:T(8,128)(2,1)S(1)}, u32[]{:S(2)}, u32[]{:S(2)}) %collective-permute-start.15) | collective-permute-done | bytes 147488 | tf_op jit(solution)/shard_map/ppermute | solution.py:40
  74.4 9.1 %collective-permute-done.18.refs_2_ = bf16[4,96,768]{2,1,0:T(8,128)(2,1)} collective-permute-done((bf16[4,96,768]{2,1,0:T(8,128)(2,1)S(1)}, bf16[4,96,768]{2,1,0:T(8,128)(2,1)}, u32[]{:S(2)}, u32[]{:S(2)}) %collective-permute-start.18) | collective-permute-done | bytes 589856 | tf_op jit(solution)/shard_map/ppermute | solution.py:31
  88.7 9.8 %collective-permute-done.8.refs_2_ = bf16[4,96,768]{2,1,0:T(8,128)(2,1)} collective-permute-done((bf16[4,96,768]{2,1,0:T(8,128)(2,1)S(1)}, bf16[4,96,768]{2,1,0:T(8,128)(2,1)}, u32[]{:S(2)}, u32[]{:S(2)}) %collective-permute-start.8) | collective-permute-done | bytes 589856 | tf_op jit(solution)/shard_map/ppermute | solution.py:35
  99.7 7.1 %collective-permute-done.42.refs_6_ = bf16[4,128,384]{2,1,0:T(8,128)(2,1)S(1)} collective-permute-done((bf16[4,128,384]{2,1,0:T(8,128)(2,1)S(1)}, bf16[4,128,384]{2,1,0:T(8,128)(2,1)S(1)}, u32[]{:S(2)}, u32[]{:S(2)}) %collective-permute-start.42) | collective-permute-done | bytes 393248 | tf_op jit(solution)/shard_map/ppermute | solution.py:35
  112.7 6.8 %collective-permute-done.22.refs_6_ = bf16[4,96,768]{2,1,0:T(8,128)(2,1)} collective-permute-done((bf16[4,96,768]{2,1,0:T(8,128)(2,1)}, bf16[4,96,768]{2,1,0:T(8,128)(2,1)}, u32[]{:S(2)}, u32[]{:S(2)}) %collective-permute-start.22) | collective-permute-done | bytes 589856 | tf_op jit(solution)/shard_map/ppermute | solution.py:35
  155.8 7.9 %collective-permute-done.30.refs_4_ = bf16[4,96,1024]{2,1,0:T(8,128)(2,1)S(1)} collective-permute-done((bf16[4,96,1024]{2,1,0:T(8,128)(2,1)S(1)}, bf16[4,96,1024]{2,1,0:T(8,128)(2,1)S(1)}, u32[]{:S(2)}, u32[]{:S(2)}) %collective-permute-start.30) | collective-permute-done | bytes 786464 | tf_op jit(solution)/shard_map/ppermute | solution.py:31
  164.3 15.9 %collective-permute-done.32.refs_6_ = bf16[4,96,1024]{2,1,0:T(8,128)(2,1)S(1)} collective-permute-done((bf16[4,96,1024]{2,1,0:T(8,128)(2,1)S(1)}, bf16[4,96,1024]{2,1,0:T(8,128)(2,1)S(1)}, u32[]{:S(2)}, u32[]{:S(2)}) %collective-permute-start.32) | collective-permute-done | bytes 786464 | tf_op jit(solution)/shard_map/ppermute | solution.py:31
  188.1 26.3 %self_forward.1 = (bf16[2,512,768]{2,1,0:T(8,128)(2,1)S(1)}, f32[2,6,2,512]{3,2,1,0:T(2,128)S(1)}) custom-call(s32[2]{0:T(128)S(1)} %copy-done.27, bf16[2,512,768]{2,1,0:T(8,128)(2,1)S(1)} %convolution_convert_fusion.7.refs_0_, bf16[2,512,768]{2,1,0:T(8,128)(2,1)S(1)} %convolution_convert_fusion.6.refs_1_, ...), custom_call_target="tpu_custom_call" | custom-call | flops 3221225472 | bytes 15728640 | tf_op jit(solution)/shard_map/self_forward/pallas_call | solution.py:355
  222.5 27.8 %cross_forward.1 = (bf16[2,512,768]{2,1,0:T(8,128)(2,1)S(1)}, f32[2,6,2,512]{3,2,1,0:T(2,128)S(1)}) custom-call(s32[2]{0:T(128)S(1)} %copy-done.28, bf16[2,512,768]{2,1,0:T(8,128)(2,1)S(1)} %convolution_convert_fusion.4.refs_0_, bf16[2,512,768]{2,1,0:T(8,128)(2,1)S(1)} %fusion.84.refs_1_, bf16[2,512,768]{2,1,0:T(8,128)(2,1)S(1)} %fusion.85.refs_2_), custom_call_target="tpu_custom_call" | custom-call | flops 3221225472 | bytes 15728640 | tf_op jit(solution)/shard_map/cross_forward/pallas_call | solution.py:355
  261.1 15.6 %fusion.6 = (bf16[2,512,2048]{2,1,0:T(8,128)(2,1)}, bf16[2,512,2048]{2,1,0:T(8,128)(2,1)}, bf16[2,512,2048]{2,1,0:T(8,128)(2,1)}) fusion(f32[2,512,2048]{2,1,0:T(8,128)} %fusion.159, f32[2,512,2048]{2,1,0:T(8,128)} %fusion.158, bf16[2,512,768]{2,1,0:T(8,128)(2,1)} %copy-done.92, bf16[768,2048,1]{1,0,2:T(8,128)(2,1)S(1)} %bitcast.391), kind=kOutput, calls=%fused_computation.8 | convolution fusion | flops 3275751424 | bytes 34078720 | tf_op jit(solution)/shard_map/vgq,qy->vgy/dot_general | solution.py:383
  304.3 31.4 %cross_backward.1 = (bf16[2,512,768]{2,1,0:T(8,128)(2,1)S(1)}, bf16[2,512,768]{2,1,0:T(8,128)(2,1)S(1)}, bf16[2,512,768]{2,1,0:T(8,128)(2,1)S(1)}) custom-call(s32[2]{0:T(128)S(1)} %copy-done.28, bf16[2,512,768]{2,1,0:T(8,128)(2,1)S(1)} %copy-done.46, bf16[2,512,768]{2,1,0:T(8,128)(2,1)S(1)} %copy-done.42, bf16[2,512,768]{2,1,0:T(8,128)(2,1)S(1)} %copy-done.44, ...), custom_call_target="tpu_custom_call" | custom-call | flops 8053063680 | bytes 15728640 | tf_op jit(solution)/shard_map/cross_backward/pallas_call | solution.py:355
  343.5 33.8 %self_backward.1 = (bf16[2,512,768]{2,1,0:T(8,128)(2,1)S(1)}, bf16[2,512,768]{2,1,0:T(8,128)(2,1)S(1)}, bf16[2,512,768]{2,1,0:T(8,128)(2,1)S(1)}, f32[6,2,512]{2,1,0:T(2,128)S(1)}) custom-call(s32[2]{0:T(128)S(1)} %copy-done.27, bf16[2,512,768]{2,1,0:T(8,128)(2,1)S(1)} %copy-done.40, bf16[2,512,768]{2,1,0:T(8,128)(2,1)S(1)} %copy-done.38, ...), custom_call_target="tpu_custom_call" | custom-call | flops 8053063680 | bytes 15728640 | tf_op jit(solution)/shard_map/self_backward/pallas_call | solution.py:355
  404.4 7.9 %reshape.405 = bf16[2,512,8,2,128]{4,3,2,1,0:T(2,128)(2,1)} reshape(bf16[2,512,2048]{2,1,0:T(8,128)(2,1)} %get-tuple-element.49) | data formatting | bytes 8388608 | tf_op jit(solution)/shard_map/reshape | solution.py:476
  412.3 8.4 %add_multiply_fusion = f32[2,512,768]{2,1,0:T(8,128)} fusion(f32[2,512,768]{2,1,0:T(8,128)} %copy-done.47, bf16[2,512,2048]{2,1,0:T(8,128)(2,1)} %get-tuple-element.49, bf16[2048,768,1]{1,0,2:T(8,128)(2,1)S(1)} %bitcast.371, f32[2,512]{1,0:T(2,128)S(1)} %copy-done.111), kind=kOutput, calls=%fused_computation.41 | convolution fusion | flops 3222798336 | bytes 13635584 | tf_op jit(solution)/shard_map/vgq,qy->vgy/dot_general | solution.py:383
  423.8 10.0 %fusion.153 = (bf16[2,512,8,1,128]{4,3,2,1,0:T(2,128)(2,1)}, bf16[2,512,8,1,128]{4,3,2,1,0:T(2,128)(2,1)}) fusion(bf16[2,512,8,2,128]{4,3,2,1,0:T(2,128)(2,1)} %reshape.405), kind=kLoop, calls=%fused_computation.335 | loop fusion | bytes 8388608 | tf_op jit(solution)/shard_map/slice | solution.py:477
  433.8 10.5 %copy.102 = bf16[2,512,8,1,128]{1,4,2,0,3:T(8,128)(2,1)} copy(bf16[2,512,8,1,128]{4,3,2,1,0:T(2,128)(2,1)} %get-tuple-element.62) | data formatting | bytes 4194304
  444.3 10.5 %copy.103 = bf16[2,512,8,1,128]{1,4,2,0,3:T(8,128)(2,1)} copy(bf16[2,512,8,1,128]{4,3,2,1,0:T(2,128)(2,1)} %get-tuple-element.63) | data formatting | bytes 4194304
  499.1 14.7 %collective-permute-done.73 = bf16[4,2,128,384]{3,2,0,1:T(8,128)(2,1)S(1)} collective-permute-done((bf16[4,2,128,384]{3,2,0,1:T(8,128)(2,1)S(1)}, bf16[4,2,128,384]{3,2,0,1:T(8,128)(2,1)S(1)}, u32[]{:S(2)}, u32[]{:S(2)}) %collective-permute-start.73) | collective-permute-done | bytes 786464 | tf_op jit(solution)/shard_map/ppermute | solution.py:31
  518.6 12.1 %collective-permute-done.74 = bf16[4,128,384]{2,1,0:T(8,128)(2,1)S(1)} collective-permute-done((bf16[4,128,384]{2,1,0:T(8,128)(2,1)S(1)}, bf16[4,128,384]{2,1,0:T(8,128)(2,1)S(1)}, u32[]{:S(2)}, u32[]{:S(2)}) %collective-permute-start.74) | collective-permute-done | bytes 393248 | tf_op jit(solution)/shard_map/ppermute | solution.py:35
  550.9 12.2 %collective-permute-done.47 = bf16[4,96,768]{2,1,0:T(8,128)(2,1)S(1)} collective-permute-done((bf16[4,96,768]{2,1,0:T(8,128)(2,1)S(1)}, bf16[4,96,768]{2,1,0:T(8,128)(2,1)S(1)}, u32[]{:S(2)}, u32[]{:S(2)}) %collective-permute-start.47) | collective-permute-done | bytes 589856 | tf_op jit(solution)/shard_map/ppermute | solution.py:31
  568.4 22.0 %collective-permute-done.56 = bf16[4,96,768]{2,1,0:T(8,128)(2,1)S(1)} collective-permute-done((bf16[4,96,768]{2,1,0:T(8,128)(2,1)S(1)}, bf16[4,96,768]{2,1,0:T(8,128)(2,1)S(1)}, u32[]{:S(2)}, u32[]{:S(2)}) %collective-permute-start.56) | collective-permute-done | bytes 589856 | tf_op jit(solution)/shard_map/ppermute | solution.py:35
  606.2 19.7 %collective-permute-done.60 = f32[96,768]{1,0:T(8,128)S(1)} collective-permute-done((f32[96,768]{1,0:T(8,128)S(1)}, f32[96,768]{1,0:T(8,128)S(1)}, u32[]{:S(2)}, u32[]{:S(2)}) %collective-permute-start.60) | collective-permute-done | bytes 294944 | tf_op jit(solution)/shard_map/ppermute | solution.py:31
  636.1 7.5 %collective-permute-done.67 = bf16[96,1024]{1,0:T(8,128)(2,1)S(1)} collective-permute-done((bf16[96,1024]{1,0:T(8,128)(2,1)S(1)}, bf16[96,1024]{1,0:T(8,128)(2,1)S(1)}, u32[]{:S(2)}, u32[]{:S(2)}) %collective-permute-start.67) | collective-permute-done | bytes 196640 | tf_op jit(solution)/shard_map/ppermute | solution.py:40
  644.5 9.7 %collective-permute-done.69 = f32[96,1024]{1,0:T(8,128)S(1)} collective-permute-done((f32[96,1024]{1,0:T(8,128)S(1)}, f32[96,1024]{1,0:T(8,128)S(1)}, u32[]{:S(2)}, u32[]{:S(2)}) %collective-permute-start.69) | collective-permute-done | bytes 393248 | tf_op jit(solution)/shard_map/ppermute | solution.py:31
  (581 shorter events, 309.8 us)
Async XLA Ops:
  2.3 27.4 %collective-permute-start.34 = (bf16[128,384]{1,0:T(8,128)(2,1)}, bf16[128,384]{1,0:T(8,128)(2,1)}, u32[]{:S(2)}, u32[]{:S(2)}) collective-permute-start(bf16[128,384]{1,0:T(8,128)(2,1)} %fusion.209), channel_id=1, source_target_pairs={{0,2},{1,3},{2,4},{3,5},{4,6},{5,7},{6,0},{7,1},{8,10},{9,11},{10,... | collective-permute-start | bytes 294920 | tf_op jit(solution)/shard_map/ppermute | solution.py:40
  31.8 27.9 %collective-permute-start.5 = (bf16[96,768]{1,0:T(8,128)(2,1)S(1)}, bf16[96,768]{1,0:T(8,128)(2,1)S(1)}, u32[]{:S(2)}, u32[]{:S(2)}) collective-permute-start(bf16[96,768]{1,0:T(8,128)(2,1)S(1)} %bitcast.414), channel_id=1, source_target_pairs={{0,4},{1,5},{2,6},{3,7},{4,0},{5,1},{6,2},{7,3},{8,12},{9,13},{10,... | collective-permute-start | bytes 442376 | tf_op jit(solution)/shard_map/ppermute | solution.py:40
  87.2 32.3 %collective-permute-start.22 = (bf16[4,96,768]{2,1,0:T(8,128)(2,1)}, bf16[4,96,768]{2,1,0:T(8,128)(2,1)}, u32[]{:S(2)}, u32[]{:S(2)}) collective-permute-start(bf16[4,96,768]{2,1,0:T(8,128)(2,1)} %collective-permute-done.18.refs_2_), channel_id=1, source_target_pairs={{0,1},{1,0},{2,3},{3,2},{4,5},{5,4},{6,7},{7,6},{8,9},{9,8},{10,11... | collective-permute-start | bytes 1769480 | tf_op jit(solution)/shard_map/ppermute | solution.py:35
  108.8 34.5 %collective-permute-start.28 = (bf16[4,96,1024]{2,1,0:T(8,128)(2,1)S(1)}, bf16[4,96,1024]{2,1,0:T(8,128)(2,1)S(1)}, u32[]{:S(2)}, u32[]{:S(2)}) collective-permute-start(bf16[4,96,1024]{2,1,0:T(8,128)(2,1)S(1)} %pad_maximum_fusion.2.refs_0_), channel_id=1, source_target_pairs={{0,1},{1,0},{2,3},{3,2},{4,5},{5,4},{6,7},{7,6},{8,9},{9,8},{10,11... | collective-permute-start | bytes 2359304 | tf_op jit(solution)/shard_map/ppermute | solution.py:35
  110.6 33.3 %collective-permute-start.19 = (bf16[4,96,768]{2,1,0:T(8,128)(2,1)}, bf16[4,96,768]{2,1,0:T(8,128)(2,1)}, u32[]{:S(2)}, u32[]{:S(2)}) collective-permute-start(bf16[4,96,768]{2,1,0:T(8,128)(2,1)} %collective-permute-done.18.refs_2_), channel_id=1, source_target_pairs={{0,8},{8,0},{16,24},{24,16},{1,9},{9,1},{17,25},{25,17},{2,10},{10... | collective-permute-start | bytes 1769480 | tf_op jit(solution)/shard_map/ppermute | solution.py:31
  111.5 32.6 %collective-permute-start.21 = (bf16[4,96,768]{2,1,0:T(8,128)(2,1)}, bf16[4,96,768]{2,1,0:T(8,128)(2,1)}, u32[]{:S(2)}, u32[]{:S(2)}) collective-permute-start(bf16[4,96,768]{2,1,0:T(8,128)(2,1)} %collective-permute-done.20.refs_4_), channel_id=1, source_target_pairs={{0,8},{8,0},{16,24},{24,16},{1,9},{9,1},{17,25},{25,17},{2,10},{10... | collective-permute-start | bytes 1769480 | tf_op jit(solution)/shard_map/ppermute | solution.py:31
  112.7 31.7 %collective-permute-start.12 = (bf16[4,96,768]{2,1,0:T(8,128)(2,1)}, bf16[4,96,768]{2,1,0:T(8,128)(2,1)}, u32[]{:S(2)}, u32[]{:S(2)}) collective-permute-start(bf16[4,96,768]{2,1,0:T(8,128)(2,1)} %collective-permute-done.8.refs_2_), channel_id=1, source_target_pairs={{0,16},{8,24},{16,0},{24,8},{1,17},{9,25},{17,1},{25,9},{2,18},{10... | collective-permute-start | bytes 1769480 | tf_op jit(solution)/shard_map/ppermute | solution.py:31
  144.4 35.8 %collective-permute-start.32 = (bf16[4,96,1024]{2,1,0:T(8,128)(2,1)S(1)}, bf16[4,96,1024]{2,1,0:T(8,128)(2,1)S(1)}, u32[]{:S(2)}, u32[]{:S(2)}) collective-permute-start(bf16[4,96,1024]{2,1,0:T(8,128)(2,1)S(1)} %collective-permute-done.28.refs_2_), channel_id=1, source_target_pairs={{0,16},{8,24},{16,0},{24,8},{1,17},{9,25},{17,1},{25,9},{2,18},{10... | collective-permute-start | bytes 2359304 | tf_op jit(solution)/shard_map/ppermute | solution.py:31
  145.9 34.3 %collective-permute-start.13 = (bf16[4,96,768]{2,1,0:T(8,128)(2,1)}, bf16[4,96,768]{2,1,0:T(8,128)(2,1)S(1)}, u32[]{:S(2)}, u32[]{:S(2)}) collective-permute-start(bf16[4,96,768]{2,1,0:T(8,128)(2,1)} %collective-permute-done.12.refs_6_), channel_id=1, source_target_pairs={{0,8},{8,0},{16,24},{24,16},{1,9},{9,1},{17,25},{25,17},{2,10},{10... | collective-permute-start | bytes 1769480 | tf_op jit(solution)/shard_map/ppermute | solution.py:31
  163.7 88.5 %collective-permute-start.27 = (bf16[4,96,1024]{2,1,0:T(8,128)(2,1)S(1)}, bf16[4,96,1024]{2,1,0:T(8,128)(2,1)S(1)}, u32[]{:S(2)}, u32[]{:S(2)}) collective-permute-start(bf16[4,96,1024]{2,1,0:T(8,128)(2,1)S(1)} %pad_maximum_fusion.2.refs_0_), channel_id=1, source_target_pairs={{0,8},{8,0},{16,24},{24,16},{1,9},{9,1},{17,25},{25,17},{2,10},{10... | collective-permute-start | bytes 2359304 | tf_op jit(solution)/shard_map/ppermute | solution.py:31
  163.7 88.5 %collective-permute-start.29 = (bf16[4,96,1024]{2,1,0:T(8,128)(2,1)S(1)}, bf16[4,96,1024]{2,1,0:T(8,128)(2,1)S(1)}, u32[]{:S(2)}, u32[]{:S(2)}) collective-permute-start(bf16[4,96,1024]{2,1,0:T(8,128)(2,1)S(1)} %collective-permute-done.28.refs_2_), channel_id=1, source_target_pairs={{0,8},{8,0},{16,24},{24,16},{1,9},{9,1},{17,25},{25,17},{2,10},{10... | collective-permute-start | bytes 2359304 | tf_op jit(solution)/shard_map/ppermute | solution.py:31
  164.2 88.0 %collective-permute-start.31 = (bf16[4,96,1024]{2,1,0:T(8,128)(2,1)S(1)}, bf16[4,96,1024]{2,1,0:T(8,128)(2,1)S(1)}, u32[]{:S(2)}, u32[]{:S(2)}) collective-permute-start(bf16[4,96,1024]{2,1,0:T(8,128)(2,1)S(1)} %collective-permute-done.30.refs_4_), channel_id=1, source_target_pairs={{0,8},{8,0},{16,24},{24,16},{1,9},{9,1},{17,25},{25,17},{2,10},{10... | collective-permute-start | bytes 2359304 | tf_op jit(solution)/shard_map/ppermute | solution.py:31
  180.2 73.3 %collective-permute-start.33 = (bf16[4,96,1024]{2,1,0:T(8,128)(2,1)S(1)}, bf16[4,96,1024]{2,1,0:T(8,128)(2,1)S(1)}, u32[]{:S(2)}, u32[]{:S(2)}) collective-permute-start(bf16[4,96,1024]{2,1,0:T(8,128)(2,1)S(1)} %collective-permute-done.32.refs_6_), channel_id=1, source_target_pairs={{0,8},{8,0},{16,24},{24,16},{1,9},{9,1},{17,25},{25,17},{2,10},{10... | collective-permute-start | bytes 2359304 | tf_op jit(solution)/shard_map/ppermute | solution.py:31
  423.3 41.3 %collective-permute-start.80 = (f32[8,384]{1,0:T(8,128)S(1)}, f32[8,384]{1,0:T(8,128)S(1)}, u32[]{:S(2)}, u32[]{:S(2)}) collective-permute-start(f32[8,384]{1,0:T(8,128)S(1)} %select_maximum_fusion), channel_id=1, source_target_pairs={{0,8},{8,0},{16,24},{24,16},{1,9},{9,1},{17,25},{25,17},{2,10},{10... | collective-permute-start | bytes 36872 | tf_op jit(solution)/shard_map/ppermute | solution.py:31
  480.9 33.7 %collective-permute-start.62 = (bf16[8,96,1024]{2,1,0:T(8,128)(2,1)}, bf16[8,96,1024]{2,1,0:T(8,128)(2,1)}, u32[]{:S(2)}, u32[]{:S(2)}) collective-permute-start(bf16[8,96,1024]{2,1,0:T(8,128)(2,1)} %bitcast.114), channel_id=1, source_target_pairs={{0,8},{8,0},{16,24},{24,16},{1,9},{9,1},{17,25},{25,17},{2,10},{10... | collective-permute-start | bytes 4718600 | tf_op jit(solution)/shard_map/ppermute | solution.py:31
  490.9 27.1 %collective-permute-start.63 = (bf16[8,96,1024]{2,1,0:T(8,128)(2,1)S(1)}, bf16[8,96,1024]{2,1,0:T(8,128)(2,1)S(1)}, u32[]{:S(2)}, u32[]{:S(2)}) collective-permute-start(bf16[8,96,1024]{2,1,0:T(8,128)(2,1)S(1)} %bitcast.429), channel_id=1, source_target_pairs={{0,8},{8,0},{16,24},{24,16},{1,9},{9,1},{17,25},{25,17},{2,10},{10... | collective-permute-start | bytes 4718600 | tf_op jit(solution)/shard_map/ppermute | solution.py:31
  494.5 52.5 %collective-permute-start.46 = (bf16[2,4,96,768]{3,2,1,0:T(8,128)(2,1)S(1)}, bf16[2,4,96,768]{3,2,1,0:T(8,128)(2,1)S(1)}, u32[]{:S(2)}, u32[]{:S(2)}) collective-permute-start(bf16[2,4,96,768]{3,2,1,0:T(8,128)(2,1)S(1)} %pad_maximum_fusion.1), channel_id=1, source_target_pairs={{0,1},{1,0},{2,3},{3,2},{4,5},{5,4},{6,7},{7,6},{8,9},{9,8},{10,11... | collective-permute-start | bytes 3538952 | tf_op jit(solution)/shard_map/ppermute | solution.py:35
  497.3 51.6 %collective-permute-start.55 = (bf16[4,2,96,768]{3,2,0,1:T(8,128)(2,1)S(1)}, bf16[4,2,96,768]{3,2,0,1:T(8,128)(2,1)S(1)}, u32[]{:S(2)}, u32[]{:S(2)}) collective-permute-start(bf16[4,2,96,768]{3,2,0,1:T(8,128)(2,1)S(1)} %copy.57), channel_id=1, source_target_pairs={{0,16},{8,24},{16,0},{24,8},{1,17},{9,25},{17,1},{25,9},{2,18},{10... | collective-permute-start | bytes 3538952 | tf_op jit(solution)/shard_map/ppermute | solution.py:31
  542.8 53.8 %collective-permute-start.64 = (bf16[2,4,96,1024]{3,2,1,0:T(8,128)(2,1)S(1)}, bf16[2,4,96,1024]{3,2,1,0:T(8,128)(2,1)S(1)}, u32[]{:S(2)}, u32[]{:S(2)}) collective-permute-start(bf16[2,4,96,1024]{3,2,1,0:T(8,128)(2,1)S(1)} %pad_maximum_fusion), channel_id=1, source_target_pairs={{0,1},{1,0},{2,3},{3,2},{4,5},{5,4},{6,7},{7,6},{8,9},{9,8},{10,11... | collective-permute-start | bytes 4718600 | tf_op jit(solution)/shard_map/ppermute | solution.py:35
  549.2 41.2 %collective-permute-start.56 = (bf16[4,96,768]{2,1,0:T(8,128)(2,1)S(1)}, bf16[4,96,768]{2,1,0:T(8,128)(2,1)S(1)}, u32[]{:S(2)}, u32[]{:S(2)}) collective-permute-start(bf16[4,96,768]{2,1,0:T(8,128)(2,1)S(1)} %fusion.91), channel_id=1, source_target_pairs={{0,1},{1,0},{2,3},{3,2},{4,5},{5,4},{6,7},{7,6},{8,9},{9,8},{10,11... | collective-permute-start | bytes 1769480 | tf_op jit(solution)/shard_map/ppermute | solution.py:35
  563.3 30.0 %collective-permute-start.48 = (bf16[96,768]{1,0:T(8,128)(2,1)S(1)}, bf16[96,768]{1,0:T(8,128)(2,1)S(1)}, u32[]{:S(2)}, u32[]{:S(2)}) collective-permute-start(bf16[96,768]{1,0:T(8,128)(2,1)S(1)} %get-tuple-element.71), channel_id=1, source_target_pairs={{0,2},{1,3},{2,4},{3,5},{4,6},{5,7},{6,0},{7,1},{8,10},{9,11},{10,... | collective-permute-start | bytes 442376 | tf_op jit(solution)/shard_map/ppermute | solution.py:40
  566.0 28.1 %collective-permute-start.49 = (bf16[96,768]{1,0:T(8,128)(2,1)S(1)}, bf16[96,768]{1,0:T(8,128)(2,1)S(1)}, u32[]{:S(2)}, u32[]{:S(2)}) collective-permute-start(bf16[96,768]{1,0:T(8,128)(2,1)S(1)} %get-tuple-element.73), channel_id=1, source_target_pairs={{0,4},{1,5},{2,6},{3,7},{4,0},{5,1},{6,2},{7,3},{8,12},{9,13},{10,... | collective-permute-start | bytes 442376 | tf_op jit(solution)/shard_map/ppermute | solution.py:40
  567.0 29.0 %collective-permute-start.50 = (bf16[96,768]{1,0:T(8,128)(2,1)S(1)}, bf16[96,768]{1,0:T(8,128)(2,1)S(1)}, u32[]{:S(2)}, u32[]{:S(2)}) collective-permute-start(bf16[96,768]{1,0:T(8,128)(2,1)S(1)} %get-tuple-element.72), channel_id=1, source_target_pairs={{0,6},{1,7},{2,0},{3,1},{4,2},{5,3},{6,4},{7,5},{8,14},{9,15},{10,... | collective-permute-start | bytes 442376 | tf_op jit(solution)/shard_map/ppermute | solution.py:40
  597.3 28.8 %collective-permute-start.65 = (bf16[4,96,1024]{2,1,0:T(8,128)(2,1)S(1)}, bf16[4,96,1024]{2,1,0:T(8,128)(2,1)S(1)}, u32[]{:S(2)}, u32[]{:S(2)}) collective-permute-start(bf16[4,96,1024]{2,1,0:T(8,128)(2,1)S(1)} %fusion.87), channel_id=1, source_target_pairs={{0,16},{8,24},{16,0},{24,8},{1,17},{9,25},{17,1},{25,9},{2,18},{10... | collective-permute-start | bytes 2359304 | tf_op jit(solution)/shard_map/ppermute | solution.py:31
  (185 other events, 1827.0 us)

commit v2 on v1

v2 whole, which is shorter than its diff:
```python
import functools

import jax
import jax.numpy as jnp
from jax import lax
from jax.experimental import pallas as pl
from jax.experimental.pallas import tpu as pltpu
from jax.sharding import PartitionSpec as P

EPS = 1e-06
STEPS = (19, 21, 24, 27, 31, 35, 40, 46, 52, 59, 67, 77, 87, 99, 113)


Z = 4


class Place:
    def __init__(self, rep, fsdp):
        self.rep, self.fsdp = rep, fsdp
        self.nx = fsdp // Z
        r = lax.axis_index("rep")
        f = lax.axis_index("fsdp")
        self.c, self.y = r % 2, (r // 2) % 2
        self.z, self.x = f // self.nx, f % self.nx
        self.q = 2 * self.y + self.c

    def core(self, v):
        return lax.ppermute(v, "rep", [(i, i ^ 1) for i in range(self.rep)])

    def across(self, v, bit):
        return lax.ppermute(v, "rep", [(i, i ^ bit) for i in range(self.rep)])

    def along_x(self, v, d):
        nx = self.nx
        return lax.ppermute(
            v, "fsdp", [(i, i // nx * nx + (i % nx + d) % nx) for i in range(self.fsdp)]
        )

    def along_z(self, v, d):
        return lax.ppermute(
            v, "fsdp", [(i, (i + d * self.nx) % self.fsdp) for i in range(self.fsdp)]
        )


def low(v):
    return v.astype(jnp.bfloat16)


def wide(v):
    return v.astype(jnp.float32)


def pick(v, i, axis=0):
    return lax.dynamic_index_in_dim(v, i, axis, keepdims=False)


FREE = pl.CostEstimate(flops=0, bytes_accessed=0, transcendentals=0)


def lasting(microseconds):
    return pl.CostEstimate(
        flops=int(microseconds * 1e9), bytes_accessed=0, transcendentals=0
    )


VMEM = pl.BlockSpec(memory_space=pltpu.VMEM)
SMEM = pl.BlockSpec(memory_space=pltpu.SMEM)


def shape_of(shape, dtype=jnp.bfloat16):
    return jax.ShapeDtypeStruct(shape, dtype)


def call(body, ins, outs, name, waits=(), specs=None, vmem=32, cost=FREE, **kw):
    waits = list(waits)
    count, late = len(ins), len(ins) + len(waits)

    def kernel(*refs):
        body(*refs[:count], *refs[late:])

    return pl.pallas_call(
        kernel,
        in_specs=list(specs or [VMEM] * count) + [pl.BlockSpec(memory_space=pl.ANY)] * len(waits),
        out_shape=outs,
        name=name,
        compiler_params=pltpu.CompilerParams(vmem_limit_bytes=vmem * 1024 * 1024),
        cost_estimate=cost,
        **kw,
    )(*ins, *waits)


def stack_kernel(*refs):
    for k, ref in enumerate(refs[:-1]):
        refs[-1][k] = ref[...]


def copy_kernel(ref, out):
    out[...] = ref[...]


def stacked(values, waits=()):
    shape = shape_of((len(values),) + values[0].shape, values[0].dtype)
    return call(stack_kernel, values, shape, "stack", waits)


def held_back(value, waits):
    return call(copy_kernel, [value], shape_of(value.shape, value.dtype), "hold", waits)


LANES = 128
SMALL_ROWS = 16


def assemble_kernel(where_ref, *refs, parts, nx, sizes, small):
    outs = refs[len(parts) :]
    c, y, z, x = (where_ref[i] for i in range(4))
    for ref, (dc, dy, dx) in zip(refs, parts):
        core = c ^ dc
        row = y ^ dy
        col = lax.rem(x - dx + nx, nx)
        for k in range(Z):
            f = lax.rem(z - k + Z, Z) * nx + col
            at = 0
            for out, (m, h, w) in zip(outs, sizes):
                for t in range(w // LANES):
                    lane = pl.ds(pl.multiple_of(core * w + t * LANES, LANES), LANES)
                    for i in range(m):
                        out[i, f, row, :, lane] = ref[k, at : at + h, :]
                        at += h
            if small and (dc, dy) == (0, 0):
                outs[-1][f] = ref[k, at : at + SMALL_ROWS, :]


class Gather:
    def __init__(self, place, shards, y_last, small=None):
        self.place, self.y_last, self.small = place, y_last, small
        self.sizes, rows = [], []
        for shard in shards:
            m, h, w = shard.shape[0], shard.shape[1] // 2, shard.shape[2] // 2
            self.sizes.append((m, h, w))
            cut = lax.dynamic_slice(shard, (0, place.y * h, place.c * w), (m, h, w))
            cut = jnp.transpose(cut.reshape(m, h, w // LANES, LANES), (2, 0, 1, 3))
            rows.append(cut.reshape(-1, LANES))
        if small is not None:
            rows.append(small)
        self.piece = rows[0] if len(rows) == 1 else jnp.concatenate(rows)

    def first(self):
        self.pieces = [self.piece] + [self.place.along_z(self.piece, d) for d in range(1, Z)]

    def second(self, *waits):
        self.stack = stacked(self.pieces, waits)

    def send(self):
        place, stack = self.place, self.stack
        self.held = {(0, 0): stack}
        for d in range(1, place.nx):
            self.held[0, d] = place.along_x(stack, d)
        self.held[1, 0] = place.across(stack, 2)

    def turn(self, *waits):
        self.onward = []
        for d in range(1, self.place.nx) if self.y_last else (0,):
            key = (0, d) if self.y_last else (1, 0)
            if waits:
                self.held[key] = held_back(self.held[key], waits)
            self.onward.append(self.held[key])

    def third(self):
        place, nx = self.place, self.place.nx
        for d in range(1, nx):
            if self.y_last:
                self.held[1, d] = place.across(self.held[0, d], 2)
            else:
                self.held[1, d] = place.along_x(self.held[1, 0], d)

    def settle(self, *waits):
        for d in range(1, self.place.nx):
            self.held[1, d] = held_back(self.held[1, d], waits)

    def whole(self, *waits):
        place = self.place
        parts, arrays = [], []
        for key, value in self.held.items():
            parts += [(0,) + key, (1,) + key]
            arrays += [value, place.across(value, 1)]
        shapes = [shape_of((m, place.fsdp, 2, h, 2 * w)) for m, h, w in self.sizes]
        if self.small is not None:
            shapes.append(shape_of((place.fsdp, SMALL_ROWS, LANES)))
        where = jnp.stack([place.c, place.y, place.z, place.x]).astype(jnp.int32)
        body = functools.partial(
            assemble_kernel,
            parts=tuple(parts),
            nx=place.nx,
            sizes=tuple(self.sizes),
            small=self.small is not None,
        )
        specs = [SMEM] + [VMEM] * len(arrays)
        full = call(body, [where] + arrays, shapes, "assemble", waits, specs, vmem=36)
        whole = [
            v.reshape(m, place.fsdp * 2 * h, 2 * w) for v, (m, h, w) in zip(full, self.sizes)
        ]
        return whole + list(full[len(whole) :])


def step_kernel(where_ref, kept_ref, *refs, axis, count, lead):
    got, keep_ref, send_refs = refs[: -count], refs[-count], refs[len(refs) - count + 1 :]
    own = where_ref[0]
    rest = [()]
    for size in lead[:axis] + lead[axis + 1 :]:
        rest = [r + (i,) for r in rest for i in range(size)]

    def value(at):
        total = kept_ref[at]
        for ref in got:
            total = total + ref[at].astype(jnp.float32)
        return total

    for r in rest:
        keep_ref[r] = value(r[:axis] + (own,) + r[axis:])
        for d, ref in enumerate(send_refs, 1):
            there = lax.rem(own + d, count)
            ref[r] = value(r[:axis] + (there,) + r[axis:]).astype(jnp.bfloat16)


def total_kernel(kept_ref, *refs):
    total = kept_ref[...]
    for ref in refs[:-1]:
        total = total + ref[...].astype(jnp.float32)
    refs[-1][...] = total


class Reduce:
    def __init__(self, place, sent, kept):
        self.place = place
        lead = (Z, place.nx, 2)
        self.sent = [sent]
        self.kept = kept.reshape(lead + kept.shape[2:])
        self.axes = ["z", "x", "y"]
        self.name = "core"

    def send(self):
        place = self.place
        if self.name == "core":
            self.got = [place.across(self.sent[0], 1).reshape(self.kept.shape)]
        elif self.name == "y":
            self.got = [place.across(self.sent[0], 2)]
        else:
            move = place.along_x if self.name == "x" else place.along_z
            self.got = [move(v, d) for d, v in enumerate(self.sent, 1)]

    def step(self, name, *waits):
        place = self.place
        axis = self.axes.index(name)
        lead, tail = self.kept.shape[:-2], self.kept.shape[-2:]
        count = lead[axis]
        left = lead[:axis] + lead[axis + 1 :] + tail
        own = {"z": place.z, "x": place.x, "y": place.y}[name].reshape(1).astype(jnp.int32)
        outs = [shape_of(left, jnp.float32)] + [shape_of(left)] * (count - 1)
        body = functools.partial(step_kernel, axis=axis, count=count, lead=lead)
        ins = [own, self.kept] + self.got
        specs = [SMEM] + [VMEM] * (len(ins) - 1)
        self.kept, *self.sent = call(body, ins, outs, "step_" + name, waits, specs)
        self.axes.remove(name)
        self.name = name

    def finish(self, *waits):
        place = self.place
        shape = shape_of(self.kept.shape, jnp.float32)
        total = call(total_kernel, [self.kept] + self.got, shape, "total", waits)
        bit = 4
        while bit < place.rep:
            total = total + place.across(total, bit)
            bit *= 2
        self.total, self.other = total, place.across(total, 2)

    def done(self):
        place = self.place
        own = place.y == 0
        rows = jnp.concatenate(
            [jnp.where(own, self.total, self.other), jnp.where(own, self.other, self.total)]
        )
        mate = place.across(rows, 1)
        return jnp.where(place.c == 0, rows, mate), jnp.where(place.c == 0, mate, rows)


def reduce_small(place, partial):
    total = partial
    bit = 1
    while bit < place.rep:
        total = total + place.across(total, bit)
        bit *= 2
    total = total.reshape(Z, place.nx, -1)
    near = pick(total, place.x, 1)
    for d in range(1, place.nx):
        near = near + place.along_x(pick(total, (place.x + d) % place.nx, 1), d)
    mine = pick(near, place.z)
    for d in range(1, Z):
        mine = mine + place.along_z(pick(near, (place.z + d) % Z), d)
    return mine


NEGATIVE = -1e30
TILE = 256
PAIR = 128


def dot(a, b, dims):
    return lax.dot_general(a, b, (dims, ((), ())), preferred_element_type=jnp.float32)


NT = ((1,), (1,))
NN = ((1,), (0,))
TN = ((0,), (0,))


def turned(v):
    return v.astype(jnp.float32).T


def half_mask(j):
    return lax.broadcasted_iota(jnp.int32, (1, PAIR), 1) // (PAIR // 2) == j


def masked_scores(k, qm, toe, length, t, causal):
    scores = dot(k, qm, NT)
    rows = scores.shape[0]
    key = lax.broadcasted_iota(jnp.int32, (rows, TILE), 0)
    if causal:
        bias = toe[:, :TILE]
        if t:
            bias = jnp.concatenate([toe[:, TILE:], bias], axis=0)
        scores = scores + bias
        query = lax.broadcasted_iota(jnp.int32, (rows, TILE), 1) + t * TILE
        allowed = key <= jnp.minimum(query, length - 1)
    else:
        allowed = key < length
    return jnp.where(allowed, scores, NEGATIVE)


def spread(row_ref, toe_ref):
    for j in range(2):
        row = jnp.broadcast_to(row_ref[0, j : j + 1, :], (TILE, 2 * TILE))
        toe_ref[j] = pltpu.roll(row, 0, 1, stride=1, stride_axis=0)


def forward_kernel(causal, len_ref, *refs):
    if causal:
        q_ref, k_ref, v_ref, row_ref, o_ref, lse_ref, toe_ref = refs
    else:
        q_ref, k_ref, v_ref, o_ref, lse_ref = refs
        toe_ref = None
    s = pl.program_id(1)
    length = len_ref[s]
    if causal:

        @pl.when(s == 0)
        def _():
            spread(row_ref, toe_ref)

    q, k, v = q_ref[0], k_ref[0], v_ref[0]
    v_turned = turned(v).astype(jnp.bfloat16)
    cells = [(t, j) for t in range(q.shape[0] // TILE) for j in range(2)]

    def score(t, j):
        seen = (t + 1) * TILE if causal else k.shape[0]
        qm = jnp.where(half_mask(j), q[t * TILE : (t + 1) * TILE], 0)
        return masked_scores(k[:seen], qm, toe_ref[j] if causal else None, length, t, causal)

    outs = []
    ahead = score(*cells[0])
    for i, (t, j) in enumerate(cells):
        scores = ahead
        if i + 1 < len(cells):
            ahead = score(*cells[i + 1])
        here = slice(t * TILE, (t + 1) * TILE)
        top = jnp.max(scores, axis=0, keepdims=True)
        grown = jnp.exp(scores - top)
        total = jnp.sum(grown, axis=0, keepdims=True)
        lse_ref[0, 0, j : j + 1, here] = top + jnp.log(total)
        chances = (grown * (1.0 / total)).astype(jnp.bfloat16)
        outs.append(dot(v_turned[j * 64 : (j + 1) * 64, : scores.shape[0]], chances, NN))
        if j:
            o_ref[0, here, :] = turned(jnp.concatenate(outs, axis=0)).astype(jnp.bfloat16)
            outs = []


def diagonal_sums(v):
    width = v.shape[1]
    groups = v[:8]
    for a in range(8, v.shape[0], 8):
        groups = groups + pltpu.roll(v[a : a + 8], width - a, 1)
    total = groups[:1]
    for b in range(1, 8):
        total = total + pltpu.roll(groups[b : b + 1], width - b, 1)
    return total


def backward_kernel(causal, len_ref, *refs):
    if causal:
        q_ref, k_ref, v_ref, do_ref, lse_ref, row_ref = refs[:6]
        dq_ref, dk_ref, dv_ref, diag_ref, toe_ref, sum_ref = refs[6:]
    else:
        q_ref, k_ref, v_ref, do_ref, lse_ref = refs[:5]
        dq_ref, dk_ref, dv_ref = refs[5:]
        toe_ref = None
    s = pl.program_id(1)
    length = len_ref[s]
    if causal:

        @pl.when(s == 0)
        def _():
            spread(row_ref, toe_ref)
            sum_ref[...] = jnp.zeros_like(sum_ref)

    q, k, v, do = q_ref[0], k_ref[0], v_ref[0], do_ref[0]
    k_turned = turned(k).astype(jnp.bfloat16)
    tiles = q.shape[0] // TILE
    dk = [None] * tiles
    dv = [None] * tiles
    cells = [(t, j) for t in range(tiles) for j in range(2)]
    outs = []

    def add(held, value):
        return value if held is None else held + value

    def score(t, j):
        seen = (t + 1) * TILE if causal else k.shape[0]
        here = slice(t * TILE, (t + 1) * TILE)
        qm = jnp.where(half_mask(j), q[here], 0)
        dom = jnp.where(half_mask(j), do[here], 0)
        scores = masked_scores(k[:seen], qm, toe_ref[j] if causal else None, length, t, causal)
        return scores, dot(v[:seen], dom, NT), qm, dom

    def finish(t, j, chances, d_scores, qm, dom):
        seen = d_scores.shape[0]
        outs.append(dot(k_turned[j * 64 : (j + 1) * 64, :seen], d_scores, NN))
        dv_part = dot(chances, dom, NN)
        dk_part = dot(d_scores, qm, NN)
        for b in range(seen // TILE):
            rows = slice(b * TILE, (b + 1) * TILE)
            dv[b] = add(dv[b], dv_part[rows])
            dk[b] = add(dk[b], dk_part[rows])
        if causal:
            if t:
                sum_ref[j, :, TILE:] += d_scores[: t * TILE].astype(jnp.float32)
            sum_ref[j, :, :TILE] += d_scores[t * TILE :].astype(jnp.float32)
        if j:
            here = slice(t * TILE, (t + 1) * TILE)
            dq_ref[0, here, :] = turned(jnp.concatenate(outs, axis=0)).astype(jnp.bfloat16)
            outs.clear()

    ahead = score(*cells[0])
    behind = None
    for i, (t, j) in enumerate(cells):
        scores, d_chances, qm, dom = ahead
        if i + 1 < len(cells):
            ahead = score(*cells[i + 1])
        here = slice(t * TILE, (t + 1) * TILE)
        chances = jnp.exp(scores - lse_ref[0, 0, j : j + 1, here])
        delta = jnp.sum(chances * d_chances, axis=0, keepdims=True)
        d_scores = (chances * (d_chances - delta)).astype(jnp.bfloat16)
        if behind is not None:
            finish(*behind)
        behind = (t, j, chances.astype(jnp.bfloat16), d_scores, qm, dom)
    finish(*behind)
    for b in range(tiles):
        rows = slice(b * TILE, (b + 1) * TILE)
        dk_ref[0, rows, :] = dk[b].astype(jnp.bfloat16)
        dv_ref[0, rows, :] = dv[b].astype(jnp.bfloat16)
    if causal:

        @pl.when(s == pl.num_programs(1) - 1)
        def _():
            for j in range(2):
                diag_ref[0, j : j + 1, :] = diagonal_sums(sum_ref[j])


def attend(kind, q, k, v, lengths, row=None, do=None, lse=None, waits=()):
    count, slots, width = q.shape
    pairs = width // PAIR
    assert slots == 2 * TILE and k.shape[1] == 2 * TILE
    block = pl.BlockSpec((1, slots, PAIR), lambda p, s: (s, 0, p))
    lse_block = pl.BlockSpec((1, 1, 2, slots), lambda p, s: (s, p, 0, 0))
    row_block = pl.BlockSpec((1, 2, slots), lambda p, s: (p, 0, 0))
    state = jax.ShapeDtypeStruct(q.shape, jnp.bfloat16)
    causal = row is not None
    ins, specs = [lengths, q, k, v], [pl.BlockSpec(memory_space=pltpu.SMEM), block, block, block]
    if kind == "forward":
        body = forward_kernel
        outs = [state, jax.ShapeDtypeStruct((count, pairs, 2, slots), jnp.float32)]
        out_specs = [block, lse_block]
    else:
        body = backward_kernel
        ins += [do, lse]
        specs += [block, lse_block]
        outs = [state] * 3
        out_specs = [block] * 3
    scratch = []
    if causal:
        ins.append(row)
        specs.append(row_block)
        scratch.append(pltpu.VMEM((2, TILE, 2 * TILE), jnp.float32))
        if kind == "backward":
            outs.append(jax.ShapeDtypeStruct(row.shape, jnp.float32))
            out_specs.append(row_block)
            scratch.append(pltpu.VMEM((2, TILE, 2 * TILE), jnp.float32))
    return call(
        functools.partial(body, causal),
        ins,
        outs,
        ("self_" if causal else "cross_") + kind,
        waits,
        specs,
        vmem=24,
        cost=lasting(200),
        grid=(pairs, count),
        out_specs=out_specs,
        scratch_shapes=scratch,
    )


FF_TILE = 256
ROW_TILE = 256


def feed_kernel(n_ref, df_ref, in_ref, out_ref, product_ref, gate_ref, up_ref):
    scale, cubic = 0.7978845608028654, 0.044715

    def dots(r):
        rows = slice(r * ROW_TILE, (r + 1) * ROW_TILE)
        n = n_ref[rows, :]
        return (
            dot(n, in_ref[0], NN),
            dot(n, in_ref[1], NN),
            dot(df_ref[rows, :], out_ref[...], NT),
        )

    count = n_ref.shape[0] // ROW_TILE
    ahead = dots(0)
    for r in range(count):
        gate, up, d_product = ahead
        if r + 1 < count:
            ahead = dots(r + 1)
        rows = slice(r * ROW_TILE, (r + 1) * ROW_TILE)
        square = gate * gate
        bend = jnp.tanh(scale * (gate + cubic * (square * gate)))
        half = 0.5 * (1.0 + bend)
        gelu = gate * half
        slope = half + (0.5 * scale) * gate * (1.0 - bend * bend) * (1.0 + 3 * cubic * square)
        product_ref[rows, :] = (gelu * up).astype(jnp.bfloat16)
        gate_ref[rows, :] = (d_product * up * slope).astype(jnp.bfloat16)
        up_ref[rows, :] = (d_product * gelu).astype(jnp.bfloat16)


def feed(n, df, ffin, ffout):
    count, width = n.shape
    hidden = ffout.shape[0]
    whole = pl.BlockSpec((count, width), lambda i: (0, 0))
    tile = pl.BlockSpec((count, FF_TILE), lambda i: (0, i))
    state = jax.ShapeDtypeStruct((count, hidden), jnp.bfloat16)
    specs = [
        whole,
        whole,
        pl.BlockSpec((2, width, FF_TILE), lambda i: (0, 0, i)),
        pl.BlockSpec((FF_TILE, width), lambda i: (i, 0)),
    ]
    return call(
        feed_kernel,
        [n, df, ffin, ffout],
        [state] * 3,
        "feed",
        (),
        specs,
        cost=lasting(100),
        grid=(hidden // FF_TILE,),
        out_specs=[tile] * 3,
    )


def matmuls_kernel(*refs, count, dims, ends):
    total = dot(refs[0][...], refs[count][0], dims)
    for i in range(1, count):
        total = total + dot(refs[i][...], refs[count + i][0], dims)
    if ends:
        total = (total + refs[2 * count][...]) * refs[2 * count + 1][...]
    refs[-1][...] = total


def matmuls(lefts, weights, dims, name, waits=(), ends=(), cost=FREE):
    lefts = [v.reshape(-1, v.shape[-1]) for v in lefts]
    ends = [v.reshape(-1, v.shape[-1]) for v in ends]
    rows = lefts[0].shape[0]
    width = weights[0][0].shape[1 if dims == NT else 2]

    def tile(v):
        return pl.BlockSpec((ROW_TILE, v.shape[1]), lambda i: (i, 0))

    def layer(v, k):
        return pl.BlockSpec((1,) + v.shape[1:], lambda i: (k, 0, 0))

    out = shape_of((rows, width), jnp.float32)
    return call(
        functools.partial(matmuls_kernel, count=len(lefts), dims=dims, ends=bool(ends)),
        lefts + [w for w, _ in weights] + ends,
        out,
        name,
        waits,
        [tile(v) for v in lefts] + [layer(*w) for w in weights] + [tile(v) for v in ends],
        cost=cost,
        grid=(rows // ROW_TILE,),
        out_specs=tile(out),
    )


def grads_kernel(where_ref, *refs, pairs, lefts, rights):
    left_refs, right_refs = refs[:lefts], refs[lefts : lefts + rights]
    sent_ref, kept_ref = refs[-2:]
    first = where_ref[0] == 0
    for i, left in enumerate(left_refs):
        for m in range(0, left.shape[1], ROW_TILE):
            rows = slice(m, m + ROW_TILE)
            block = turned(left[:, rows]).astype(jnp.bfloat16)
            at = 0
            for k, j in pairs:
                right = right_refs[j]
                w = right.shape[1] // 2
                if k == i:
                    both = dot(block, right[...], NN)
                    near, far = both[:, :w], both[:, w:]
                    sent_ref[rows, at : at + w] = jnp.where(first, far, near).astype(jnp.bfloat16)
                    kept_ref[rows, at : at + w] = jnp.where(first, near, far)
                at += w


def stage_grads(place, lefts, rights, pairs, *waits):
    lefts = [v.reshape(-1, v.shape[-1]) for v in lefts]
    rights = [v.reshape(-1, v.shape[-1]) for v in rights]
    height = lefts[0].shape[1]
    width = sum(rights[j].shape[1] // 2 for _, j in pairs)
    ins = [place.c.reshape(1).astype(jnp.int32)] + lefts + rights
    sent, kept = call(
        functools.partial(
            grads_kernel, pairs=tuple(pairs), lefts=len(lefts), rights=len(rights)
        ),
        ins,
        [shape_of((height, width)), shape_of((height, width), jnp.float32)],
        "grads",
        waits,
        [SMEM] + [VMEM] * (len(ins) - 1),
        vmem=36,
    )
    shape = (place.fsdp, 2, height // place.fsdp // 2, width)
    return Reduce(place, sent.reshape(shape), kept.reshape(shape))


def rms_scale(values, factor):
    return values * lax.rsqrt(jnp.mean(values * values, axis=-1, keepdims=True) + EPS) * factor


def rms_back(values, factor, grad_out):
    return jax.vjp(rms_scale, values, factor)[1](grad_out)


def project(a, w):
    return jnp.einsum("vgq,qy->vgy", a, w, preferred_element_type=jnp.float32)


def project_back(a, w):
    return jnp.einsum("gjr,fr->gjf", a, w, preferred_element_type=jnp.float32)


def bucket_hot(extent, buckets):
    distance = jnp.arange(extent, dtype=jnp.int32)
    far = 16 + sum(((distance >= border).astype(jnp.int32) for border in STEPS))
    bucket = jnp.where(distance < 16, distance, far)
    return (bucket[:, None] == jnp.arange(buckets, dtype=jnp.int32)).astype(jnp.float32)


def per_device(
    rep,
    fsdp,
    tokens,
    encoder_states,
    cotangent,
    qkv_weight,
    out_weight,
    ffin_weight,
    ffout_weight,
    norm_gains,
    bias_table,
    lengths,
    enc_lengths,
):
    place = Place(rep, fsdp)
    seq_len, width = tokens.shape[1:]
    table_rows, heads = bias_table.shape
    shard = qkv_weight.shape[3]
    first = place.c == 0
    half = ffin_weight.shape[3] // 2
    part = width // 2

    small_count = 3 * shard + table_rows * heads
    small = jnp.concatenate([norm_gains.reshape(-1), bias_table.reshape(-1)])
    small = jnp.pad(small, (0, SMALL_ROWS * LANES - small_count)).reshape(SMALL_ROWS, LANES)
    stages = [
        Gather(place, [jnp.concatenate([qkv_weight[0, 0], out_weight[0, :1]])], True, small),
        Gather(place, [jnp.concatenate([qkv_weight[0, 1], out_weight[0, 1:]])], False),
        Gather(place, [ffin_weight[0], ffout_weight], True),
    ]
    for stage in stages:
        stage.first()
    stages[0].second()
    stages[0].send()
    stages[1].second()
    stages[0].turn(stages[1].stack)
    stages[0].third()
    stages[2].second()
    self_w, small = stages[0].whole(stages[2].stack)
    small = small.reshape(fsdp, SMALL_ROWS * LANES)
    gains = small[:, : 3 * shard].reshape(fsdp, 3, shard)
    gains = wide(jnp.transpose(gains, (1, 0, 2)).reshape(3, width))
    table = wide(small[:, 3 * shard : small_count].reshape(fsdp * table_rows, heads))
    hot = bucket_hot(seq_len, fsdp * table_rows)
    row = jnp.einsum("nb,bh->hn", hot, table, precision=lax.Precision.HIGHEST)
    row = row.reshape(heads // 2, 2, seq_len)

    live = wide(jnp.arange(seq_len, dtype=jnp.int32)[None, :] < lengths[:, None])[:, :, None]
    stream = wide(tokens)
    normed_self = low(rms_scale(stream, gains[0]))
    q1, k1, v1 = (low(project(normed_self, self_w[i])) for i in range(3))
    ready = [stages[1].stack, stages[2].stack]
    stages[1].send()
    stages[2].send()
    o1, lse1 = attend("forward", q1, k1, v1, lengths, row, waits=ready)
    stages[1].turn(o1)
    stages[1].third()
    middle = stream + project(o1, self_w[3])
    normed_cross = low(rms_scale(middle, gains[1]))
    cross_w, = stages[1].whole(*stages[1].onward)
    q2 = low(project(normed_cross, cross_w[0]))
    k2, v2 = (low(project(encoder_states, cross_w[i])) for i in (1, 2))
    stages[2].turn(cross_w)
    stages[2].third()
    o2, lse2 = attend("forward", q2, k2, v2, enc_lengths, waits=stages[2].onward)
    later = middle + project(o2, cross_w[3])
    normed_feed = low(rms_scale(later, gains[2]))
    stages[2].settle(o2)
    ffin, ffout = stages[2].whole(o2)

    def flat(v):
        return v.reshape(-1, v.shape[-1])

    grad = wide(cotangent) * live
    grad_low = low(grad)
    product, grad_gate, grad_upward = (
        v.reshape(tokens.shape[:2] + (2 * half,))
        for v in feed(flat(normed_feed), flat(grad_low), ffin, ffout[0])
    )

    ffin_sum = stage_grads(place, [normed_feed], [grad_gate, grad_upward], [(0, 0), (0, 1)])
    ffin_sum.send()
    ffout_sum = stage_grads(place, [product], [grad_low], [(0, 0)], *ffin_sum.sent)
    ffin_sum.step("x", *ffout_sum.sent)
    ffout_sum.send()
    grad_normed = matmuls(
        [grad_gate, grad_upward], [(ffin, 0), (ffin, 1)], NT, "grad_normed", ffin_sum.sent, cost=lasting(100)
    ).reshape(tokens.shape)
    grad_norm, gain_feed = rms_back(later, gains[2], grad_normed)
    grad_later = grad + grad_norm
    ffout_sum.step("y", *ffin_sum.sent)

    da2 = low(grad_later)
    do = low(project_back(da2, cross_w[3]))
    ready = ffout_sum.sent + ffin_sum.sent
    ffin_sum.send()
    ffout_sum.send()
    dq2, dk2, dv2 = attend("backward", q2, k2, v2, enc_lengths, None, do, lse2, ready)
    ffin_sum.step("y", dq2)
    ffout_sum.step("x", *ffin_sum.sent)
    ffin_sum.send()
    ffout_sum.send()
    grad_norm, gain_cross = rms_back(middle, gains[1], project_back(dq2, cross_w[0]))
    grad_middle = grad_later + grad_norm
    da1 = low(grad_middle)
    cross_sum = stage_grads(
        place,
        [normed_cross, encoder_states, o2, o1],
        [dq2, dk2, dv2, da2, da1],
        [(0, 0), (1, 1), (1, 2), (2, 3), (3, 4)],
        *ffout_sum.sent,
    )
    cross_sum.send()
    do = low(project_back(da1, self_w[3]))
    cross_sum.step("y")
    ffin_sum.step("z", *cross_sum.sent)

    ready = cross_sum.sent + ffin_sum.sent
    cross_sum.send()
    ffin_sum.send()
    dq1, dk1, dv1, diagonals = attend("backward", q1, k1, v1, lengths, row, do, lse1, ready)
    self_sum = stage_grads(
        place, [normed_self], [dq1, dk1, dv1], [(0, 0), (0, 1), (0, 2)]
    )
    ffout_sum.step("z", *self_sum.sent)
    cross_sum.step("x", *self_sum.sent)
    ready = self_sum.sent + ffout_sum.sent + cross_sum.sent
    self_sum.send()
    cross_sum.send()
    ffout_sum.send()
    encoder_grad = matmuls(
        [dk2, dv2], [(cross_w, 1), (cross_w, 2)], NT, "encoder_grad", ready, cost=lasting(100)
    ).reshape(tokens.shape)
    self_sum.step("y", encoder_grad)
    self_sum.send()
    into = matmuls(
        [dq1, dk1, dv1],
        [(self_w, 0), (self_w, 1), (self_w, 2)],
        NT,
        "into",
        self_sum.sent,
        cost=lasting(200),
    ).reshape(tokens.shape)
    grad_norm, gain_self = rms_back(stream, gains[0], into)
    token_grad = grad_middle + grad_norm
    cross_sum.step("z", into)
    cross_sum.send()
    output_state = matmuls(
        [product],
        [(ffout, 0)],
        NN,
        "output_state",
        cross_sum.sent,
        [later, jnp.broadcast_to(live, tokens.shape[:2] + (1,))],
    ).reshape(tokens.shape)
    self_sum.step("x", output_state)
    self_sum.send()
    ffin_sum.finish(*self_sum.sent)
    ffout_sum.finish(*self_sum.sent)
    grad_table = jnp.einsum(
        "nb,hn->bh", hot, diagonals.reshape(heads, seq_len), precision=lax.Precision.HIGHEST
    )
    small = jnp.stack([gain_self, gain_cross, gain_feed]).reshape(3, fsdp, shard)
    small = jnp.concatenate(
        [
            jnp.transpose(small, (1, 0, 2)).reshape(fsdp, 3 * shard),
            grad_table.reshape(fsdp, table_rows * heads),
        ],
        axis=1,
    )
    small = held_back(jnp.pad(small, ((0, 0), (0, -small_count % 128))), self_sum.sent)
    small = reduce_small(place, small)
    self_sum.step("z")
    self_sum.send()
    cross_sum.finish(*self_sum.sent)
    self_sum.finish()

    def matrices(stage, size):
        near, far = stage.done()
        return [
            jnp.concatenate([near[:, i : i + size], far[:, i : i + size]], axis=1)
            for i in range(0, near.shape[1], size)
        ]

    cross_grads = matrices(cross_sum, part)
    self_grads = matrices(self_sum, part)
    qkv_grad = jnp.stack([jnp.stack(self_grads), jnp.stack(cross_grads[:3])])[None]
    out_grad = jnp.stack([cross_grads[4], cross_grads[3]])[None]
    ffin_grad = jnp.stack(matrices(ffin_sum, half))[None]
    ffout_grad = matrices(ffout_sum, part)[0][None]
    return (
        output_state,
        token_grad,
        encoder_grad,
        qkv_grad,
        out_grad,
        ffin_grad,
        ffout_grad,
        small[: 3 * shard].reshape(1, 3, shard),
        small[3 * shard : small_count].reshape(table_rows, heads),
    )


def solution(mesh):
    in_specs = (
        P(("rep", "fsdp"), None, None),
        P(("rep", "fsdp"), None, None),
        P(("rep", "fsdp"), None, None),
        P(None, None, None, "fsdp", None),
        P(None, None, "fsdp", None),
        P(None, None, "fsdp", None),
        P(None, "fsdp", None),
        P(None, None, "fsdp"),
        P("fsdp", None),
        P(("rep", "fsdp")),
        P(("rep", "fsdp")),
    )
    out_specs = (
        P(("rep", "fsdp"), None, None),
        P(("rep", "fsdp"), None, None),
        P(("rep", "fsdp"), None, None),
        P(None, None, None, "fsdp", None),
        P(None, None, "fsdp", None),
        P(None, None, "fsdp", None),
        P(None, "fsdp", None),
        P(None, None, "fsdp"),
        P("fsdp", None),
    )
    return jax.shard_map(
        functools.partial(per_device, mesh.shape["rep"], mesh.shape["fsdp"]),
        mesh=mesh, in_specs=in_specs, out_specs=out_specs, check_vma=False
    )
```

time: 666 us -> 508 us (0.76)
  matrix products: 124 us -> 23.8 us
  waiting for transfers between devices: 206 us -> 114 us
  Pallas kernels: 125 us -> 195 us
  local copies, waits for them, and re-layouts: 96.5 us -> 64.6 us
    pallas_call x8 -> x40, Pallas kernels: 125 us -> 195 us  [call(): pl.pallas_call(kernel, in_specs=list(specs or [VMEM] * count) + [pl.Block...]
    dot_general x16 -> x0, matrix products: 48.5 us -> none  [weight_grad(): return jnp.einsum('nou,noi->ui', a, b, preferred_element_type=jnp.float32)]
    ppermute x44 -> x35, waiting for transfers between devices: 95.6 us -> 51 us  [across(): return lax.ppermute(v, 'rep', [(i, i ^ bit) for i in range(self.rep)])]
    ppermute x12 -> x9, waiting for transfers between devices: 64.4 us -> 25.6 us  [along_x(): lax.ppermute(v, 'fsdp', [(i, i // nx * nx + (i % nx + d) % nx) for i in r...]
    dot_general x11 -> x3, matrix products: 32.8 us -> 6 us  [project_back(): return jnp.einsum('gjr,fr->gjf', a, w, preferred_element_type=jnp.float32)]
    dot_general x11 -> x8, matrix products: 41.4 us -> 17.5 us  [project(): return jnp.einsum('vgq,qy->vgy', a, w, preferred_element_type=jnp.float32)]
    slice x5 -> x6, local copies, waits for them, and re-layouts: 11 us -> 0.28 us  [the longest x3 0.14 us: matrices(): far[:, i:i + size]]
    reshape x2, local copies, waits for them, and re-layouts: 9.15 us -> 0.09 us  [__init__(): cut = jnp.transpose(cut.reshape(m, h, w // LANES, LANES), (2, 0, 1, 3))]
  transfers between devices with their start and end apart: 86 -> 68, of which waited for: 30 -> 23; matrix products, arithmetic and copies ran while one was open for 18% -> 12% of each run, Pallas kernels for 9% -> 29%
where the time goes in v2:
time: 508 us; the launch traced here: 500 us
  Pallas kernels  195 us (38%)
  waiting for transfers between devices  114 us (22%)
  starting transfers between devices  73.2 us (14%)
  local copies, waits for them, and re-layouts  64.6 us (13%)
  other arithmetic  27.1 us (5%)
  matrix products  23.8 us (5%)
    pallas_call x40, Pallas kernels, call(): pl.pallas_call(kernel, in_specs=list(specs or [VMEM] * count) + [pl.Block...  195 us
    ppermute x35, waiting for transfers between devices, across(): return lax.ppermute(v, 'rep', [(i, i ^ bit) for i in range(self.rep)])  51 us
    unnamed x308, local copies, waits for them, and re-layouts  49.4 us
    ppermute x24, starting transfers between devices, along_z(): lax.ppermute(v, 'fsdp', [(i, (i + d * self.nx) % self.fsdp) for i in rang...  48.2 us
    ppermute x24, waiting for transfers between devices, along_z(): lax.ppermute(v, 'fsdp', [(i, (i + d * self.nx) % self.fsdp) for i in rang...  37.4 us
    ppermute x9, waiting for transfers between devices, along_x(): lax.ppermute(v, 'fsdp', [(i, i // nx * nx + (i % nx + d) % nx) for i in r...  25.6 us
    dot_general x8, matrix products, project(): return jnp.einsum('vgq,qy->vgy', a, w, preferred_element_type=jnp.float32)  17.5 us
    ppermute x35, starting transfers between devices, across(): return lax.ppermute(v, 'rep', [(i, i ^ bit) for i in range(self.rep)])  15.1 us
  transfers between devices with their start and end apart: 68, of which 23 were waited for; matrix products, arithmetic and copies ran while one was open for 12% of the time, Pallas kernels for 29%

profile of v2, /device:TPU:0, one launch (start us, length us, event | category | flops | bytes accessed | tf_op | source)
XLA Modules:
  0.0 500.2 jit_solution(2315944426855846195)
XLA Ops:
  13.0 5.7 %collective-permute-done.1.refs_2_ = bf16[592,128]{1,0:T(8,128)(2,1)S(1)} collective-permute-done((bf16[592,128]{1,0:T(8,128)(2,1)S(1)}, bf16[592,128]{1,0:T(8,128)(2,1)S(1)}, u32[]{:S(2)}, u32[]{:S(2)}) %collective-permute-start.1) | collective-permute-done | bytes 151584 | tf_op jit(solution)/shard_map/ppermute | solution.py:40
  29.8 4.9 collective-permute-done.6.refs_2_
  44.5 7.5 %collective-permute-done.13.refs_1_ = bf16[1152,128]{1,0:T(8,128)(2,1)S(1)} collective-permute-done((bf16[1152,128]{1,0:T(8,128)(2,1)S(1)}, bf16[1152,128]{1,0:T(8,128)(2,1)S(1)}, u32[]{:S(2)}, u32[]{:S(2)}) %collective-permute-start.13) | collective-permute-done | bytes 294944 | tf_op jit(solution)/shard_map/ppermute | solution.py:40
  52.4 11.6 %collective-permute-done.11.refs_7_ = bf16[4,592,128]{2,1,0:T(8,128)(2,1)S(1)} collective-permute-done((bf16[4,592,128]{2,1,0:T(8,128)(2,1)S(1)}, bf16[4,592,128]{2,1,0:T(8,128)(2,1)S(1)}, u32[]{:S(2)}, u32[]{:S(2)}) %collective-permute-start.11) | collective-permute-done | bytes 606240 | tf_op jit(solution)/shard_map/ppermute | solution.py:31
  70.3 7.1 %collective-permute-done.15.refs_3_ = bf16[1152,128]{1,0:T(8,128)(2,1)S(1)} collective-permute-done((bf16[1152,128]{1,0:T(8,128)(2,1)S(1)}, bf16[1152,128]{1,0:T(8,128)(2,1)S(1)}, u32[]{:S(2)}, u32[]{:S(2)}) %collective-permute-start.15) | collective-permute-done | bytes 294944 | tf_op jit(solution)/shard_map/ppermute | solution.py:40
  97.9 17.1 %self_forward.1 = (bf16[2,512,768]{2,1,0:T(8,128)(2,1)S(1)}, f32[2,6,2,512]{3,2,1,0:T(2,128)S(1)}) custom-call(s32[2]{0:T(128)S(1)} %copy-done.75, bf16[2,512,768]{2,1,0:T(8,128)(2,1)S(1)} %copy-done.90, bf16[2,512,768]{2,1,0:T(8,128)(2,1)S(1)} %copy-done.88, bf16[2,512,768]{2,1,0:T(8,128)(2,1)S(1)} %convolution_convert_fusion.5.refs_3_, ...), custom_call_target="tpu_custom_call" | custom-call | flops 199999995904 | tf_op jit(solution)/shard_map/self_forward/pallas_call | solution.py:81
  121.1 12.4 %collective-permute-done.21.refs_7_ = bf16[4,576,128]{2,1,0:T(8,128)(2,1)S(1)} collective-permute-done((bf16[4,576,128]{2,1,0:T(8,128)(2,1)S(1)}, bf16[4,576,128]{2,1,0:T(8,128)(2,1)S(1)}, u32[]{:S(2)}, u32[]{:S(2)}) %collective-permute-start.21) | collective-permute-done | bytes 589856 | tf_op jit(solution)/shard_map/ppermute | solution.py:35
  139.6 7.7 %collective-permute-done.26.refs_5_ = bf16[4,1152,128]{2,1,0:T(8,128)(2,1)} collective-permute-done((bf16[4,1152,128]{2,1,0:T(8,128)(2,1)}, bf16[4,1152,128]{2,1,0:T(8,128)(2,1)}, u32[]{:S(2)}, u32[]{:S(2)}) %collective-permute-start.26) | collective-permute-done | bytes 1179680 | tf_op jit(solution)/shard_map/ppermute | solution.py:31
  151.4 7.0 %collective-permute-done.23.refs_0_ = bf16[4,1152,128]{2,1,0:T(8,128)(2,1)S(1)} collective-permute-done((bf16[4,1152,128]{2,1,0:T(8,128)(2,1)}, bf16[4,1152,128]{2,1,0:T(8,128)(2,1)S(1)}, u32[]{:S(2)}, u32[]{:S(2)}) %collective-permute-start.23) | collective-permute-done | bytes 1179680 | tf_op jit(solution)/shard_map/ppermute | solution.py:35
  164.5 18.8 %cross_forward.1 = (bf16[2,512,768]{2,1,0:T(8,128)(2,1)S(1)}, f32[2,6,2,512]{3,2,1,0:T(2,128)S(1)}) custom-call(s32[2]{0:T(128)S(1)} %copy-done.84, bf16[2,512,768]{2,1,0:T(8,128)(2,1)S(1)} %convolution_convert_fusion.4.refs_1_, bf16[2,512,768]{2,1,0:T(8,128)(2,1)S(1)} %fusion.10.refs_2_, bf16[2,512,768]{2,1,0:T(8,128)(2,1)S(1)} %fusion.11.refs_3_, ...), custom_call_target="tpu_custom_call" | custom-call | flops 199999995904 | tf_op jit(solution)/shard_map/cross_forward/pallas_call | solution.py:81
  196.1 8.7 %assemble.5 = (bf16[2,8,2,48,2048]{4,3,2,1,0:T(8,128)(2,1)}, bf16[1,8,2,128,768]{4,3,2,1,0:T(8,128)(2,1)S(1)}) custom-call(s32[4]{0:T(128)S(1)} %copy-done.74, bf16[4,1152,128]{2,1,0:T(8,128)(2,1)} %stack.119.refs_9_.refs_6_.refs_1_, bf16[4,1152,128]{2,1,0:T(8,128)(2,1)} %collective-permute-done.24.refs_2_, bf16[4,1152,128]{2,1,0:T(8,128)(2,1)} %hold.7.refs_4_.refs_3_, ...), custom_call_target="tpu_custom_call" | custom-call | tf_op jit(solution)/shard_map/assemble/pallas_call | solution.py:81
  204.8 16.2 %feed.1 = (bf16[1024,2048]{1,0:T(8,128)(2,1)S(1)}, bf16[1024,2048]{1,0:T(8,128)(2,1)S(1)}, bf16[1024,2048]{1,0:T(8,128)(2,1)S(1)}) custom-call(bf16[1024,768]{1,0:T(8,128)(2,1)S(1)} %bitcast.201, bf16[1024,768]{1,0:T(8,128)(2,1)S(1)} %bitcast.199, bf16[2,768,2048]{2,1,0:T(8,128)(2,1)} %bitcast.241, bf16[2048,768]{1,0:T(8,128)(2,1)S(1)} %bitcast.220), custom_call_target="tpu_custom_call" | custom-call | flops 99999997952 | tf_op jit(solution)/shard_map/feed/pallas_call | solution.py:81
  221.0 10.5 %grads.4 = (bf16[768,2048]{1,0:T(8,128)(2,1)}, f32[768,2048]{1,0:T(8,128)}) custom-call(s32[1]{0:T(128)} %bitcast.refs_0_, bf16[1024,768]{1,0:T(8,128)(2,1)S(1)} %bitcast.202, bf16[1024,2048]{1,0:T(8,128)(2,1)S(1)} %get-tuple-element.74.refs_2_.refs_0_, bf16[1024,2048]{1,0:T(8,128)(2,1)S(1)} %get-tuple-element.75.refs_3_.refs_1_), custom_call_target="tpu_custom_call" | custom-call | tf_op jit(solution)/shard_map/grads/pallas_call | solution.py:81
  234.1 4.7 grads.5
  252.9 7.3 %grad_normed.1 = f32[1024,768]{1,0:T(8,128)S(1)} custom-call(bf16[1024,2048]{1,0:T(8,128)(2,1)S(1)} %copy-done.22, bf16[1024,2048]{1,0:T(8,128)(2,1)S(1)} %copy-done.24, bf16[2,768,2048]{2,1,0:T(8,128)(2,1)S(1)} %bitcast.242, bf16[2,768,2048]{2,1,0:T(8,128)(2,1)S(1)} %bitcast.243, bf16[4,2,48,2048]{3,2,1,0:T(8,128)(2,1)} %get-tuple-element.79.refs_4_.refs_3_.refs_7_), custom_call_target="tpu_custom_call" | custom-call | flops 99999997952 | tf_op jit(solution)/shard_map/grad_normed/pallas_call | solution.py:81
  269.0 21.7 %cross_backward.1 = (bf16[2,512,768]{2,1,0:T(8,128)(2,1)S(1)}, bf16[2,512,768]{2,1,0:T(8,128)(2,1)S(1)}, bf16[2,512,768]{2,1,0:T(8,128)(2,1)S(1)}) custom-call(s32[2]{0:T(128)S(1)} %copy-done.85, bf16[2,512,768]{2,1,0:T(8,128)(2,1)S(1)} %copy-done.97, bf16[2,512,768]{2,1,0:T(8,128)(2,1)S(1)} %copy-done.93, bf16[2,512,768]{2,1,0:T(8,128)(2,1)S(1)} %copy-done.95, ...), custom_call_target="tpu_custom_call" | custom-call | flops 199999995904 | tf_op jit(solution)/shard_map/cross_backward/pallas_call | solution.py:81
  304.9 10.0 %grads.6 = (bf16[768,1920]{1,0:T(8,128)(2,1)}, f32[768,1920]{1,0:T(8,128)}) custom-call(s32[1]{0:T(128)} %bitcast.refs_0_, bf16[1024,768]{1,0:T(8,128)(2,1)S(1)} %bitcast.207, bf16[1024,768]{1,0:T(8,128)(2,1)S(1)} %bitcast.231, bf16[1024,768]{1,0:T(8,128)(2,1)S(1)} %bitcast.192, bf16[1024,768]{1,0:T(8,128)(2,1)S(1)} %bitcast.206, ...), custom_call_target="tpu_custom_call" | custom-call | tf_op jit(solution)/shard_map/grads/pallas_call | solution.py:81
  327.6 8.2 %collective-permute-done.36.refs_2_ = bf16[4,48,2048]{2,1,0:T(8,128)(2,1)S(1)} collective-permute-done((bf16[4,48,2048]{2,1,0:T(8,128)(2,1)}, bf16[4,48,2048]{2,1,0:T(8,128)(2,1)S(1)}, u32[]{:S(2)}, u32[]{:S(2)}) %collective-permute-start.36) | collective-permute-done | bytes 786464 | tf_op jit(solution)/shard_map/ppermute | solution.py:31
  337.9 25.9 %self_backward.1 = (bf16[2,512,768]{2,1,0:T(8,128)(2,1)S(1)}, bf16[2,512,768]{2,1,0:T(8,128)(2,1)S(1)}, bf16[2,512,768]{2,1,0:T(8,128)(2,1)S(1)}, f32[6,2,512]{2,1,0:T(2,128)S(1)}) custom-call(s32[2]{0:T(128)S(1)} %copy-done.76, bf16[2,512,768]{2,1,0:T(8,128)(2,1)S(1)} %copy-done.91, bf16[2,512,768]{2,1,0:T(8,128)(2,1)S(1)} %copy-done.89, ...), custom_call_target="tpu_custom_call" | custom-call | flops 199999995904 | tf_op jit(solution)/shard_map/self_backward/pallas_call | solution.py:81
  389.3 4.5 into.1
  407.7 4.9 output_state.1
  445.9 4.9 fusion.6
  461.1 4.4 collective-permute-done.60
  485.0 9.2 %collective-permute-done.45 = f32[48,1152]{1,0:T(8,128)S(1)} collective-permute-done((f32[48,1152]{1,0:T(8,128)S(1)}, f32[48,1152]{1,0:T(8,128)S(1)}, u32[]{:S(2)}, u32[]{:S(2)}) %collective-permute-start.45) | collective-permute-done | bytes 221216 | tf_op jit(solution)/shard_map/ppermute | solution.py:31
  (576 shorter events, 256.6 us)
Async XLA Ops:
  37.1 26.9 %collective-permute-start.11 = (bf16[4,592,128]{2,1,0:T(8,128)(2,1)S(1)}, bf16[4,592,128]{2,1,0:T(8,128)(2,1)S(1)}, u32[]{:S(2)}, u32[]{:S(2)}) collective-permute-start(bf16[4,592,128]{2,1,0:T(8,128)(2,1)S(1)} %hold.5.refs_3_), channel_id=1, source_target_pairs={{0,16},{8,24},{16,0},{24,8},{1,17},{9,25},{17,1},{25,9},{2,18},{10... | collective-permute-start | bytes 1818632 | tf_op jit(solution)/shard_map/ppermute | solution.py:31
  42.5 23.3 %collective-permute-start.14 = (bf16[1152,128]{1,0:T(8,128)(2,1)S(1)}, bf16[1152,128]{1,0:T(8,128)(2,1)S(1)}, u32[]{:S(2)}, u32[]{:S(2)}) collective-permute-start(bf16[1152,128]{1,0:T(8,128)(2,1)S(1)} %pad_maximum_fusion.4.refs_0_), channel_id=1, source_target_pairs={{0,4},{1,5},{2,6},{3,7},{4,0},{5,1},{6,2},{7,3},{8,12},{9,13},{10,... | collective-permute-start | bytes 884744 | tf_op jit(solution)/shard_map/ppermute | solution.py:40
  44.5 35.5 %collective-permute-start.3 = (bf16[4,592,128]{2,1,0:T(8,128)(2,1)S(1)}, bf16[4,592,128]{2,1,0:T(8,128)(2,1)S(1)}, u32[]{:S(2)}, u32[]{:S(2)}) collective-permute-start(bf16[4,592,128]{2,1,0:T(8,128)(2,1)S(1)} %stack.117.refs_1_), channel_id=1, source_target_pairs={{0,8},{8,0},{16,24},{24,16},{1,9},{9,1},{17,25},{25,17},{2,10},{10... | collective-permute-start | bytes 1818632 | tf_op jit(solution)/shard_map/ppermute | solution.py:31
  51.9 28.5 %collective-permute-start.8 = (bf16[4,592,128]{2,1,0:T(8,128)(2,1)S(1)}, bf16[4,592,128]{2,1,0:T(8,128)(2,1)S(1)}, u32[]{:S(2)}, u32[]{:S(2)}) collective-permute-start(bf16[4,592,128]{2,1,0:T(8,128)(2,1)S(1)} %hold.5.refs_3_), channel_id=1, source_target_pairs={{0,8},{8,0},{16,24},{24,16},{1,9},{9,1},{17,25},{25,17},{2,10},{10... | collective-permute-start | bytes 1818632 | tf_op jit(solution)/shard_map/ppermute | solution.py:31
  52.1 28.4 %collective-permute-start.10 = (bf16[4,592,128]{2,1,0:T(8,128)(2,1)S(1)}, bf16[4,592,128]{2,1,0:T(8,128)(2,1)S(1)}, u32[]{:S(2)}, u32[]{:S(2)}) collective-permute-start(bf16[4,592,128]{2,1,0:T(8,128)(2,1)S(1)} %collective-permute-done.9.refs_5_), channel_id=1, source_target_pairs={{0,8},{8,0},{16,24},{24,16},{1,9},{9,1},{17,25},{25,17},{2,10},{10... | collective-permute-start | bytes 1818632 | tf_op jit(solution)/shard_map/ppermute | solution.py:31
  77.3 38.3 %collective-permute-start.19 = (bf16[4,576,128]{2,1,0:T(8,128)(2,1)}, bf16[4,576,128]{2,1,0:T(8,128)(2,1)}, u32[]{:S(2)}, u32[]{:S(2)}) collective-permute-start(bf16[4,576,128]{2,1,0:T(8,128)(2,1)} %stack.118.refs_1_.refs_5_), channel_id=1, source_target_pairs={{0,16},{8,24},{16,0},{24,8},{1,17},{9,25},{17,1},{25,9},{2,18},{10... | collective-permute-start | bytes 1769480 | tf_op jit(solution)/shard_map/ppermute | solution.py:31
  79.9 40.6 %collective-permute-start.17 = (bf16[4,576,128]{2,1,0:T(8,128)(2,1)}, bf16[4,576,128]{2,1,0:T(8,128)(2,1)}, u32[]{:S(2)}, u32[]{:S(2)}) collective-permute-start(bf16[4,576,128]{2,1,0:T(8,128)(2,1)} %stack.118.refs_1_.refs_5_), channel_id=1, source_target_pairs={{0,1},{1,0},{2,3},{3,2},{4,5},{5,4},{6,7},{7,6},{8,9},{9,8},{10,11... | collective-permute-start | bytes 1769480 | tf_op jit(solution)/shard_map/ppermute | solution.py:35
  80.5 40.1 %collective-permute-start.16 = (bf16[4,576,128]{2,1,0:T(8,128)(2,1)}, bf16[4,576,128]{2,1,0:T(8,128)(2,1)}, u32[]{:S(2)}, u32[]{:S(2)}) collective-permute-start(bf16[4,576,128]{2,1,0:T(8,128)(2,1)} %stack.118.refs_1_.refs_5_), channel_id=1, source_target_pairs={{0,8},{8,0},{16,24},{24,16},{1,9},{9,1},{17,25},{25,17},{2,10},{10... | collective-permute-start | bytes 1769480 | tf_op jit(solution)/shard_map/ppermute | solution.py:31
  118.9 28.4 %collective-permute-start.26 = (bf16[4,1152,128]{2,1,0:T(8,128)(2,1)}, bf16[4,1152,128]{2,1,0:T(8,128)(2,1)}, u32[]{:S(2)}, u32[]{:S(2)}) collective-permute-start(bf16[4,1152,128]{2,1,0:T(8,128)(2,1)} %stack.119.refs_9_.refs_6_.refs_1_), channel_id=1, source_target_pairs={{0,16},{8,24},{16,0},{24,8},{1,17},{9,25},{17,1},{25,9},{2,18},{10... | collective-permute-start | bytes 3538952 | tf_op jit(solution)/shard_map/ppermute | solution.py:31
  120.0 38.3 %collective-permute-start.23 = (bf16[4,1152,128]{2,1,0:T(8,128)(2,1)}, bf16[4,1152,128]{2,1,0:T(8,128)(2,1)S(1)}, u32[]{:S(2)}, u32[]{:S(2)}) collective-permute-start(bf16[4,1152,128]{2,1,0:T(8,128)(2,1)} %stack.119.refs_9_.refs_6_.refs_1_), channel_id=1, source_target_pairs={{0,1},{1,0},{2,3},{3,2},{4,5},{5,4},{6,7},{7,6},{8,9},{9,8},{10,11... | collective-permute-start | bytes 3538952 | tf_op jit(solution)/shard_map/ppermute | solution.py:35
  120.6 26.7 %collective-permute-start.20 = (bf16[4,576,128]{2,1,0:T(8,128)(2,1)S(1)}, bf16[4,576,128]{2,1,0:T(8,128)(2,1)S(1)}, u32[]{:S(2)}, u32[]{:S(2)}) collective-permute-start(bf16[4,576,128]{2,1,0:T(8,128)(2,1)S(1)} %hold.6.refs_5_.refs_9_), channel_id=1, source_target_pairs={{0,8},{8,0},{16,24},{24,16},{1,9},{9,1},{17,25},{25,17},{2,10},{10... | collective-permute-start | bytes 1769480 | tf_op jit(solution)/shard_map/ppermute | solution.py:31
  139.0 57.0 %collective-permute-start.24 = (bf16[4,1152,128]{2,1,0:T(8,128)(2,1)}, bf16[4,1152,128]{2,1,0:T(8,128)(2,1)}, u32[]{:S(2)}, u32[]{:S(2)}) collective-permute-start(bf16[4,1152,128]{2,1,0:T(8,128)(2,1)} %stack.119.refs_9_.refs_6_.refs_1_), channel_id=1, source_target_pairs={{0,8},{8,0},{16,24},{24,16},{1,9},{9,1},{17,25},{25,17},{2,10},{10... | collective-permute-start | bytes 3538952 | tf_op jit(solution)/shard_map/ppermute | solution.py:31
  147.3 48.8 %collective-permute-start.27 = (bf16[4,1152,128]{2,1,0:T(8,128)(2,1)}, bf16[4,1152,128]{2,1,0:T(8,128)(2,1)}, u32[]{:S(2)}, u32[]{:S(2)}) collective-permute-start(bf16[4,1152,128]{2,1,0:T(8,128)(2,1)} %collective-permute-done.26.refs_5_), channel_id=1, source_target_pairs={{0,8},{8,0},{16,24},{24,16},{1,9},{9,1},{17,25},{25,17},{2,10},{10... | collective-permute-start | bytes 3538952 | tf_op jit(solution)/shard_map/ppermute | solution.py:31
  159.5 27.9 %collective-permute-start.28 = (bf16[4,1152,128]{2,1,0:T(8,128)(2,1)}, bf16[4,1152,128]{2,1,0:T(8,128)(2,1)}, u32[]{:S(2)}, u32[]{:S(2)}) collective-permute-start(bf16[4,1152,128]{2,1,0:T(8,128)(2,1)} %hold.7.refs_4_.refs_3_), channel_id=1, source_target_pairs={{0,16},{8,24},{16,0},{24,8},{1,17},{9,25},{17,1},{25,9},{2,18},{10... | collective-permute-start | bytes 3538952 | tf_op jit(solution)/shard_map/ppermute | solution.py:31
  160.0 36.0 %collective-permute-start.25 = (bf16[4,1152,128]{2,1,0:T(8,128)(2,1)}, bf16[4,1152,128]{2,1,0:T(8,128)(2,1)}, u32[]{:S(2)}, u32[]{:S(2)}) collective-permute-start(bf16[4,1152,128]{2,1,0:T(8,128)(2,1)} %hold.7.refs_4_.refs_3_), channel_id=1, source_target_pairs={{0,8},{8,0},{16,24},{24,16},{1,9},{9,1},{17,25},{25,17},{2,10},{10... | collective-permute-start | bytes 3538952 | tf_op jit(solution)/shard_map/ppermute | solution.py:31
  240.4 25.5 %collective-permute-start.31 = (bf16[8,2,128,384]{3,2,1,0:T(8,128)(2,1)}, bf16[8,2,128,384]{3,2,1,0:T(8,128)(2,1)S(1)}, u32[]{:S(2)}, u32[]{:S(2)}) collective-permute-start(bf16[8,2,128,384]{3,2,1,0:T(8,128)(2,1)} %bitcast.53.refs_3_), channel_id=1, source_target_pairs={{0,8},{8,0},{16,24},{24,16},{1,9},{9,1},{17,25},{25,17},{2,10},{10... | collective-permute-start | bytes 4718600 | tf_op jit(solution)/shard_map/ppermute | solution.py:31
  260.2 37.8 %collective-permute-start.33 = (bf16[4,2,48,2048]{3,2,1,0:T(8,128)(2,1)}, bf16[4,2,48,2048]{3,2,1,0:T(8,128)(2,1)}, u32[]{:S(2)}, u32[]{:S(2)}) collective-permute-start(bf16[4,2,48,2048]{3,2,1,0:T(8,128)(2,1)} %get-tuple-element.79.refs_4_.refs_3_.refs_7_), channel_id=1, source_target_pairs={{0,1},{1,0},{2,3},{3,2},{4,5},{5,4},{6,7},{7,6},{8,9},{9,8},{10,11... | collective-permute-start | bytes 4718600 | tf_op jit(solution)/shard_map/ppermute | solution.py:35
  267.5 34.4 %collective-permute-start.32 = (bf16[4,2,128,384]{3,2,1,0:T(8,128)(2,1)}, bf16[4,2,128,384]{3,2,1,0:T(8,128)(2,1)}, u32[]{:S(2)}, u32[]{:S(2)}) collective-permute-start(bf16[4,2,128,384]{3,2,1,0:T(8,128)(2,1)} %get-tuple-element.82.refs_6_), channel_id=1, source_target_pairs={{0,16},{8,24},{16,0},{24,8},{1,17},{9,25},{17,1},{25,9},{2,18},{10... | collective-permute-start | bytes 2359304 | tf_op jit(solution)/shard_map/ppermute | solution.py:31
  320.9 49.7 %collective-permute-start.39 = (bf16[4,128,384]{2,1,0:T(8,128)(2,1)}, bf16[4,128,384]{2,1,0:T(8,128)(2,1)}, u32[]{:S(2)}, u32[]{:S(2)}) collective-permute-start(bf16[4,128,384]{2,1,0:T(8,128)(2,1)} %get-tuple-element.89.refs_10_), channel_id=1, source_target_pairs={{0,1},{1,0},{2,3},{3,2},{4,5},{5,4},{6,7},{7,6},{8,9},{9,8},{10,11... | collective-permute-start | bytes 1179656 | tf_op jit(solution)/shard_map/ppermute | solution.py:35
  326.0 45.9 %collective-permute-start.35 = (bf16[4,2,48,1920]{3,2,1,0:T(8,128)(2,1)}, bf16[4,2,48,1920]{3,2,1,0:T(8,128)(2,1)}, u32[]{:S(2)}, u32[]{:S(2)}) collective-permute-start(bf16[4,2,48,1920]{3,2,1,0:T(8,128)(2,1)} %get-tuple-element.93.refs_3_.refs_7_), channel_id=1, source_target_pairs={{0,16},{8,24},{16,0},{24,8},{1,17},{9,25},{17,1},{25,9},{2,18},{10... | collective-permute-start | bytes 4423688 | tf_op jit(solution)/shard_map/ppermute | solution.py:31
  375.9 23.4 %collective-permute-start.37 = (bf16[4,48,1920]{2,1,0:T(8,128)(2,1)}, bf16[4,48,1920]{2,1,0:T(8,128)(2,1)}, u32[]{:S(2)}, u32[]{:S(2)}) collective-permute-start(bf16[4,48,1920]{2,1,0:T(8,128)(2,1)} %get-tuple-element.104.refs_8_), channel_id=1, source_target_pairs={{0,1},{1,0},{2,3},{3,2},{4,5},{5,4},{6,7},{7,6},{8,9},{9,8},{10,11... | collective-permute-start | bytes 2211848 | tf_op jit(solution)/shard_map/ppermute | solution.py:35
  388.8 23.7 %collective-permute-start.40 = (bf16[4,2,48,1152]{3,2,1,0:T(8,128)(2,1)}, bf16[4,2,48,1152]{3,2,1,0:T(8,128)(2,1)}, u32[]{:S(2)}, u32[]{:S(2)}) collective-permute-start(bf16[4,2,48,1152]{3,2,1,0:T(8,128)(2,1)} %get-tuple-element.110.refs_6_), channel_id=1, source_target_pairs={{0,16},{8,24},{16,0},{24,8},{1,17},{9,25},{17,1},{25,9},{2,18},{10... | collective-permute-start | bytes 2654216 | tf_op jit(solution)/shard_map/ppermute | solution.py:31
  451.9 23.2 %collective-permute-start.47 = (bf16[48,1920]{1,0:T(8,128)(2,1)}, bf16[48,1920]{1,0:T(8,128)(2,1)S(1)}, u32[]{:S(2)}, u32[]{:S(2)}) collective-permute-start(bf16[48,1920]{1,0:T(8,128)(2,1)} %get-tuple-element.111.refs_4_), channel_id=1, source_target_pairs={{0,2},{1,3},{2,4},{3,5},{4,6},{5,7},{6,0},{7,1},{8,10},{9,11},{10,... | collective-permute-start | bytes 552968 | tf_op jit(solution)/shard_map/ppermute | solution.py:40
  451.9 23.3 %collective-permute-start.48 = (bf16[48,1920]{1,0:T(8,128)(2,1)}, bf16[48,1920]{1,0:T(8,128)(2,1)S(1)}, u32[]{:S(2)}, u32[]{:S(2)}) collective-permute-start(bf16[48,1920]{1,0:T(8,128)(2,1)} %get-tuple-element.112.refs_5_), channel_id=1, source_target_pairs={{0,4},{1,5},{2,6},{3,7},{4,0},{5,1},{6,2},{7,3},{8,12},{9,13},{10,... | collective-permute-start | bytes 552968 | tf_op jit(solution)/shard_map/ppermute | solution.py:40
  (195 other events, 1549.1 us)

commit v3 on v2

--- a/solution.py
+++ b/solution.py
@@ -230,6 +230,13 @@
     refs[-1][...] = total
 
 
+def rows_kernel(where_ref, total_ref, other_ref, out):
+    h = total_ref.shape[0]
+    y = where_ref[0]
+    out[pl.ds(pl.multiple_of(y * h, 8), h), :] = total_ref[...]
+    out[pl.ds(pl.multiple_of((1 - y) * h, 8), h), :] = other_ref[...]
+
+
 class Reduce:
     def __init__(self, place, sent, kept):
         self.place = place
@@ -249,7 +256,7 @@
             move = place.along_x if self.name == "x" else place.along_z
             self.got = [move(v, d) for d, v in enumerate(self.sent, 1)]
 
-    def step(self, name, *waits):
+    def step(self, name, *waits, cost=FREE):
         place = self.place
         axis = self.axes.index(name)
         lead, tail = self.kept.shape[:-2], self.kept.shape[-2:]
@@ -260,37 +267,45 @@
         body = functools.partial(step_kernel, axis=axis, count=count, lead=lead)
         ins = [own, self.kept] + self.got
         specs = [SMEM] + [VMEM] * (len(ins) - 1)
-        self.kept, *self.sent = call(body, ins, outs, "step_" + name, waits, specs)
+        self.kept, *self.sent = call(
+            body, ins, outs, "step_" + name, waits, specs, cost=cost
+        )
         self.axes.remove(name)
         self.name = name
 
-    def finish(self, *waits):
+    def finish(self, *waits, cost=FREE):
         place = self.place
         shape = shape_of(self.kept.shape, jnp.float32)
-        total = call(total_kernel, [self.kept] + self.got, shape, "total", waits)
+        total = call(total_kernel, [self.kept] + self.got, shape, "total", waits, cost=cost)
         bit = 4
         while bit < place.rep:
             total = total + place.across(total, bit)
             bit *= 2
         self.total, self.other = total, place.across(total, 2)
 
+    def rows(self, *waits, cost=FREE):
+        place = self.place
+        h, w = self.total.shape
+        ins = [place.y.reshape(1).astype(jnp.int32), self.total, self.other]
+        out = shape_of((2 * h, w), jnp.float32)
+        self.near = call(rows_kernel, ins, out, "rows", waits, [SMEM, VMEM, VMEM], cost=cost)
+        self.far = place.across(self.near, 1)
+
     def done(self):
-        place = self.place
-        own = place.y == 0
-        rows = jnp.concatenate(
-            [jnp.where(own, self.total, self.other), jnp.where(own, self.other, self.total)]
-        )
-        mate = place.across(rows, 1)
-        return jnp.where(place.c == 0, rows, mate), jnp.where(place.c == 0, mate, rows)
-
-
-def reduce_small(place, partial):
-    total = partial
+        first = self.place.c == 0
+        return jnp.where(first, self.near, self.far), jnp.where(first, self.far, self.near)
+
+
+def sum_replicas(place, partial):
     bit = 1
     while bit < place.rep:
-        total = total + place.across(total, bit)
+        partial = partial + place.across(partial, bit)
         bit *= 2
-    total = total.reshape(Z, place.nx, -1)
+    return partial
+
+
+def sum_owners(place, partial):
+    total = partial.reshape(Z, place.nx, -1)
     near = pick(total, place.x, 1)
     for d in range(1, place.nx):
         near = near + place.along_x(pick(total, (place.x + d) % place.nx, 1), d)
@@ -584,10 +599,10 @@
         total = total + dot(refs[i][...], refs[count + i][0], dims)
     if ends:
         total = (total + refs[2 * count][...]) * refs[2 * count + 1][...]
-    refs[-1][...] = total
-
-
-def matmuls(lefts, weights, dims, name, waits=(), ends=(), cost=FREE):
+    refs[-1][...] = total.astype(refs[-1].dtype)
+
+
+def matmuls(lefts, weights, dims, name, waits=(), ends=(), cost=FREE, dtype=jnp.float32):
     lefts = [v.reshape(-1, v.shape[-1]) for v in lefts]
     ends = [v.reshape(-1, v.shape[-1]) for v in ends]
     rows = lefts[0].shape[0]
@@ -599,7 +614,7 @@
     def layer(v, k):
         return pl.BlockSpec((1,) + v.shape[1:], lambda i: (k, 0, 0))
 
-    out = shape_of((rows, width), jnp.float32)
+    out = shape_of((rows, width), dtype)
     return call(
         functools.partial(matmuls_kernel, count=len(lefts), dims=dims, ends=bool(ends)),
         lefts + [w for w, _ in weights] + ends,
@@ -633,7 +648,7 @@
                 at += w
 
 
-def stage_grads(place, lefts, rights, pairs, *waits):
+def stage_grads(place, lefts, rights, pairs, *waits, cost=FREE):
     lefts = [v.reshape(-1, v.shape[-1]) for v in lefts]
     rights = [v.reshape(-1, v.shape[-1]) for v in rights]
     height = lefts[0].shape[1]
@@ -649,6 +664,7 @@
         waits,
         [SMEM] + [VMEM] * (len(ins) - 1),
         vmem=36,
+        cost=cost,
     )
     shape = (place.fsdp, 2, height // place.fsdp // 2, width)
     return Reduce(place, sent.reshape(shape), kept.reshape(shape))
@@ -713,7 +729,7 @@
     stages[0].second()
     stages[0].send()
     stages[1].second()
-    stages[0].turn(stages[1].stack)
+    stages[0].turn(stages[1].stack, stages[0].held[1, 0])
     stages[0].third()
     stages[2].second()
     self_w, small = stages[0].whole(stages[2].stack)
@@ -729,15 +745,15 @@
     stream = wide(tokens)
     normed_self = low(rms_scale(stream, gains[0]))
     q1, k1, v1 = (low(project(normed_self, self_w[i])) for i in range(3))
-    ready = [stages[1].stack, stages[2].stack]
     stages[1].send()
+    stages[1].turn(self_w)
+    stages[1].third()
     stages[2].send()
+    ready = stages[1].onward + [stages[2].stack]
     o1, lse1 = attend("forward", q1, k1, v1, lengths, row, waits=ready)
-    stages[1].turn(o1)
-    stages[1].third()
     middle = stream + project(o1, self_w[3])
     normed_cross = low(rms_scale(middle, gains[1]))
-    cross_w, = stages[1].whole(*stages[1].onward)
+    cross_w, = stages[1].whole(o1)
     q2 = low(project(normed_cross, cross_w[0]))
     k2, v2 = (low(project(encoder_states, cross_w[i])) for i in (1, 2))
     stages[2].turn(cross_w)
@@ -789,54 +805,70 @@
         [dq2, dk2, dv2, da2, da1],
         [(0, 0), (1, 1), (1, 2), (2, 3), (3, 4)],
         *ffout_sum.sent,
+        cost=lasting(100),
     )
     cross_sum.send()
-    do = low(project_back(da1, self_w[3]))
-    cross_sum.step("y")
     ffin_sum.step("z", *cross_sum.sent)
+    do = matmuls(
+        [da1],
+        [(self_w, 3)],
+        NT,
+        "self_do",
+        ffin_sum.sent,
+        cost=lasting(100),
+        dtype=jnp.bfloat16,
+    ).reshape(tokens.shape)
+    cross_sum.step("y", do)
 
     ready = cross_sum.sent + ffin_sum.sent
     cross_sum.send()
     ffin_sum.send()
     dq1, dk1, dv1, diagonals = attend("backward", q1, k1, v1, lengths, row, do, lse1, ready)
+    ffin_sum.finish(dq1)
+    cross_sum.step("x", ffin_sum.total)
+    cross_sum.send()
     self_sum = stage_grads(
-        place, [normed_self], [dq1, dk1, dv1], [(0, 0), (0, 1), (0, 2)]
-    )
-    ffout_sum.step("z", *self_sum.sent)
-    cross_sum.step("x", *self_sum.sent)
-    ready = self_sum.sent + ffout_sum.sent + cross_sum.sent
+        place, [normed_self], [dq1, dk1, dv1], [(0, 0), (0, 1), (0, 2)], *cross_sum.sent
+    )
     self_sum.send()
-    cross_sum.send()
+    ffout_sum.step("z", *self_sum.sent, cost=lasting(100))
     ffout_sum.send()
+    self_sum.step("y", *ffout_sum.sent)
+    self_sum.send()
     encoder_grad = matmuls(
-        [dk2, dv2], [(cross_w, 1), (cross_w, 2)], NT, "encoder_grad", ready, cost=lasting(100)
+        [dk2, dv2],
+        [(cross_w, 1), (cross_w, 2)],
+        NT,
+        "encoder_grad",
+        self_sum.sent,
+        cost=lasting(100),
     ).reshape(tokens.shape)
-    self_sum.step("y", encoder_grad)
-    self_sum.send()
     into = matmuls(
         [dq1, dk1, dv1],
         [(self_w, 0), (self_w, 1), (self_w, 2)],
         NT,
         "into",
-        self_sum.sent,
-        cost=lasting(200),
+        [encoder_grad],
     ).reshape(tokens.shape)
+    cross_sum.step("z", into)
+    cross_sum.send()
+    self_sum.step("x", *cross_sum.sent)
+    self_sum.send()
     grad_norm, gain_self = rms_back(stream, gains[0], into)
     token_grad = grad_middle + grad_norm
-    cross_sum.step("z", into)
-    cross_sum.send()
+    ffout_sum.finish(*self_sum.sent, cost=lasting(100))
+    ffin_sum.rows(ffout_sum.total)
     output_state = matmuls(
         [product],
         [(ffout, 0)],
         NN,
         "output_state",
-        cross_sum.sent,
+        [ffout_sum.total, ffin_sum.near],
         [later, jnp.broadcast_to(live, tokens.shape[:2] + (1,))],
     ).reshape(tokens.shape)
-    self_sum.step("x", output_state)
+    self_sum.step("z", output_state)
     self_sum.send()
-    ffin_sum.finish(*self_sum.sent)
-    ffout_sum.finish(*self_sum.sent)
+    cross_sum.finish(*self_sum.sent, cost=lasting(100))
     grad_table = jnp.einsum(
         "nb,hn->bh", hot, diagonals.reshape(heads, seq_len), precision=lax.Precision.HIGHEST
     )
@@ -849,11 +881,11 @@
         axis=1,
     )
     small = held_back(jnp.pad(small, ((0, 0), (0, -small_count % 128))), self_sum.sent)
-    small = reduce_small(place, small)
-    self_sum.step("z")
-    self_sum.send()
-    cross_sum.finish(*self_sum.sent)
-    self_sum.finish()
+    small = sum_owners(place, sum_replicas(place, small))
+    ffout_sum.rows(cross_sum.total)
+    cross_sum.rows(ffout_sum.near)
+    self_sum.finish(cross_sum.near)
+    self_sum.rows()
 
     def matrices(stage, size):
         near, far = stage.done()

time: 508 us -> 455 us (0.90)
  waiting for transfers between devices: 114 us -> 62.7 us
  Pallas kernels: 195 us -> 204 us
  local copies, waits for them, and re-layouts: 64.6 us -> 55.7 us
    ppermute x35, waiting for transfers between devices: 51 us -> 20 us  [across(): return lax.ppermute(v, 'rep', [(i, i ^ bit) for i in range(self.rep)])]
    ppermute x9, waiting for transfers between devices: 25.6 us -> 8.85 us  [along_x(): lax.ppermute(v, 'fsdp', [(i, i // nx * nx + (i % nx + d) % nx) for i in r...]
    pallas_call x40 -> x45, Pallas kernels: 195 us -> 204 us  [call(): pl.pallas_call(kernel, in_specs=list(specs or [VMEM] * count) + [pl.Block...]
    unnamed x308 -> x332, local copies, waits for them, and re-layouts: 49.4 us -> 42.4 us
  transfers between devices with their start and end apart: 68 -> 68, of which waited for: 23 -> 17; matrix products, arithmetic and copies ran while one was open for 12% -> 13% of each run, Pallas kernels for 29% -> 38%
where the time goes in v3:
time: 455 us; the launch traced here: 447 us
  Pallas kernels  204 us (45%)
  starting transfers between devices  71.6 us (16%)
  waiting for transfers between devices  62.7 us (14%)
  local copies, waits for them, and re-layouts  55.7 us (12%)
  other arithmetic  29.1 us (6%)
  matrix products  21 us (5%)
    pallas_call x45, Pallas kernels, call(): pl.pallas_call(kernel, in_specs=list(specs or [VMEM] * count) + [pl.Block...  204 us
    ppermute x24, starting transfers between devices, along_z(): lax.ppermute(v, 'fsdp', [(i, (i + d * self.nx) % self.fsdp) for i in rang...  46.8 us
    unnamed x332, local copies, waits for them, and re-layouts  42.4 us
    ppermute x24, waiting for transfers between devices, along_z(): lax.ppermute(v, 'fsdp', [(i, (i + d * self.nx) % self.fsdp) for i in rang...  33.9 us
    ppermute x35, waiting for transfers between devices, across(): return lax.ppermute(v, 'rep', [(i, i ^ bit) for i in range(self.rep)])  20 us
    ppermute x35, starting transfers between devices, across(): return lax.ppermute(v, 'rep', [(i, i ^ bit) for i in range(self.rep)])  16.4 us
    dot_general x8, matrix products, project(): return jnp.einsum('vgq,qy->vgy', a, w, preferred_element_type=jnp.float32)  15.2 us
    convert_element_type x6, other arithmetic, low(): return v.astype(jnp.bfloat16)  10.8 us
  transfers between devices with their start and end apart: 68, of which 17 were waited for; matrix products, arithmetic and copies ran while one was open for 13% of the time, Pallas kernels for 38%

profile of v3, /device:TPU:0, one launch (start us, length us, event | category | flops | bytes accessed | tf_op | source)
XLA Modules:
  0.0 447.3 jit_solution(11006400189360796561)
XLA Ops:
  13.0 5.7 %collective-permute-done.1.refs_2_ = bf16[592,128]{1,0:T(8,128)(2,1)S(1)} collective-permute-done((bf16[592,128]{1,0:T(8,128)(2,1)S(1)}, bf16[592,128]{1,0:T(8,128)(2,1)S(1)}, u32[]{:S(2)}, u32[]{:S(2)}) %collective-permute-start.1) | collective-permute-done | bytes 151584 | tf_op jit(solution)/shard_map/ppermute | solution.py:40
  31.4 4.6 %collective-permute-done.6.refs_2_ = bf16[576,128]{1,0:T(8,128)(2,1)S(1)} collective-permute-done((bf16[576,128]{1,0:T(8,128)(2,1)S(1)}, bf16[576,128]{1,0:T(8,128)(2,1)S(1)}, u32[]{:S(2)}, u32[]{:S(2)}) %collective-permute-start.6) | collective-permute-done | bytes 147488 | tf_op jit(solution)/shard_map/ppermute | solution.py:40
  47.3 4.5 collective-permute-done.13.refs_1_
  51.7 10.4 %collective-permute-done.14.refs_2_ = bf16[1152,128]{1,0:T(8,128)(2,1)S(1)} collective-permute-done((bf16[1152,128]{1,0:T(8,128)(2,1)S(1)}, bf16[1152,128]{1,0:T(8,128)(2,1)S(1)}, u32[]{:S(2)}, u32[]{:S(2)}) %collective-permute-start.14) | collective-permute-done | bytes 294944 | tf_op jit(solution)/shard_map/ppermute | solution.py:40
  83.4 17.1 %self_forward.1 = (bf16[2,512,768]{2,1,0:T(8,128)(2,1)S(1)}, f32[2,6,2,512]{3,2,1,0:T(2,128)S(1)}) custom-call(s32[2]{0:T(128)S(1)} %copy-done.72, bf16[2,512,768]{2,1,0:T(8,128)(2,1)S(1)} %convolution_convert_fusion.6.refs_1_, bf16[2,512,768]{2,1,0:T(8,128)(2,1)S(1)} %convolution_convert_fusion.5.refs_2_, ...), custom_call_target="tpu_custom_call" | custom-call | flops 199999995904 | tf_op jit(solution)/shard_map/self_forward/pallas_call | solution.py:81
  100.7 7.8 %collective-permute-done.21.refs_7_ = bf16[4,576,128]{2,1,0:T(8,128)(2,1)} collective-permute-done((bf16[4,576,128]{2,1,0:T(8,128)(2,1)}, bf16[4,576,128]{2,1,0:T(8,128)(2,1)}, u32[]{:S(2)}, u32[]{:S(2)}) %collective-permute-start.21) | collective-permute-done | bytes 589856 | tf_op jit(solution)/shard_map/ppermute | solution.py:35
  127.5 18.8 %cross_forward.1 = (bf16[2,512,768]{2,1,0:T(8,128)(2,1)S(1)}, f32[2,6,2,512]{3,2,1,0:T(2,128)S(1)}) custom-call(s32[2]{0:T(128)S(1)} %copy-done.81, bf16[2,512,768]{2,1,0:T(8,128)(2,1)S(1)} %convolution_convert_fusion.3.refs_1_, bf16[2,512,768]{2,1,0:T(8,128)(2,1)S(1)} %fusion.10.refs_2_, bf16[2,512,768]{2,1,0:T(8,128)(2,1)S(1)} %fusion.11.refs_3_, ...), custom_call_target="tpu_custom_call" | custom-call | flops 199999995904 | tf_op jit(solution)/shard_map/cross_forward/pallas_call | solution.py:81
  146.3 4.9 %collective-permute-done.28.refs_0_ = bf16[4,1152,128]{2,1,0:T(8,128)(2,1)} collective-permute-done((bf16[4,1152,128]{2,1,0:T(8,128)(2,1)}, bf16[4,1152,128]{2,1,0:T(8,128)(2,1)}, u32[]{:S(2)}, u32[]{:S(2)}) %collective-permute-start.28) | collective-permute-done | bytes 1179680 | tf_op jit(solution)/shard_map/ppermute | solution.py:31
  159.9 8.7 %assemble.5 = (bf16[2,8,2,48,2048]{4,3,2,1,0:T(8,128)(2,1)}, bf16[1,8,2,128,768]{4,3,2,1,0:T(8,128)(2,1)S(1)}) custom-call(s32[4]{0:T(128)S(1)} %copy-done.71, bf16[4,1152,128]{2,1,0:T(8,128)(2,1)} %stack.119.refs_9_.refs_6_.refs_1_, bf16[4,1152,128]{2,1,0:T(8,128)(2,1)} %collective-permute-done.24.refs_2_, bf16[4,1152,128]{2,1,0:T(8,128)(2,1)} %hold.7.refs_4_.refs_3_, ...), custom_call_target="tpu_custom_call" | custom-call | tf_op jit(solution)/shard_map/assemble/pallas_call | solution.py:81
  168.6 16.2 %feed.1 = (bf16[1024,2048]{1,0:T(8,128)(2,1)S(1)}, bf16[1024,2048]{1,0:T(8,128)(2,1)S(1)}, bf16[1024,2048]{1,0:T(8,128)(2,1)S(1)}) custom-call(bf16[1024,768]{1,0:T(8,128)(2,1)S(1)} %bitcast.213, bf16[1024,768]{1,0:T(8,128)(2,1)S(1)} %bitcast.211, bf16[2,768,2048]{2,1,0:T(8,128)(2,1)} %bitcast.244, bf16[2048,768]{1,0:T(8,128)(2,1)S(1)} %bitcast.224), custom_call_target="tpu_custom_call" | custom-call | flops 99999997952 | tf_op jit(solution)/shard_map/feed/pallas_call | solution.py:81
  186.8 10.4 %grads.4 = (bf16[768,2048]{1,0:T(8,128)(2,1)}, f32[768,2048]{1,0:T(8,128)}) custom-call(s32[1]{0:T(128)} %bitcast.refs_0_, bf16[1024,768]{1,0:T(8,128)(2,1)S(1)} %bitcast.214, bf16[1024,2048]{1,0:T(8,128)(2,1)S(1)} %get-tuple-element.74.refs_2_.refs_0_, bf16[1024,2048]{1,0:T(8,128)(2,1)S(1)} %get-tuple-element.75.refs_3_.refs_1_), custom_call_target="tpu_custom_call" | custom-call | tf_op jit(solution)/shard_map/grads/pallas_call | solution.py:81
  200.6 4.7 %grads.5 = (bf16[2048,384]{1,0:T(8,128)(2,1)}, f32[2048,384]{1,0:T(8,128)S(1)}) custom-call(s32[1]{0:T(128)} %bitcast.refs_0_, bf16[1024,2048]{1,0:T(8,128)(2,1)S(1)} %copy-done.12, bf16[1024,768]{1,0:T(8,128)(2,1)S(1)} %bitcast.212, bf16[8,2,48,2048]{3,2,1,0:T(8,128)(2,1)} %bitcast.47.refs_3_), custom_call_target="tpu_custom_call" | custom-call | tf_op jit(solution)/shard_map/grads/pallas_call | solution.py:81
  215.6 7.4 %grad_normed.1 = f32[1024,768]{1,0:T(8,128)S(1)} custom-call(bf16[1024,2048]{1,0:T(8,128)(2,1)S(1)} %copy-done.31, bf16[1024,2048]{1,0:T(8,128)(2,1)S(1)} %copy-done.33, bf16[2,768,2048]{2,1,0:T(8,128)(2,1)S(1)} %bitcast.245, bf16[2,768,2048]{2,1,0:T(8,128)(2,1)S(1)} %bitcast.246, bf16[4,2,48,2048]{3,2,1,0:T(8,128)(2,1)} %get-tuple-element.80.refs_3_.refs_4_.refs_7_), custom_call_target="tpu_custom_call" | custom-call | flops 99999997952 | tf_op jit(solution)/shard_map/grad_normed/pallas_call | solution.py:81
  232.5 21.7 %cross_backward.1 = (bf16[2,512,768]{2,1,0:T(8,128)(2,1)S(1)}, bf16[2,512,768]{2,1,0:T(8,128)(2,1)S(1)}, bf16[2,512,768]{2,1,0:T(8,128)(2,1)S(1)}) custom-call(s32[2]{0:T(128)S(1)} %copy-done.82, bf16[2,512,768]{2,1,0:T(8,128)(2,1)S(1)} %copy-done.100, bf16[2,512,768]{2,1,0:T(8,128)(2,1)S(1)} %copy-done.96, bf16[2,512,768]{2,1,0:T(8,128)(2,1)S(1)} %copy-done.98, ...), custom_call_target="tpu_custom_call" | custom-call | flops 199999995904 | tf_op jit(solution)/shard_map/cross_backward/pallas_call | solution.py:81
  259.3 6.3 %fusion.34 = (bf16[2,512,768]{2,1,0:T(8,128)(2,1)S(1)}, f32[2,512,768]{2,1,0:T(8,128)}) fusion(f32[2,512,768]{2,1,0:T(8,128)} %get-tuple-element.185, f32[2,512]{1,0:T(2,128)S(1)} %multiply_multiply_fusion.1, f32[2,512]{1,0:T(2,128)S(1)} %copy-done.140, f32[2,512,768]{2,1,0:T(8,128)} %get-tuple-element.188, f32[768]{0:T(1024)S(1)} %copy-done.138, ...), kind=kLoop, calls=%fused_computation.139 | loop fusion | flops 11796480 | bytes 18900992 | tf_op jit(solution)/shard_map/convert_element_type | solution.py:46
  278.9 9.1 %grads.6 = (bf16[768,1920]{1,0:T(8,128)(2,1)S(1)}, f32[768,1920]{1,0:T(8,128)}) custom-call(s32[1]{0:T(128)} %bitcast.refs_0_, bf16[1024,768]{1,0:T(8,128)(2,1)S(1)} %bitcast.232, bf16[1024,768]{1,0:T(8,128)(2,1)S(1)} %bitcast.249, bf16[1024,768]{1,0:T(8,128)(2,1)S(1)} %bitcast.204, bf16[1024,768]{1,0:T(8,128)(2,1)S(1)} %bitcast.234, ...), custom_call_target="tpu_custom_call" | custom-call | flops 99999997952 | tf_op jit(solution)/shard_map/grads/pallas_call | solution.py:81
  291.3 6.8 %collective-permute-start.38 = (bf16[48,2048]{1,0:T(8,128)(2,1)}, bf16[48,2048]{1,0:T(8,128)(2,1)}, u32[]{:S(2)}, u32[]{:S(2)}) collective-permute-start(bf16[48,2048]{1,0:T(8,128)(2,1)} %get-tuple-element.93.refs_2_.refs_8_), channel_id=1, source_target_pairs={{0,2},{1,3},{2,4},{3,5},{4,6},{5,7},{6,0},{7,1},{8,10},{9,11},{10,... | collective-permute-start | bytes 589832 | tf_op jit(solution)/shard_map/ppermute | solution.py:40
  306.7 25.9 %self_backward.1 = (bf16[2,512,768]{2,1,0:T(8,128)(2,1)S(1)}, bf16[2,512,768]{2,1,0:T(8,128)(2,1)S(1)}, bf16[2,512,768]{2,1,0:T(8,128)(2,1)S(1)}, f32[6,2,512]{2,1,0:T(2,128)S(1)}) custom-call(s32[2]{0:T(128)S(1)} %copy-done.73, bf16[2,512,768]{2,1,0:T(8,128)(2,1)S(1)} %copy-done.94, bf16[2,512,768]{2,1,0:T(8,128)(2,1)S(1)} %copy-done.92, ...), custom_call_target="tpu_custom_call" | custom-call | flops 199999995904 | tf_op jit(solution)/shard_map/self_backward/pallas_call | solution.py:81
  349.7 4.0 grads.7
  361.2 4.2 encoder_grad.1
  367.3 4.5 %into.1 = f32[1024,768]{1,0:T(8,128)S(1)} custom-call(bf16[1024,768]{1,0:T(8,128)(2,1)S(1)} %bitcast.203, bf16[1024,768]{1,0:T(8,128)(2,1)S(1)} %bitcast.208, bf16[1024,768]{1,0:T(8,128)(2,1)S(1)} %bitcast.210, bf16[4,768,768]{2,1,0:T(8,128)(2,1)S(1)} %bitcast.190, bf16[4,768,768]{2,1,0:T(8,128)(2,1)S(1)} %bitcast.191, bf16[4,768,768]{2,1,0:T(8,128)(2,1)S(1)} %bitcast.192, ...), custom_call_target="tpu_custom_call" | custom-call | tf_op jit(solution)/shard_map/into/pallas_call | solution.py:81
  388.8 4.9 %output_state.1 = f32[1024,768]{1,0:T(8,128)} custom-call(bf16[1024,2048]{1,0:T(8,128)(2,1)S(1)} %copy-done.13, bf16[1,2048,768]{2,1,0:T(8,128)(2,1)S(1)} %bitcast.225, f32[1024,768]{1,0:T(8,128)S(1)} %bitcast.193, f32[1024,1]{1,0:T(8,128)S(1)} %bitcast.229, f32[128,384]{1,0:T(8,128)S(1)} %total.5.refs_3_.refs_4_.refs_1_, f32[96,2048]{1,0:T(8,128)} %rows.4.refs_5_), custom_call_target="tpu_custom_call" | custom-call | tf_op jit(solution)/shard_map/output_state/pallas_call | solution.py:81
  410.7 4.9 %fusion.6 = f32[2,512,768]{2,1,0:T(8,128)} fusion(f32[2,512,768]{2,1,0:T(8,128)} %get-tuple-element.139, bf16[2,512,768]{2,1,0:T(8,128)(2,1)} %param.11, f32[2,512]{1,0:T(2,128)} %multiply_multiply_fusion, f32[768]{0:T(1024)S(1)} %copy-done.127, f32[2,512]{1,0:T(2,128)S(1)} %copy-done.125, f32[1024,768]{1,0:T(8,128)S(1)} %copy-done.8), kind=kLoop, calls=%fused_computation.14 | loop fusion | flops 5505024 | bytes 11021312 | tf_op jit(solution)/shard_map/add | solution.py:858
  435.4 5.1 %collective-permute-done.57.refs_2_ = f32[48,1152]{1,0:T(8,128)S(1)} collective-permute-done((f32[48,1152]{1,0:T(8,128)S(1)}, f32[48,1152]{1,0:T(8,128)S(1)}, u32[]{:S(2)}, u32[]{:S(2)}) %collective-permute-start.57) | collective-permute-done | bytes 221216 | tf_op jit(solution)/shard_map/ppermute | solution.py:31
  (599 shorter events, 225.7 us)
Async XLA Ops:
  37.0 25.7 %collective-permute-start.11 = (bf16[4,592,128]{2,1,0:T(8,128)(2,1)S(1)}, bf16[4,592,128]{2,1,0:T(8,128)(2,1)S(1)}, u32[]{:S(2)}, u32[]{:S(2)}) collective-permute-start(bf16[4,592,128]{2,1,0:T(8,128)(2,1)S(1)} %hold.5.refs_3_), channel_id=1, source_target_pairs={{0,16},{8,24},{16,0},{24,8},{1,17},{9,25},{17,1},{25,9},{2,18},{10... | collective-permute-start | bytes 1818632 | tf_op jit(solution)/shard_map/ppermute | solution.py:31
  42.4 19.7 %collective-permute-start.14 = (bf16[1152,128]{1,0:T(8,128)(2,1)S(1)}, bf16[1152,128]{1,0:T(8,128)(2,1)S(1)}, u32[]{:S(2)}, u32[]{:S(2)}) collective-permute-start(bf16[1152,128]{1,0:T(8,128)(2,1)S(1)} %pad_maximum_fusion.refs_0_), channel_id=1, source_target_pairs={{0,4},{1,5},{2,6},{3,7},{4,0},{5,1},{6,2},{7,3},{8,12},{9,13},{10,... | collective-permute-start | bytes 884744 | tf_op jit(solution)/shard_map/ppermute | solution.py:40
  67.1 33.4 %collective-permute-start.17 = (bf16[4,576,128]{2,1,0:T(8,128)(2,1)}, bf16[4,576,128]{2,1,0:T(8,128)(2,1)}, u32[]{:S(2)}, u32[]{:S(2)}) collective-permute-start(bf16[4,576,128]{2,1,0:T(8,128)(2,1)} %stack.118.refs_1_), channel_id=1, source_target_pairs={{0,8},{8,0},{16,24},{24,16},{1,9},{9,1},{17,25},{25,17},{2,10},{10... | collective-permute-start | bytes 1769480 | tf_op jit(solution)/shard_map/ppermute | solution.py:31
  67.3 51.8 %collective-permute-start.23 = (bf16[4,1152,128]{2,1,0:T(8,128)(2,1)}, bf16[4,1152,128]{2,1,0:T(8,128)(2,1)}, u32[]{:S(2)}, u32[]{:S(2)}) collective-permute-start(bf16[4,1152,128]{2,1,0:T(8,128)(2,1)} %stack.119.refs_9_.refs_6_.refs_1_), channel_id=1, source_target_pairs={{0,1},{1,0},{2,3},{3,2},{4,5},{5,4},{6,7},{7,6},{8,9},{9,8},{10,11... | collective-permute-start | bytes 3538952 | tf_op jit(solution)/shard_map/ppermute | solution.py:35
  67.8 46.7 %collective-permute-start.26 = (bf16[4,1152,128]{2,1,0:T(8,128)(2,1)}, bf16[4,1152,128]{2,1,0:T(8,128)(2,1)}, u32[]{:S(2)}, u32[]{:S(2)}) collective-permute-start(bf16[4,1152,128]{2,1,0:T(8,128)(2,1)} %stack.119.refs_9_.refs_6_.refs_1_), channel_id=1, source_target_pairs={{0,16},{8,24},{16,0},{24,8},{1,17},{9,25},{17,1},{25,9},{2,18},{10... | collective-permute-start | bytes 3538952 | tf_op jit(solution)/shard_map/ppermute | solution.py:31
  68.3 45.6 %collective-permute-start.19 = (bf16[4,576,128]{2,1,0:T(8,128)(2,1)}, bf16[4,576,128]{2,1,0:T(8,128)(2,1)}, u32[]{:S(2)}, u32[]{:S(2)}) collective-permute-start(bf16[4,576,128]{2,1,0:T(8,128)(2,1)} %collective-permute-done.18.refs_3_), channel_id=1, source_target_pairs={{0,8},{8,0},{16,24},{24,16},{1,9},{9,1},{17,25},{25,17},{2,10},{10... | collective-permute-start | bytes 1769480 | tf_op jit(solution)/shard_map/ppermute | solution.py:31
  82.8 25.7 %collective-permute-start.21 = (bf16[4,576,128]{2,1,0:T(8,128)(2,1)}, bf16[4,576,128]{2,1,0:T(8,128)(2,1)}, u32[]{:S(2)}, u32[]{:S(2)}) collective-permute-start(bf16[4,576,128]{2,1,0:T(8,128)(2,1)} %hold.6.refs_5_), channel_id=1, source_target_pairs={{0,1},{1,0},{2,3},{3,2},{4,5},{5,4},{6,7},{7,6},{8,9},{9,8},{10,11... | collective-permute-start | bytes 1769480 | tf_op jit(solution)/shard_map/ppermute | solution.py:35
  114.0 45.9 %collective-permute-start.24 = (bf16[4,1152,128]{2,1,0:T(8,128)(2,1)}, bf16[4,1152,128]{2,1,0:T(8,128)(2,1)}, u32[]{:S(2)}, u32[]{:S(2)}) collective-permute-start(bf16[4,1152,128]{2,1,0:T(8,128)(2,1)} %stack.119.refs_9_.refs_6_.refs_1_), channel_id=1, source_target_pairs={{0,8},{8,0},{16,24},{24,16},{1,9},{9,1},{17,25},{25,17},{2,10},{10... | collective-permute-start | bytes 3538952 | tf_op jit(solution)/shard_map/ppermute | solution.py:31
  114.5 45.3 %collective-permute-start.27 = (bf16[4,1152,128]{2,1,0:T(8,128)(2,1)}, bf16[4,1152,128]{2,1,0:T(8,128)(2,1)}, u32[]{:S(2)}, u32[]{:S(2)}) collective-permute-start(bf16[4,1152,128]{2,1,0:T(8,128)(2,1)} %collective-permute-done.26.refs_5_), channel_id=1, source_target_pairs={{0,8},{8,0},{16,24},{24,16},{1,9},{9,1},{17,25},{25,17},{2,10},{10... | collective-permute-start | bytes 3538952 | tf_op jit(solution)/shard_map/ppermute | solution.py:31
  122.5 28.6 %collective-permute-start.28 = (bf16[4,1152,128]{2,1,0:T(8,128)(2,1)}, bf16[4,1152,128]{2,1,0:T(8,128)(2,1)}, u32[]{:S(2)}, u32[]{:S(2)}) collective-permute-start(bf16[4,1152,128]{2,1,0:T(8,128)(2,1)} %hold.7.refs_4_.refs_3_), channel_id=1, source_target_pairs={{0,16},{8,24},{16,0},{24,8},{1,17},{9,25},{17,1},{25,9},{2,18},{10... | collective-permute-start | bytes 3538952 | tf_op jit(solution)/shard_map/ppermute | solution.py:31
  123.1 36.8 %collective-permute-start.25 = (bf16[4,1152,128]{2,1,0:T(8,128)(2,1)}, bf16[4,1152,128]{2,1,0:T(8,128)(2,1)}, u32[]{:S(2)}, u32[]{:S(2)}) collective-permute-start(bf16[4,1152,128]{2,1,0:T(8,128)(2,1)} %hold.7.refs_4_.refs_3_), channel_id=1, source_target_pairs={{0,8},{8,0},{16,24},{24,16},{1,9},{9,1},{17,25},{25,17},{2,10},{10... | collective-permute-start | bytes 3538952 | tf_op jit(solution)/shard_map/ppermute | solution.py:31
  206.9 21.4 %collective-permute-start.30 = (bf16[8,2,128,384]{3,2,1,0:T(8,128)(2,1)}, bf16[8,2,128,384]{3,2,1,0:T(8,128)(2,1)}, u32[]{:S(2)}, u32[]{:S(2)}) collective-permute-start(bf16[8,2,128,384]{3,2,1,0:T(8,128)(2,1)} %bitcast.49.refs_3_), channel_id=1, source_target_pairs={{0,8},{8,0},{16,24},{24,16},{1,9},{9,1},{17,25},{25,17},{2,10},{10... | collective-permute-start | bytes 4718600 | tf_op jit(solution)/shard_map/ppermute | solution.py:31
  223.0 42.6 %collective-permute-start.33 = (bf16[4,2,48,2048]{3,2,1,0:T(8,128)(2,1)}, bf16[4,2,48,2048]{3,2,1,0:T(8,128)(2,1)}, u32[]{:S(2)}, u32[]{:S(2)}) collective-permute-start(bf16[4,2,48,2048]{3,2,1,0:T(8,128)(2,1)} %get-tuple-element.80.refs_3_.refs_4_.refs_7_), channel_id=1, source_target_pairs={{0,1},{1,0},{2,3},{3,2},{4,5},{5,4},{6,7},{7,6},{8,9},{9,8},{10,11... | collective-permute-start | bytes 4718600 | tf_op jit(solution)/shard_map/ppermute | solution.py:35
  231.9 40.2 %collective-permute-start.32 = (bf16[4,2,128,384]{3,2,1,0:T(8,128)(2,1)}, bf16[4,2,128,384]{3,2,1,0:T(8,128)(2,1)}, u32[]{:S(2)}, u32[]{:S(2)}) collective-permute-start(bf16[4,2,128,384]{3,2,1,0:T(8,128)(2,1)} %get-tuple-element.82.refs_6_), channel_id=1, source_target_pairs={{0,16},{8,24},{16,0},{24,8},{1,17},{9,25},{17,1},{25,9},{2,18},{10... | collective-permute-start | bytes 2359304 | tf_op jit(solution)/shard_map/ppermute | solution.py:31
  275.1 78.7 %collective-permute-start.34 = (bf16[4,128,384]{2,1,0:T(8,128)(2,1)}, bf16[4,128,384]{2,1,0:T(8,128)(2,1)}, u32[]{:S(2)}, u32[]{:S(2)}) collective-permute-start(bf16[4,128,384]{2,1,0:T(8,128)(2,1)} %get-tuple-element.88.refs_10_), channel_id=1, source_target_pairs={{0,1},{1,0},{2,3},{3,2},{4,5},{5,4},{6,7},{7,6},{8,9},{9,8},{10,11... | collective-permute-start | bytes 1179656 | tf_op jit(solution)/shard_map/ppermute | solution.py:35
  291.3 48.3 %collective-permute-start.38 = (bf16[48,2048]{1,0:T(8,128)(2,1)}, bf16[48,2048]{1,0:T(8,128)(2,1)}, u32[]{:S(2)}, u32[]{:S(2)}) collective-permute-start(bf16[48,2048]{1,0:T(8,128)(2,1)} %get-tuple-element.93.refs_2_.refs_8_), channel_id=1, source_target_pairs={{0,2},{1,3},{2,4},{3,5},{4,6},{5,7},{6,0},{7,1},{8,10},{9,11},{10,... | collective-permute-start | bytes 589832 | tf_op jit(solution)/shard_map/ppermute | solution.py:40
  298.1 41.5 %collective-permute-start.39 = (bf16[48,2048]{1,0:T(8,128)(2,1)}, bf16[48,2048]{1,0:T(8,128)(2,1)}, u32[]{:S(2)}, u32[]{:S(2)}) collective-permute-start(bf16[48,2048]{1,0:T(8,128)(2,1)} %get-tuple-element.94.refs_3_.refs_9_), channel_id=1, source_target_pairs={{0,4},{1,5},{2,6},{3,7},{4,0},{5,1},{6,2},{7,3},{8,12},{9,13},{10,... | collective-permute-start | bytes 589832 | tf_op jit(solution)/shard_map/ppermute | solution.py:40
  302.4 37.2 %collective-permute-start.40 = (bf16[48,2048]{1,0:T(8,128)(2,1)}, bf16[48,2048]{1,0:T(8,128)(2,1)}, u32[]{:S(2)}, u32[]{:S(2)}) collective-permute-start(bf16[48,2048]{1,0:T(8,128)(2,1)} %get-tuple-element.95.refs_4_.refs_10_), channel_id=1, source_target_pairs={{0,6},{1,7},{2,0},{3,1},{4,2},{5,3},{6,4},{7,5},{8,14},{9,15},{10,... | collective-permute-start | bytes 589832 | tf_op jit(solution)/shard_map/ppermute | solution.py:40
  304.7 39.6 %collective-permute-start.37 = (bf16[4,2,48,1920]{3,2,1,0:T(8,128)(2,1)}, bf16[4,2,48,1920]{3,2,1,0:T(8,128)(2,1)}, u32[]{:S(2)}, u32[]{:S(2)}) collective-permute-start(bf16[4,2,48,1920]{3,2,1,0:T(8,128)(2,1)} %get-tuple-element.98.refs_7_), channel_id=1, source_target_pairs={{0,16},{8,24},{16,0},{24,8},{1,17},{9,25},{17,1},{25,9},{2,18},{10... | collective-permute-start | bytes 4423688 | tf_op jit(solution)/shard_map/ppermute | solution.py:31
  343.1 43.1 %collective-permute-start.47 = (f32[48,2048]{1,0:T(8,128)}, f32[48,2048]{1,0:T(8,128)}, u32[]{:S(2)}, u32[]{:S(2)}) collective-permute-start(f32[48,2048]{1,0:T(8,128)} %total.4.refs_3_.refs_1_), channel_id=1, source_target_pairs={{0,16},{8,24},{16,0},{24,8},{1,17},{9,25},{17,1},{25,9},{2,18},{10... | collective-permute-start | bytes 1179656 | tf_op jit(solution)/shard_map/ppermute | solution.py:31
  348.9 24.8 %collective-permute-start.46 = (bf16[4,48,1920]{2,1,0:T(8,128)(2,1)}, bf16[4,48,1920]{2,1,0:T(8,128)(2,1)}, u32[]{:S(2)}, u32[]{:S(2)}) collective-permute-start(bf16[4,48,1920]{2,1,0:T(8,128)(2,1)} %get-tuple-element.104.refs_5_), channel_id=1, source_target_pairs={{0,1},{1,0},{2,3},{3,2},{4,5},{5,4},{6,7},{7,6},{8,9},{9,8},{10,11... | collective-permute-start | bytes 2211848 | tf_op jit(solution)/shard_map/ppermute | solution.py:35
  355.7 29.2 %collective-permute-start.41 = (bf16[128,384]{1,0:T(8,128)(2,1)}, bf16[128,384]{1,0:T(8,128)(2,1)}, u32[]{:S(2)}, u32[]{:S(2)}) collective-permute-start(bf16[128,384]{1,0:T(8,128)(2,1)} %get-tuple-element.107.refs_3_), channel_id=1, source_target_pairs={{0,2},{1,3},{2,4},{3,5},{4,6},{5,7},{6,0},{7,1},{8,10},{9,11},{10,... | collective-permute-start | bytes 294920 | tf_op jit(solution)/shard_map/ppermute | solution.py:40
  357.1 27.8 %collective-permute-start.42 = (bf16[128,384]{1,0:T(8,128)(2,1)}, bf16[128,384]{1,0:T(8,128)(2,1)}, u32[]{:S(2)}, u32[]{:S(2)}) collective-permute-start(bf16[128,384]{1,0:T(8,128)(2,1)} %get-tuple-element.108.refs_4_), channel_id=1, source_target_pairs={{0,4},{1,5},{2,6},{3,7},{4,0},{5,1},{6,2},{7,3},{8,12},{9,13},{10,... | collective-permute-start | bytes 294920 | tf_op jit(solution)/shard_map/ppermute | solution.py:40
  360.4 21.8 %collective-permute-start.45 = (bf16[4,2,48,1152]{3,2,1,0:T(8,128)(2,1)}, bf16[4,2,48,1152]{3,2,1,0:T(8,128)(2,1)}, u32[]{:S(2)}, u32[]{:S(2)}) collective-permute-start(bf16[4,2,48,1152]{3,2,1,0:T(8,128)(2,1)} %get-tuple-element.112.refs_4_), channel_id=1, source_target_pairs={{0,16},{8,24},{16,0},{24,8},{1,17},{9,25},{17,1},{25,9},{2,18},{10... | collective-permute-start | bytes 2654216 | tf_op jit(solution)/shard_map/ppermute | solution.py:31
  (207 other events, 1496.7 us)

commit v4 on v3

--- a/solution.py
+++ b/solution.py
@@ -71,7 +71,7 @@
     return jax.ShapeDtypeStruct(shape, dtype)
 
 
-def call(body, ins, outs, name, waits=(), specs=None, vmem=32, cost=FREE, **kw):
+def call(body, ins, outs, name, waits=(), specs=None, vmem=16, cost=FREE, **kw):
     waits = list(waits)
     count, late = len(ins), len(ins) + len(waits)
 
@@ -196,7 +196,7 @@
             small=self.small is not None,
         )
         specs = [SMEM] + [VMEM] * len(arrays)
-        full = call(body, [where] + arrays, shapes, "assemble", waits, specs, vmem=36)
+        full = call(body, [where] + arrays, shapes, "assemble", waits, specs, vmem=28)
         whole = [
             v.reshape(m, place.fsdp * 2 * h, 2 * w) for v, (m, h, w) in zip(full, self.sizes)
         ]
@@ -268,7 +268,7 @@
         ins = [own, self.kept] + self.got
         specs = [SMEM] + [VMEM] * (len(ins) - 1)
         self.kept, *self.sent = call(
-            body, ins, outs, "step_" + name, waits, specs, cost=cost
+            body, ins, outs, "step_" + name, waits, specs, vmem=20, cost=cost
         )
         self.axes.remove(name)
         self.name = name
@@ -527,7 +527,7 @@
         ("self_" if causal else "cross_") + kind,
         waits,
         specs,
-        vmem=24,
+        vmem=16,
         cost=lasting(200),
         grid=(pairs, count),
         out_specs=out_specs,
@@ -588,6 +588,7 @@
         (),
         specs,
         cost=lasting(100),
+        vmem=24,
         grid=(hidden // FF_TILE,),
         out_specs=[tile] * 3,
     )
@@ -622,6 +623,7 @@
         name,
         waits,
         [tile(v) for v in lefts] + [layer(*w) for w in weights] + [tile(v) for v in ends],
+        vmem=24,
         cost=cost,
         grid=(rows // ROW_TILE,),
         out_specs=tile(out),
@@ -663,7 +665,7 @@
         "grads",
         waits,
         [SMEM] + [VMEM] * (len(ins) - 1),
-        vmem=36,
+        vmem=28,
         cost=cost,
     )
     shape = (place.fsdp, 2, height // place.fsdp // 2, width)
@@ -824,14 +826,14 @@
     cross_sum.send()
     ffin_sum.send()
     dq1, dk1, dv1, diagonals = attend("backward", q1, k1, v1, lengths, row, do, lse1, ready)
-    ffin_sum.finish(dq1)
-    cross_sum.step("x", ffin_sum.total)
+    cross_sum.step("x", dq1)
     cross_sum.send()
     self_sum = stage_grads(
         place, [normed_self], [dq1, dk1, dv1], [(0, 0), (0, 1), (0, 2)], *cross_sum.sent
     )
     self_sum.send()
     ffout_sum.step("z", *self_sum.sent, cost=lasting(100))
+    ffin_sum.finish(*ffout_sum.sent)
     ffout_sum.send()
     self_sum.step("y", *ffout_sum.sent)
     self_sum.send()
@@ -848,7 +850,7 @@
         [(self_w, 0), (self_w, 1), (self_w, 2)],
         NT,
         "into",
-        [encoder_grad],
+        [encoder_grad, ffin_sum.total],
     ).reshape(tokens.shape)
     cross_sum.step("z", into)
     cross_sum.send()
@@ -869,6 +871,7 @@
     self_sum.step("z", output_state)
     self_sum.send()
     cross_sum.finish(*self_sum.sent, cost=lasting(100))
+    diagonals = held_back(diagonals, [output_state])
     grad_table = jnp.einsum(
         "nb,hn->bh", hot, diagonals.reshape(heads, seq_len), precision=lax.Precision.HIGHEST
     )

time: 455 us -> 448 us (0.985)
  Pallas kernels: 204 us -> 192 us
  waiting for transfers between devices: 62.7 us -> 71.6 us
  local copies, waits for them, and re-layouts: 55.7 us -> 50.8 us
    pallas_call x45 -> x46, Pallas kernels: 204 us -> 192 us  [call(): pl.pallas_call(kernel, in_specs=list(specs or [VMEM] * count) + [pl.Block...]
    ppermute x35, waiting for transfers between devices: 20 us -> 29.7 us  [across(): return lax.ppermute(v, 'rep', [(i, i ^ bit) for i in range(self.rep)])]
    unnamed x332 -> x308, local copies, waits for them, and re-layouts: 42.4 us -> 37.3 us
  transfers between devices with their start and end apart: 68 -> 68, of which waited for: 17 -> 18; matrix products, arithmetic and copies ran while one was open for 13% -> 14% of each run, Pallas kernels for 38% -> 36%
where the time goes in v4:
time: 448 us; the launch traced here: 440 us
  Pallas kernels  192 us (43%)
  waiting for transfers between devices  71.6 us (16%)
  starting transfers between devices  70.3 us (16%)
  local copies, waits for them, and re-layouts  50.8 us (11%)
  other arithmetic  32 us (7%)
  matrix products  20.4 us (5%)
    pallas_call x46, Pallas kernels, call(): pl.pallas_call(kernel, in_specs=list(specs or [VMEM] * count) + [pl.Block...  192 us
    ppermute x24, starting transfers between devices, along_z(): lax.ppermute(v, 'fsdp', [(i, (i + d * self.nx) % self.fsdp) for i in rang...  46.4 us
    unnamed x308, local copies, waits for them, and re-layouts  37.3 us
    ppermute x24, waiting for transfers between devices, along_z(): lax.ppermute(v, 'fsdp', [(i, (i + d * self.nx) % self.fsdp) for i in rang...  34.1 us
    ppermute x35, waiting for transfers between devices, across(): return lax.ppermute(v, 'rep', [(i, i ^ bit) for i in range(self.rep)])  29.7 us
    ppermute x35, starting transfers between devices, across(): return lax.ppermute(v, 'rep', [(i, i ^ bit) for i in range(self.rep)])  15.3 us
    dot_general x8, matrix products, project(): return jnp.einsum('vgq,qy->vgy', a, w, preferred_element_type=jnp.float32)  15.3 us
    convert_element_type x6, other arithmetic, low(): return v.astype(jnp.bfloat16)  10.8 us
  transfers between devices with their start and end apart: 68, of which 18 were waited for; matrix products, arithmetic and copies ran while one was open for 14% of the time, Pallas kernels for 36%

profile of v4, /device:TPU:0, one launch (start us, length us, event | category | flops | bytes accessed | tf_op | source)
XLA Modules:
  0.0 440.5 jit_solution(16535361385018524191)
XLA Ops:
  13.0 5.7 %collective-permute-done.1.refs_2_ = bf16[592,128]{1,0:T(8,128)(2,1)S(1)} collective-permute-done((bf16[592,128]{1,0:T(8,128)(2,1)S(1)}, bf16[592,128]{1,0:T(8,128)(2,1)S(1)}, u32[]{:S(2)}, u32[]{:S(2)}) %collective-permute-start.1) | collective-permute-done | bytes 151584 | tf_op jit(solution)/shard_map/ppermute | solution.py:40
  31.4 4.6 %collective-permute-done.6.refs_2_ = bf16[576,128]{1,0:T(8,128)(2,1)S(1)} collective-permute-done((bf16[576,128]{1,0:T(8,128)(2,1)S(1)}, bf16[576,128]{1,0:T(8,128)(2,1)S(1)}, u32[]{:S(2)}, u32[]{:S(2)}) %collective-permute-start.6) | collective-permute-done | bytes 147488 | tf_op jit(solution)/shard_map/ppermute | solution.py:40
  47.3 4.5 %collective-permute-done.13.refs_1_ = bf16[1152,128]{1,0:T(8,128)(2,1)S(1)} collective-permute-done((bf16[1152,128]{1,0:T(8,128)(2,1)S(1)}, bf16[1152,128]{1,0:T(8,128)(2,1)S(1)}, u32[]{:S(2)}, u32[]{:S(2)}) %collective-permute-start.13) | collective-permute-done | bytes 294944 | tf_op jit(solution)/shard_map/ppermute | solution.py:40
  51.7 10.4 %collective-permute-done.14.refs_2_ = bf16[1152,128]{1,0:T(8,128)(2,1)S(1)} collective-permute-done((bf16[1152,128]{1,0:T(8,128)(2,1)S(1)}, bf16[1152,128]{1,0:T(8,128)(2,1)S(1)}, u32[]{:S(2)}, u32[]{:S(2)}) %collective-permute-start.14) | collective-permute-done | bytes 294944 | tf_op jit(solution)/shard_map/ppermute | solution.py:40
  83.4 17.1 %self_forward.1 = (bf16[2,512,768]{2,1,0:T(8,128)(2,1)S(1)}, f32[2,6,2,512]{3,2,1,0:T(2,128)S(1)}) custom-call(s32[2]{0:T(128)S(1)} %copy-done.67, bf16[2,512,768]{2,1,0:T(8,128)(2,1)S(1)} %convolution_convert_fusion.6.refs_1_, bf16[2,512,768]{2,1,0:T(8,128)(2,1)S(1)} %convolution_convert_fusion.5.refs_2_, ...), custom_call_target="tpu_custom_call" | custom-call | flops 199999995904 | tf_op jit(solution)/shard_map/self_forward/pallas_call | solution.py:81
  100.7 7.8 %collective-permute-done.21.refs_7_ = bf16[4,576,128]{2,1,0:T(8,128)(2,1)} collective-permute-done((bf16[4,576,128]{2,1,0:T(8,128)(2,1)}, bf16[4,576,128]{2,1,0:T(8,128)(2,1)}, u32[]{:S(2)}, u32[]{:S(2)}) %collective-permute-start.21) | collective-permute-done | bytes 589856 | tf_op jit(solution)/shard_map/ppermute | solution.py:35
  127.5 18.8 %cross_forward.1 = (bf16[2,512,768]{2,1,0:T(8,128)(2,1)S(1)}, f32[2,6,2,512]{3,2,1,0:T(2,128)S(1)}) custom-call(s32[2]{0:T(128)S(1)} %copy-done.76, bf16[2,512,768]{2,1,0:T(8,128)(2,1)S(1)} %convolution_convert_fusion.3.refs_1_, bf16[2,512,768]{2,1,0:T(8,128)(2,1)S(1)} %fusion.10.refs_2_, bf16[2,512,768]{2,1,0:T(8,128)(2,1)S(1)} %fusion.11.refs_3_, ...), custom_call_target="tpu_custom_call" | custom-call | flops 199999995904 | tf_op jit(solution)/shard_map/cross_forward/pallas_call | solution.py:81
  146.3 4.8 %collective-permute-done.28.refs_0_ = bf16[4,1152,128]{2,1,0:T(8,128)(2,1)} collective-permute-done((bf16[4,1152,128]{2,1,0:T(8,128)(2,1)}, bf16[4,1152,128]{2,1,0:T(8,128)(2,1)}, u32[]{:S(2)}, u32[]{:S(2)}) %collective-permute-start.28) | collective-permute-done | bytes 1179680 | tf_op jit(solution)/shard_map/ppermute | solution.py:31
  160.0 6.0 %assemble.5 = (bf16[2,8,2,48,2048]{4,3,2,1,0:T(8,128)(2,1)S(1)}, bf16[1,8,2,128,768]{4,3,2,1,0:T(8,128)(2,1)S(1)}) custom-call(s32[4]{0:T(128)S(1)} %copy-done.66, bf16[4,1152,128]{2,1,0:T(8,128)(2,1)} %stack.119.refs_9_.refs_6_.refs_1_, bf16[4,1152,128]{2,1,0:T(8,128)(2,1)} %collective-permute-done.24.refs_2_, bf16[4,1152,128]{2,1,0:T(8,128)(2,1)} %hold.8.refs_4_.refs_3_, ...), custom_call_target="tpu_custom_call" | custom-call | tf_op jit(solution)/shard_map/assemble/pallas_call | solution.py:81
  166.0 15.1 %feed.1 = (bf16[1024,2048]{1,0:T(8,128)(2,1)S(1)}, bf16[1024,2048]{1,0:T(8,128)(2,1)S(1)}, bf16[1024,2048]{1,0:T(8,128)(2,1)S(1)}) custom-call(bf16[1024,768]{1,0:T(8,128)(2,1)S(1)} %bitcast.212, bf16[1024,768]{1,0:T(8,128)(2,1)S(1)} %bitcast.210, bf16[2,768,2048]{2,1,0:T(8,128)(2,1)S(1)} %bitcast.244, bf16[2048,768]{1,0:T(8,128)(2,1)S(1)} %bitcast.221), custom_call_target="tpu_custom_call" | custom-call | flops 99999997952 | tf_op jit(solution)/shard_map/feed/pallas_call | solution.py:81
  183.2 8.4 %grads.4 = (bf16[768,2048]{1,0:T(8,128)(2,1)}, f32[768,2048]{1,0:T(8,128)S(1)}) custom-call(s32[1]{0:T(128)} %bitcast.refs_0_, bf16[1024,768]{1,0:T(8,128)(2,1)S(1)} %bitcast.213, bf16[1024,2048]{1,0:T(8,128)(2,1)S(1)} %get-tuple-element.74.refs_2_.refs_0_, bf16[1024,2048]{1,0:T(8,128)(2,1)S(1)} %get-tuple-element.75.refs_3_.refs_1_), custom_call_target="tpu_custom_call" | custom-call | tf_op jit(solution)/shard_map/grads/pallas_call | solution.py:81
  209.9 7.4 %grad_normed.1 = f32[1024,768]{1,0:T(8,128)S(1)} custom-call(bf16[1024,2048]{1,0:T(8,128)(2,1)S(1)} %copy-done.29, bf16[1024,2048]{1,0:T(8,128)(2,1)S(1)} %copy-done.31, bf16[2,768,2048]{2,1,0:T(8,128)(2,1)S(1)} %bitcast.245, bf16[2,768,2048]{2,1,0:T(8,128)(2,1)S(1)} %bitcast.246, bf16[4,2,48,2048]{3,2,1,0:T(8,128)(2,1)} %get-tuple-element.80.refs_3_.refs_4_.refs_7_), custom_call_target="tpu_custom_call" | custom-call | flops 99999997952 | tf_op jit(solution)/shard_map/grad_normed/pallas_call | solution.py:81
  225.8 21.7 %cross_backward.1 = (bf16[2,512,768]{2,1,0:T(8,128)(2,1)S(1)}, bf16[2,512,768]{2,1,0:T(8,128)(2,1)S(1)}, bf16[2,512,768]{2,1,0:T(8,128)(2,1)S(1)}) custom-call(s32[2]{0:T(128)S(1)} %copy-done.77, bf16[2,512,768]{2,1,0:T(8,128)(2,1)S(1)} %copy-done.95, bf16[2,512,768]{2,1,0:T(8,128)(2,1)S(1)} %copy-done.91, bf16[2,512,768]{2,1,0:T(8,128)(2,1)S(1)} %copy-done.93, ...), custom_call_target="tpu_custom_call" | custom-call | flops 199999995904 | tf_op jit(solution)/shard_map/cross_backward/pallas_call | solution.py:81
  252.7 6.3 %fusion.34 = (bf16[2,512,768]{2,1,0:T(8,128)(2,1)S(1)}, f32[2,512,768]{2,1,0:T(8,128)}) fusion(f32[2,512,768]{2,1,0:T(8,128)} %get-tuple-element.185, f32[2,512]{1,0:T(2,128)S(1)} %multiply_multiply_fusion.1, f32[2,512]{1,0:T(2,128)S(1)} %copy-done.133, f32[2,512,768]{2,1,0:T(8,128)} %get-tuple-element.188, f32[768]{0:T(1024)S(1)} %copy-done.131, ...), kind=kLoop, calls=%fused_computation.139 | loop fusion | flops 11796480 | bytes 18900992 | tf_op jit(solution)/shard_map/convert_element_type | solution.py:46
  268.6 6.6 %grads.6 = (bf16[768,1920]{1,0:T(8,128)(2,1)S(1)}, f32[768,1920]{1,0:T(8,128)S(1)}) custom-call(s32[1]{0:T(128)} %bitcast.refs_0_, bf16[1024,768]{1,0:T(8,128)(2,1)S(1)} %bitcast.229, bf16[1024,768]{1,0:T(8,128)(2,1)S(1)} %bitcast.249, bf16[1024,768]{1,0:T(8,128)(2,1)S(1)} %bitcast.205, bf16[1024,768]{1,0:T(8,128)(2,1)S(1)} %bitcast.232, ...), custom_call_target="tpu_custom_call" | custom-call | flops 99999997952 | tf_op jit(solution)/shard_map/grads/pallas_call | solution.py:81
  275.2 6.0 %collective-permute-done.35.refs_2_ = bf16[4,48,2048]{2,1,0:T(8,128)(2,1)S(1)} collective-permute-done((bf16[4,48,2048]{2,1,0:T(8,128)(2,1)S(1)}, bf16[4,48,2048]{2,1,0:T(8,128)(2,1)S(1)}, u32[]{:S(2)}, u32[]{:S(2)}) %collective-permute-start.35) | collective-permute-done | bytes 786464 | tf_op jit(solution)/shard_map/ppermute | solution.py:31
  282.2 6.8 %collective-permute-start.44 = (bf16[48,2048]{1,0:T(8,128)(2,1)}, bf16[48,2048]{1,0:T(8,128)(2,1)}, u32[]{:S(2)}, u32[]{:S(2)}) collective-permute-start(bf16[48,2048]{1,0:T(8,128)(2,1)} %get-tuple-element.93.refs_2_.refs_8_), channel_id=1, source_target_pairs={{0,2},{1,3},{2,4},{3,5},{4,6},{5,7},{6,0},{7,1},{8,10},{9,11},{10,... | collective-permute-start | bytes 589832 | tf_op jit(solution)/shard_map/ppermute | solution.py:40
  296.4 25.9 %self_backward.1 = (bf16[2,512,768]{2,1,0:T(8,128)(2,1)S(1)}, bf16[2,512,768]{2,1,0:T(8,128)(2,1)S(1)}, bf16[2,512,768]{2,1,0:T(8,128)(2,1)S(1)}, f32[6,2,512]{2,1,0:T(2,128)S(1)}) custom-call(s32[2]{0:T(128)S(1)} %copy-done.67, bf16[2,512,768]{2,1,0:T(8,128)(2,1)S(1)} %copy-done.89, bf16[2,512,768]{2,1,0:T(8,128)(2,1)S(1)} %copy-done.87, ...), custom_call_target="tpu_custom_call" | custom-call | flops 199999995904 | tf_op jit(solution)/shard_map/self_backward/pallas_call | solution.py:81
  322.3 6.1 %collective-permute-done.37.refs_2_ = bf16[4,2,48,1920]{3,2,1,0:T(8,128)(2,1)} collective-permute-done((bf16[4,2,48,1920]{3,2,1,0:T(8,128)(2,1)}, bf16[4,2,48,1920]{3,2,1,0:T(8,128)(2,1)}, u32[]{:S(2)}, u32[]{:S(2)}) %collective-permute-start.37) | collective-permute-done | bytes 1474592 | tf_op jit(solution)/shard_map/ppermute | solution.py:31
  347.0 4.2 encoder_grad.1
  353.1 4.5 %into.1 = f32[1024,768]{1,0:T(8,128)S(1)} custom-call(bf16[1024,768]{1,0:T(8,128)(2,1)S(1)} %bitcast.204, bf16[1024,768]{1,0:T(8,128)(2,1)S(1)} %bitcast.207, bf16[1024,768]{1,0:T(8,128)(2,1)S(1)} %bitcast.209, bf16[4,768,768]{2,1,0:T(8,128)(2,1)S(1)} %bitcast.188, bf16[4,768,768]{2,1,0:T(8,128)(2,1)S(1)} %bitcast.189, bf16[4,768,768]{2,1,0:T(8,128)(2,1)S(1)} %bitcast.190, ...), custom_call_target="tpu_custom_call" | custom-call | tf_op jit(solution)/shard_map/into/pallas_call | solution.py:81
  377.3 4.9 %output_state.1 = f32[1024,768]{1,0:T(8,128)} custom-call(bf16[1024,2048]{1,0:T(8,128)(2,1)S(1)} %copy-done.15, bf16[1,2048,768]{2,1,0:T(8,128)(2,1)S(1)} %bitcast.222, f32[1024,768]{1,0:T(8,128)S(1)} %bitcast.191, f32[1024,1]{1,0:T(8,128)S(1)} %bitcast.226, f32[128,384]{1,0:T(8,128)S(1)} %total.5.refs_3_.refs_4_.refs_1_, f32[96,2048]{1,0:T(8,128)} %rows.4.refs_5_), custom_call_target="tpu_custom_call" | custom-call | tf_op jit(solution)/shard_map/output_state/pallas_call | solution.py:81
  403.6 4.9 %fusion.6 = f32[2,512,768]{2,1,0:T(8,128)} fusion(f32[2,512,768]{2,1,0:T(8,128)} %get-tuple-element.139, bf16[2,512,768]{2,1,0:T(8,128)(2,1)} %param.11, f32[2,512]{1,0:T(2,128)} %multiply_multiply_fusion, f32[768]{0:T(1024)} %copy-done.120, f32[2,512]{1,0:T(2,128)S(1)} %copy-done.119, f32[1024,768]{1,0:T(8,128)S(1)} %copy-done.8), kind=kLoop, calls=%fused_computation.14 | loop fusion | flops 5505024 | bytes 11021312 | tf_op jit(solution)/shard_map/add | solution.py:860
  428.3 5.4 %collective-permute-done.57.refs_2_ = f32[48,1152]{1,0:T(8,128)S(1)} collective-permute-done((f32[48,1152]{1,0:T(8,128)S(1)}, f32[48,1152]{1,0:T(8,128)S(1)}, u32[]{:S(2)}, u32[]{:S(2)}) %collective-permute-start.57) | collective-permute-done | bytes 221216 | tf_op jit(solution)/shard_map/ppermute | solution.py:31
  (574 shorter events, 223.4 us)
Async XLA Ops:
  37.0 25.7 %collective-permute-start.11 = (bf16[4,592,128]{2,1,0:T(8,128)(2,1)S(1)}, bf16[4,592,128]{2,1,0:T(8,128)(2,1)S(1)}, u32[]{:S(2)}, u32[]{:S(2)}) collective-permute-start(bf16[4,592,128]{2,1,0:T(8,128)(2,1)S(1)} %hold.6.refs_3_), channel_id=1, source_target_pairs={{0,16},{8,24},{16,0},{24,8},{1,17},{9,25},{17,1},{25,9},{2,18},{10... | collective-permute-start | bytes 1818632 | tf_op jit(solution)/shard_map/ppermute | solution.py:31
  42.4 19.7 %collective-permute-start.14 = (bf16[1152,128]{1,0:T(8,128)(2,1)S(1)}, bf16[1152,128]{1,0:T(8,128)(2,1)S(1)}, u32[]{:S(2)}, u32[]{:S(2)}) collective-permute-start(bf16[1152,128]{1,0:T(8,128)(2,1)S(1)} %pad_maximum_fusion.refs_0_), channel_id=1, source_target_pairs={{0,4},{1,5},{2,6},{3,7},{4,0},{5,1},{6,2},{7,3},{8,12},{9,13},{10,... | collective-permute-start | bytes 884744 | tf_op jit(solution)/shard_map/ppermute | solution.py:40
  67.1 33.4 %collective-permute-start.17 = (bf16[4,576,128]{2,1,0:T(8,128)(2,1)}, bf16[4,576,128]{2,1,0:T(8,128)(2,1)}, u32[]{:S(2)}, u32[]{:S(2)}) collective-permute-start(bf16[4,576,128]{2,1,0:T(8,128)(2,1)} %stack.118.refs_1_), channel_id=1, source_target_pairs={{0,8},{8,0},{16,24},{24,16},{1,9},{9,1},{17,25},{25,17},{2,10},{10... | collective-permute-start | bytes 1769480 | tf_op jit(solution)/shard_map/ppermute | solution.py:31
  67.3 51.9 %collective-permute-start.23 = (bf16[4,1152,128]{2,1,0:T(8,128)(2,1)}, bf16[4,1152,128]{2,1,0:T(8,128)(2,1)}, u32[]{:S(2)}, u32[]{:S(2)}) collective-permute-start(bf16[4,1152,128]{2,1,0:T(8,128)(2,1)} %stack.119.refs_9_.refs_6_.refs_1_), channel_id=1, source_target_pairs={{0,1},{1,0},{2,3},{3,2},{4,5},{5,4},{6,7},{7,6},{8,9},{9,8},{10,11... | collective-permute-start | bytes 3538952 | tf_op jit(solution)/shard_map/ppermute | solution.py:35
  67.8 46.7 %collective-permute-start.26 = (bf16[4,1152,128]{2,1,0:T(8,128)(2,1)}, bf16[4,1152,128]{2,1,0:T(8,128)(2,1)}, u32[]{:S(2)}, u32[]{:S(2)}) collective-permute-start(bf16[4,1152,128]{2,1,0:T(8,128)(2,1)} %stack.119.refs_9_.refs_6_.refs_1_), channel_id=1, source_target_pairs={{0,16},{8,24},{16,0},{24,8},{1,17},{9,25},{17,1},{25,9},{2,18},{10... | collective-permute-start | bytes 3538952 | tf_op jit(solution)/shard_map/ppermute | solution.py:31
  68.3 45.6 %collective-permute-start.19 = (bf16[4,576,128]{2,1,0:T(8,128)(2,1)}, bf16[4,576,128]{2,1,0:T(8,128)(2,1)}, u32[]{:S(2)}, u32[]{:S(2)}) collective-permute-start(bf16[4,576,128]{2,1,0:T(8,128)(2,1)} %collective-permute-done.18.refs_3_), channel_id=1, source_target_pairs={{0,8},{8,0},{16,24},{24,16},{1,9},{9,1},{17,25},{25,17},{2,10},{10... | collective-permute-start | bytes 1769480 | tf_op jit(solution)/shard_map/ppermute | solution.py:31
  82.8 25.7 %collective-permute-start.21 = (bf16[4,576,128]{2,1,0:T(8,128)(2,1)}, bf16[4,576,128]{2,1,0:T(8,128)(2,1)}, u32[]{:S(2)}, u32[]{:S(2)}) collective-permute-start(bf16[4,576,128]{2,1,0:T(8,128)(2,1)} %hold.7.refs_5_), channel_id=1, source_target_pairs={{0,1},{1,0},{2,3},{3,2},{4,5},{5,4},{6,7},{7,6},{8,9},{9,8},{10,11... | collective-permute-start | bytes 1769480 | tf_op jit(solution)/shard_map/ppermute | solution.py:35
  114.0 45.9 %collective-permute-start.24 = (bf16[4,1152,128]{2,1,0:T(8,128)(2,1)}, bf16[4,1152,128]{2,1,0:T(8,128)(2,1)}, u32[]{:S(2)}, u32[]{:S(2)}) collective-permute-start(bf16[4,1152,128]{2,1,0:T(8,128)(2,1)} %stack.119.refs_9_.refs_6_.refs_1_), channel_id=1, source_target_pairs={{0,8},{8,0},{16,24},{24,16},{1,9},{9,1},{17,25},{25,17},{2,10},{10... | collective-permute-start | bytes 3538952 | tf_op jit(solution)/shard_map/ppermute | solution.py:31
  114.6 45.3 %collective-permute-start.27 = (bf16[4,1152,128]{2,1,0:T(8,128)(2,1)}, bf16[4,1152,128]{2,1,0:T(8,128)(2,1)}, u32[]{:S(2)}, u32[]{:S(2)}) collective-permute-start(bf16[4,1152,128]{2,1,0:T(8,128)(2,1)} %collective-permute-done.26.refs_5_), channel_id=1, source_target_pairs={{0,8},{8,0},{16,24},{24,16},{1,9},{9,1},{17,25},{25,17},{2,10},{10... | collective-permute-start | bytes 3538952 | tf_op jit(solution)/shard_map/ppermute | solution.py:31
  122.5 28.6 %collective-permute-start.28 = (bf16[4,1152,128]{2,1,0:T(8,128)(2,1)}, bf16[4,1152,128]{2,1,0:T(8,128)(2,1)}, u32[]{:S(2)}, u32[]{:S(2)}) collective-permute-start(bf16[4,1152,128]{2,1,0:T(8,128)(2,1)} %hold.8.refs_4_.refs_3_), channel_id=1, source_target_pairs={{0,16},{8,24},{16,0},{24,8},{1,17},{9,25},{17,1},{25,9},{2,18},{10... | collective-permute-start | bytes 3538952 | tf_op jit(solution)/shard_map/ppermute | solution.py:31
  123.0 36.9 %collective-permute-start.25 = (bf16[4,1152,128]{2,1,0:T(8,128)(2,1)}, bf16[4,1152,128]{2,1,0:T(8,128)(2,1)}, u32[]{:S(2)}, u32[]{:S(2)}) collective-permute-start(bf16[4,1152,128]{2,1,0:T(8,128)(2,1)} %hold.8.refs_4_.refs_3_), channel_id=1, source_target_pairs={{0,8},{8,0},{16,24},{24,16},{1,9},{9,1},{17,25},{25,17},{2,10},{10... | collective-permute-start | bytes 3538952 | tf_op jit(solution)/shard_map/ppermute | solution.py:31
  201.2 21.4 %collective-permute-start.30 = (bf16[8,2,128,384]{3,2,1,0:T(8,128)(2,1)S(1)}, bf16[8,2,128,384]{3,2,1,0:T(8,128)(2,1)S(1)}, u32[]{:S(2)}, u32[]{:S(2)}) collective-permute-start(bf16[8,2,128,384]{3,2,1,0:T(8,128)(2,1)S(1)} %bitcast.233), channel_id=1, source_target_pairs={{0,8},{8,0},{16,24},{24,16},{1,9},{9,1},{17,25},{25,17},{2,10},{10... | collective-permute-start | bytes 4718600 | tf_op jit(solution)/shard_map/ppermute | solution.py:31
  217.3 41.6 %collective-permute-start.33 = (bf16[4,2,48,2048]{3,2,1,0:T(8,128)(2,1)}, bf16[4,2,48,2048]{3,2,1,0:T(8,128)(2,1)}, u32[]{:S(2)}, u32[]{:S(2)}) collective-permute-start(bf16[4,2,48,2048]{3,2,1,0:T(8,128)(2,1)} %get-tuple-element.80.refs_3_.refs_4_.refs_7_), channel_id=1, source_target_pairs={{0,1},{1,0},{2,3},{3,2},{4,5},{5,4},{6,7},{7,6},{8,9},{9,8},{10,11... | collective-permute-start | bytes 4718600 | tf_op jit(solution)/shard_map/ppermute | solution.py:35
  224.9 37.9 %collective-permute-start.32 = (bf16[4,2,128,384]{3,2,1,0:T(8,128)(2,1)}, bf16[4,2,128,384]{3,2,1,0:T(8,128)(2,1)}, u32[]{:S(2)}, u32[]{:S(2)}) collective-permute-start(bf16[4,2,128,384]{3,2,1,0:T(8,128)(2,1)} %get-tuple-element.82.refs_6_), channel_id=1, source_target_pairs={{0,16},{8,24},{16,0},{24,8},{1,17},{9,25},{17,1},{25,9},{2,18},{10... | collective-permute-start | bytes 2359304 | tf_op jit(solution)/shard_map/ppermute | solution.py:31
  266.1 70.5 %collective-permute-start.34 = (bf16[4,128,384]{2,1,0:T(8,128)(2,1)}, bf16[4,128,384]{2,1,0:T(8,128)(2,1)}, u32[]{:S(2)}, u32[]{:S(2)}) collective-permute-start(bf16[4,128,384]{2,1,0:T(8,128)(2,1)} %get-tuple-element.88.refs_10_), channel_id=1, source_target_pairs={{0,1},{1,0},{2,3},{3,2},{4,5},{5,4},{6,7},{7,6},{8,9},{9,8},{10,11... | collective-permute-start | bytes 1179656 | tf_op jit(solution)/shard_map/ppermute | solution.py:35
  282.2 56.4 %collective-permute-start.44 = (bf16[48,2048]{1,0:T(8,128)(2,1)}, bf16[48,2048]{1,0:T(8,128)(2,1)}, u32[]{:S(2)}, u32[]{:S(2)}) collective-permute-start(bf16[48,2048]{1,0:T(8,128)(2,1)} %get-tuple-element.93.refs_2_.refs_8_), channel_id=1, source_target_pairs={{0,2},{1,3},{2,4},{3,5},{4,6},{5,7},{6,0},{7,1},{8,10},{9,11},{10,... | collective-permute-start | bytes 589832 | tf_op jit(solution)/shard_map/ppermute | solution.py:40
  289.0 51.1 %collective-permute-start.45 = (bf16[48,2048]{1,0:T(8,128)(2,1)}, bf16[48,2048]{1,0:T(8,128)(2,1)}, u32[]{:S(2)}, u32[]{:S(2)}) collective-permute-start(bf16[48,2048]{1,0:T(8,128)(2,1)} %get-tuple-element.94.refs_3_.refs_9_), channel_id=1, source_target_pairs={{0,4},{1,5},{2,6},{3,7},{4,0},{5,1},{6,2},{7,3},{8,12},{9,13},{10,... | collective-permute-start | bytes 589832 | tf_op jit(solution)/shard_map/ppermute | solution.py:40
  293.3 47.5 %collective-permute-start.46 = (bf16[48,2048]{1,0:T(8,128)(2,1)}, bf16[48,2048]{1,0:T(8,128)(2,1)}, u32[]{:S(2)}, u32[]{:S(2)}) collective-permute-start(bf16[48,2048]{1,0:T(8,128)(2,1)} %get-tuple-element.95.refs_4_.refs_10_), channel_id=1, source_target_pairs={{0,6},{1,7},{2,0},{3,1},{4,2},{5,3},{6,4},{7,5},{8,14},{9,15},{10,... | collective-permute-start | bytes 589832 | tf_op jit(solution)/shard_map/ppermute | solution.py:40
  295.1 33.3 %collective-permute-start.37 = (bf16[4,2,48,1920]{3,2,1,0:T(8,128)(2,1)}, bf16[4,2,48,1920]{3,2,1,0:T(8,128)(2,1)}, u32[]{:S(2)}, u32[]{:S(2)}) collective-permute-start(bf16[4,2,48,1920]{3,2,1,0:T(8,128)(2,1)} %get-tuple-element.98.refs_7_), channel_id=1, source_target_pairs={{0,16},{8,24},{16,0},{24,8},{1,17},{9,25},{17,1},{25,9},{2,18},{10... | collective-permute-start | bytes 4423688 | tf_op jit(solution)/shard_map/ppermute | solution.py:31
  332.2 29.5 %collective-permute-start.43 = (bf16[4,48,1920]{2,1,0:T(8,128)(2,1)}, bf16[4,48,1920]{2,1,0:T(8,128)(2,1)}, u32[]{:S(2)}, u32[]{:S(2)}) collective-permute-start(bf16[4,48,1920]{2,1,0:T(8,128)(2,1)} %get-tuple-element.103.refs_5_), channel_id=1, source_target_pairs={{0,1},{1,0},{2,3},{3,2},{4,5},{5,4},{6,7},{7,6},{8,9},{9,8},{10,11... | collective-permute-start | bytes 2211848 | tf_op jit(solution)/shard_map/ppermute | solution.py:35
  338.5 34.6 %collective-permute-start.38 = (bf16[128,384]{1,0:T(8,128)(2,1)}, bf16[128,384]{1,0:T(8,128)(2,1)}, u32[]{:S(2)}, u32[]{:S(2)}) collective-permute-start(bf16[128,384]{1,0:T(8,128)(2,1)} %get-tuple-element.106.refs_3_.refs_4_), channel_id=1, source_target_pairs={{0,2},{1,3},{2,4},{3,5},{4,6},{5,7},{6,0},{7,1},{8,10},{9,11},{10,... | collective-permute-start | bytes 294920 | tf_op jit(solution)/shard_map/ppermute | solution.py:40
  340.1 33.0 %collective-permute-start.39 = (bf16[128,384]{1,0:T(8,128)(2,1)}, bf16[128,384]{1,0:T(8,128)(2,1)}, u32[]{:S(2)}, u32[]{:S(2)}) collective-permute-start(bf16[128,384]{1,0:T(8,128)(2,1)} %get-tuple-element.107.refs_4_.refs_5_), channel_id=1, source_target_pairs={{0,4},{1,5},{2,6},{3,7},{4,0},{5,1},{6,2},{7,3},{8,12},{9,13},{10,... | collective-permute-start | bytes 294920 | tf_op jit(solution)/shard_map/ppermute | solution.py:40
  340.8 32.3 %collective-permute-start.40 = (bf16[128,384]{1,0:T(8,128)(2,1)}, bf16[128,384]{1,0:T(8,128)(2,1)}, u32[]{:S(2)}, u32[]{:S(2)}) collective-permute-start(bf16[128,384]{1,0:T(8,128)(2,1)} %get-tuple-element.108.refs_5_.refs_6_), channel_id=1, source_target_pairs={{0,6},{1,7},{2,0},{3,1},{4,2},{5,3},{6,4},{7,5},{8,14},{9,15},{10,... | collective-permute-start | bytes 294920 | tf_op jit(solution)/shard_map/ppermute | solution.py:40
  346.5 22.9 %collective-permute-start.42 = (bf16[4,2,48,1152]{3,2,1,0:T(8,128)(2,1)}, bf16[4,2,48,1152]{3,2,1,0:T(8,128)(2,1)}, u32[]{:S(2)}, u32[]{:S(2)}) collective-permute-start(bf16[4,2,48,1152]{3,2,1,0:T(8,128)(2,1)} %get-tuple-element.111.refs_4_), channel_id=1, source_target_pairs={{0,16},{8,24},{16,0},{24,8},{1,17},{9,25},{17,1},{25,9},{2,18},{10... | collective-permute-start | bytes 2654216 | tf_op jit(solution)/shard_map/ppermute | solution.py:31
  (195 other events, 1439.7 us)

commit v5 on v4

--- a/solution.py
+++ b/solution.py
@@ -826,13 +826,13 @@
     cross_sum.send()
     ffin_sum.send()
     dq1, dk1, dv1, diagonals = attend("backward", q1, k1, v1, lengths, row, do, lse1, ready)
-    cross_sum.step("x", dq1)
+    self_sum = stage_grads(
+        place, [normed_self], [dq1, dk1, dv1], [(0, 0), (0, 1), (0, 2)]
+    )
+    self_sum.send()
+    cross_sum.step("x", *self_sum.sent)
     cross_sum.send()
-    self_sum = stage_grads(
-        place, [normed_self], [dq1, dk1, dv1], [(0, 0), (0, 1), (0, 2)], *cross_sum.sent
-    )
-    self_sum.send()
-    ffout_sum.step("z", *self_sum.sent, cost=lasting(100))
+    ffout_sum.step("z", *cross_sum.sent, cost=lasting(100))
     ffin_sum.finish(*ffout_sum.sent)
     ffout_sum.send()
     self_sum.step("y", *ffout_sum.sent)

time: 448 us -> 447 us (level)
  starting transfers between devices: 70.3 us -> 75.4 us
    ppermute x24, starting transfers between devices: 46.4 us -> 51.9 us  [along_z(): lax.ppermute(v, 'fsdp', [(i, (i + d * self.nx) % self.fsdp) for i in rang...]
    unnamed x308 -> x314, local copies, waits for them, and re-layouts: 37.3 us -> 37.4 us
  transfers between devices with their start and end apart: 68 -> 68, of which waited for: 18 -> 20; matrix products, arithmetic and copies ran while one was open for 14% -> 13% of each run, Pallas kernels for 36% -> 36%
where the time goes in v5:
time: 447 us; the launch traced here: 440 us
  Pallas kernels  191 us (43%)
  starting transfers between devices  75.4 us (17%)
  waiting for transfers between devices  71.2 us (16%)
  local copies, waits for them, and re-layouts  50 us (11%)
  other arithmetic  29.1 us (7%)
  matrix products  20.4 us (5%)
    pallas_call x46, Pallas kernels, call(): pl.pallas_call(kernel, in_specs=list(specs or [VMEM] * count) + [pl.Block...  191 us
    ppermute x24, starting transfers between devices, along_z(): lax.ppermute(v, 'fsdp', [(i, (i + d * self.nx) % self.fsdp) for i in rang...  51.9 us
    unnamed x314, local copies, waits for them, and re-layouts  37.4 us
    ppermute x24, waiting for transfers between devices, along_z(): lax.ppermute(v, 'fsdp', [(i, (i + d * self.nx) % self.fsdp) for i in rang...  37.4 us
    ppermute x35, waiting for transfers between devices, across(): return lax.ppermute(v, 'rep', [(i, i ^ bit) for i in range(self.rep)])  26 us
    dot_general x8, matrix products, project(): return jnp.einsum('vgq,qy->vgy', a, w, preferred_element_type=jnp.float32)  15.3 us
    ppermute x35, starting transfers between devices, across(): return lax.ppermute(v, 'rep', [(i, i ^ bit) for i in range(self.rep)])  15.2 us
    convert_element_type x6, other arithmetic, low(): return v.astype(jnp.bfloat16)  11 us
  transfers between devices with their start and end apart: 68, of which 20 were waited for; matrix products, arithmetic and copies ran while one was open for 13% of the time, Pallas kernels for 36%

profile of v5, /device:TPU:0, one launch (start us, length us, event | category | flops | bytes accessed | tf_op | source)
XLA Modules:
  0.0 440.0 jit_solution(4129392563061101858)
XLA Ops:
  13.0 5.7 %collective-permute-done.1.refs_2_ = bf16[592,128]{1,0:T(8,128)(2,1)S(1)} collective-permute-done((bf16[592,128]{1,0:T(8,128)(2,1)S(1)}, bf16[592,128]{1,0:T(8,128)(2,1)S(1)}, u32[]{:S(2)}, u32[]{:S(2)}) %collective-permute-start.1) | collective-permute-done | bytes 151584 | tf_op jit(solution)/shard_map/ppermute | solution.py:40
  31.4 4.6 %collective-permute-done.6.refs_2_ = bf16[576,128]{1,0:T(8,128)(2,1)S(1)} collective-permute-done((bf16[576,128]{1,0:T(8,128)(2,1)S(1)}, bf16[576,128]{1,0:T(8,128)(2,1)S(1)}, u32[]{:S(2)}, u32[]{:S(2)}) %collective-permute-start.6) | collective-permute-done | bytes 147488 | tf_op jit(solution)/shard_map/ppermute | solution.py:40
  47.3 4.5 %collective-permute-done.13.refs_1_ = bf16[1152,128]{1,0:T(8,128)(2,1)S(1)} collective-permute-done((bf16[1152,128]{1,0:T(8,128)(2,1)S(1)}, bf16[1152,128]{1,0:T(8,128)(2,1)S(1)}, u32[]{:S(2)}, u32[]{:S(2)}) %collective-permute-start.13) | collective-permute-done | bytes 294944 | tf_op jit(solution)/shard_map/ppermute | solution.py:40
  51.7 10.4 %collective-permute-done.14.refs_2_ = bf16[1152,128]{1,0:T(8,128)(2,1)S(1)} collective-permute-done((bf16[1152,128]{1,0:T(8,128)(2,1)S(1)}, bf16[1152,128]{1,0:T(8,128)(2,1)S(1)}, u32[]{:S(2)}, u32[]{:S(2)}) %collective-permute-start.14) | collective-permute-done | bytes 294944 | tf_op jit(solution)/shard_map/ppermute | solution.py:40
  83.4 17.1 %self_forward.1 = (bf16[2,512,768]{2,1,0:T(8,128)(2,1)S(1)}, f32[2,6,2,512]{3,2,1,0:T(2,128)S(1)}) custom-call(s32[2]{0:T(128)S(1)} %copy-done.69, bf16[2,512,768]{2,1,0:T(8,128)(2,1)S(1)} %convolution_convert_fusion.6.refs_1_, bf16[2,512,768]{2,1,0:T(8,128)(2,1)S(1)} %convolution_convert_fusion.5.refs_2_, ...), custom_call_target="tpu_custom_call" | custom-call | flops 199999995904 | tf_op jit(solution)/shard_map/self_forward/pallas_call | solution.py:81
  100.7 7.8 %collective-permute-done.21.refs_7_ = bf16[4,576,128]{2,1,0:T(8,128)(2,1)} collective-permute-done((bf16[4,576,128]{2,1,0:T(8,128)(2,1)}, bf16[4,576,128]{2,1,0:T(8,128)(2,1)}, u32[]{:S(2)}, u32[]{:S(2)}) %collective-permute-start.21) | collective-permute-done | bytes 589856 | tf_op jit(solution)/shard_map/ppermute | solution.py:35
  127.5 18.8 %cross_forward.1 = (bf16[2,512,768]{2,1,0:T(8,128)(2,1)S(1)}, f32[2,6,2,512]{3,2,1,0:T(2,128)S(1)}) custom-call(s32[2]{0:T(128)S(1)} %copy-done.78, bf16[2,512,768]{2,1,0:T(8,128)(2,1)S(1)} %convolution_convert_fusion.3.refs_1_, bf16[2,512,768]{2,1,0:T(8,128)(2,1)S(1)} %fusion.10.refs_2_, bf16[2,512,768]{2,1,0:T(8,128)(2,1)S(1)} %fusion.11.refs_3_, ...), custom_call_target="tpu_custom_call" | custom-call | flops 199999995904 | tf_op jit(solution)/shard_map/cross_forward/pallas_call | solution.py:81
  146.3 4.8 %collective-permute-done.28.refs_0_ = bf16[4,1152,128]{2,1,0:T(8,128)(2,1)} collective-permute-done((bf16[4,1152,128]{2,1,0:T(8,128)(2,1)}, bf16[4,1152,128]{2,1,0:T(8,128)(2,1)}, u32[]{:S(2)}, u32[]{:S(2)}) %collective-permute-start.28) | collective-permute-done | bytes 1179680 | tf_op jit(solution)/shard_map/ppermute | solution.py:31
  159.9 6.0 %assemble.5 = (bf16[2,8,2,48,2048]{4,3,2,1,0:T(8,128)(2,1)S(1)}, bf16[1,8,2,128,768]{4,3,2,1,0:T(8,128)(2,1)S(1)}) custom-call(s32[4]{0:T(128)S(1)} %copy-done.68, bf16[4,1152,128]{2,1,0:T(8,128)(2,1)} %stack.119.refs_9_.refs_6_.refs_1_, bf16[4,1152,128]{2,1,0:T(8,128)(2,1)} %collective-permute-done.24.refs_2_, bf16[4,1152,128]{2,1,0:T(8,128)(2,1)} %hold.8.refs_4_.refs_3_, ...), custom_call_target="tpu_custom_call" | custom-call | tf_op jit(solution)/shard_map/assemble/pallas_call | solution.py:81
  166.0 15.1 %feed.1 = (bf16[1024,2048]{1,0:T(8,128)(2,1)S(1)}, bf16[1024,2048]{1,0:T(8,128)(2,1)S(1)}, bf16[1024,2048]{1,0:T(8,128)(2,1)S(1)}) custom-call(bf16[1024,768]{1,0:T(8,128)(2,1)S(1)} %bitcast.212, bf16[1024,768]{1,0:T(8,128)(2,1)S(1)} %bitcast.210, bf16[2,768,2048]{2,1,0:T(8,128)(2,1)S(1)} %bitcast.246, bf16[2048,768]{1,0:T(8,128)(2,1)S(1)} %bitcast.221), custom_call_target="tpu_custom_call" | custom-call | flops 99999997952 | tf_op jit(solution)/shard_map/feed/pallas_call | solution.py:81
  183.1 8.4 %grads.4 = (bf16[768,2048]{1,0:T(8,128)(2,1)}, f32[768,2048]{1,0:T(8,128)S(1)}) custom-call(s32[1]{0:T(128)} %bitcast.refs_0_, bf16[1024,768]{1,0:T(8,128)(2,1)S(1)} %bitcast.213, bf16[1024,2048]{1,0:T(8,128)(2,1)S(1)} %get-tuple-element.74.refs_2_.refs_0_, bf16[1024,2048]{1,0:T(8,128)(2,1)S(1)} %get-tuple-element.75.refs_3_.refs_1_), custom_call_target="tpu_custom_call" | custom-call | tf_op jit(solution)/shard_map/grads/pallas_call | solution.py:81
  209.9 7.4 %grad_normed.1 = f32[1024,768]{1,0:T(8,128)S(1)} custom-call(bf16[1024,2048]{1,0:T(8,128)(2,1)S(1)} %copy-done.29, bf16[1024,2048]{1,0:T(8,128)(2,1)S(1)} %copy-done.31, bf16[2,768,2048]{2,1,0:T(8,128)(2,1)S(1)} %bitcast.247, bf16[2,768,2048]{2,1,0:T(8,128)(2,1)S(1)} %bitcast.248, bf16[4,2,48,2048]{3,2,1,0:T(8,128)(2,1)} %get-tuple-element.80.refs_3_.refs_4_.refs_7_), custom_call_target="tpu_custom_call" | custom-call | flops 99999997952 | tf_op jit(solution)/shard_map/grad_normed/pallas_call | solution.py:81
  225.8 21.7 %cross_backward.1 = (bf16[2,512,768]{2,1,0:T(8,128)(2,1)S(1)}, bf16[2,512,768]{2,1,0:T(8,128)(2,1)S(1)}, bf16[2,512,768]{2,1,0:T(8,128)(2,1)S(1)}) custom-call(s32[2]{0:T(128)S(1)} %copy-done.79, bf16[2,512,768]{2,1,0:T(8,128)(2,1)S(1)} %copy-done.97, bf16[2,512,768]{2,1,0:T(8,128)(2,1)S(1)} %copy-done.93, bf16[2,512,768]{2,1,0:T(8,128)(2,1)S(1)} %copy-done.95, ...), custom_call_target="tpu_custom_call" | custom-call | flops 199999995904 | tf_op jit(solution)/shard_map/cross_backward/pallas_call | solution.py:81
  252.6 6.5 %fusion.34 = (bf16[2,512,768]{2,1,0:T(8,128)(2,1)S(1)}, f32[2,512,768]{2,1,0:T(8,128)}) fusion(f32[2,512,768]{2,1,0:T(8,128)} %get-tuple-element.185, f32[2,512]{1,0:T(2,128)S(1)} %multiply_multiply_fusion.1, f32[2,512]{1,0:T(2,128)S(1)} %copy-done.137, f32[2,512,768]{2,1,0:T(8,128)} %get-tuple-element.188, f32[768]{0:T(1024)S(1)} %copy-done.135, ...), kind=kLoop, calls=%fused_computation.139 | loop fusion | flops 11796480 | bytes 18900992 | tf_op jit(solution)/shard_map/convert_element_type | solution.py:46
  268.5 6.6 %grads.6 = (bf16[768,1920]{1,0:T(8,128)(2,1)S(1)}, f32[768,1920]{1,0:T(8,128)S(1)}) custom-call(s32[1]{0:T(128)} %bitcast.refs_0_, bf16[1024,768]{1,0:T(8,128)(2,1)S(1)} %bitcast.231, bf16[1024,768]{1,0:T(8,128)(2,1)S(1)} %bitcast.249, bf16[1024,768]{1,0:T(8,128)(2,1)S(1)} %bitcast.203, bf16[1024,768]{1,0:T(8,128)(2,1)S(1)} %bitcast.234, ...), custom_call_target="tpu_custom_call" | custom-call | flops 99999997952 | tf_op jit(solution)/shard_map/grads/pallas_call | solution.py:81
  275.2 6.2 %collective-permute-done.36.refs_2_ = bf16[4,48,2048]{2,1,0:T(8,128)(2,1)S(1)} collective-permute-done((bf16[4,48,2048]{2,1,0:T(8,128)(2,1)S(1)}, bf16[4,48,2048]{2,1,0:T(8,128)(2,1)S(1)}, u32[]{:S(2)}, u32[]{:S(2)}) %collective-permute-start.36) | collective-permute-done | bytes 786464 | tf_op jit(solution)/shard_map/ppermute | solution.py:31
  282.3 6.8 %collective-permute-start.44 = (bf16[48,2048]{1,0:T(8,128)(2,1)}, bf16[48,2048]{1,0:T(8,128)(2,1)}, u32[]{:S(2)}, u32[]{:S(2)}) collective-permute-start(bf16[48,2048]{1,0:T(8,128)(2,1)} %get-tuple-element.94.refs_2_.refs_8_), channel_id=1, source_target_pairs={{0,2},{1,3},{2,4},{3,5},{4,6},{5,7},{6,0},{7,1},{8,10},{9,11},{10,... | collective-permute-start | bytes 589832 | tf_op jit(solution)/shard_map/ppermute | solution.py:40
  296.5 25.9 %self_backward.1 = (bf16[2,512,768]{2,1,0:T(8,128)(2,1)S(1)}, bf16[2,512,768]{2,1,0:T(8,128)(2,1)S(1)}, bf16[2,512,768]{2,1,0:T(8,128)(2,1)S(1)}, f32[6,2,512]{2,1,0:T(2,128)S(1)}) custom-call(s32[2]{0:T(128)S(1)} %copy-done.69, bf16[2,512,768]{2,1,0:T(8,128)(2,1)S(1)} %copy-done.91, bf16[2,512,768]{2,1,0:T(8,128)(2,1)S(1)} %copy-done.89, ...), custom_call_target="tpu_custom_call" | custom-call | flops 199999995904 | tf_op jit(solution)/shard_map/self_backward/pallas_call | solution.py:81
  342.1 4.5 %encoder_grad.1 = f32[1024,768]{1,0:T(8,128)} custom-call(bf16[1024,768]{1,0:T(8,128)(2,1)S(1)} %bitcast.251, bf16[1024,768]{1,0:T(8,128)(2,1)S(1)} %bitcast.253, bf16[4,768,768]{2,1,0:T(8,128)(2,1)S(1)} %bitcast.198, bf16[4,768,768]{2,1,0:T(8,128)(2,1)S(1)} %bitcast.199, bf16[4,2,48,1152]{3,2,1,0:T(8,128)(2,1)} %get-tuple-element.111.refs_4_), custom_call_target="tpu_custom_call" | custom-call | flops 99999997952 | tf_op jit(solution)/shard_map/encoder_grad/pallas_call | solution.py:81
  348.5 4.5 %into.1 = f32[1024,768]{1,0:T(8,128)S(1)} custom-call(bf16[1024,768]{1,0:T(8,128)(2,1)S(1)} %bitcast.205, bf16[1024,768]{1,0:T(8,128)(2,1)S(1)} %bitcast.207, bf16[1024,768]{1,0:T(8,128)(2,1)S(1)} %bitcast.209, bf16[4,768,768]{2,1,0:T(8,128)(2,1)S(1)} %bitcast.188, bf16[4,768,768]{2,1,0:T(8,128)(2,1)S(1)} %bitcast.189, bf16[4,768,768]{2,1,0:T(8,128)(2,1)S(1)} %bitcast.190, ...), custom_call_target="tpu_custom_call" | custom-call | tf_op jit(solution)/shard_map/into/pallas_call | solution.py:81
  372.4 4.9 %output_state.1 = f32[1024,768]{1,0:T(8,128)} custom-call(bf16[1024,2048]{1,0:T(8,128)(2,1)S(1)} %copy-done.15, bf16[1,2048,768]{2,1,0:T(8,128)(2,1)S(1)} %bitcast.222, f32[1024,768]{1,0:T(8,128)S(1)} %bitcast.191, f32[1024,1]{1,0:T(8,128)S(1)} %bitcast.226, f32[128,384]{1,0:T(8,128)S(1)} %total.5.refs_3_.refs_4_.refs_1_, f32[96,2048]{1,0:T(8,128)} %rows.4.refs_5_), custom_call_target="tpu_custom_call" | custom-call | tf_op jit(solution)/shard_map/output_state/pallas_call | solution.py:81
  390.9 4.9 %fusion.6 = f32[2,512,768]{2,1,0:T(8,128)} fusion(f32[2,512,768]{2,1,0:T(8,128)} %get-tuple-element.139, bf16[2,512,768]{2,1,0:T(8,128)(2,1)} %param.11, f32[2,512]{1,0:T(2,128)S(1)} %multiply_multiply_fusion, f32[768]{0:T(1024)S(1)} %copy-done.123, f32[2,512]{1,0:T(2,128)S(1)} %copy-done.121, f32[1024,768]{1,0:T(8,128)S(1)} %copy-done.8), kind=kLoop, calls=%fused_computation.14 | loop fusion | flops 5505024 | bytes 11021312 | tf_op jit(solution)/shard_map/add | solution.py:860
  405.2 5.2 %collective-permute-start.65 = (f32[384]{0:T(512)S(1)}, f32[384]{0:T(512)S(1)}, u32[]{:S(2)}, u32[]{:S(2)}) collective-permute-start(f32[384]{0:T(512)S(1)} %get-tuple-element.134), channel_id=1, source_target_pairs={{0,2},{1,3},{2,4},{3,5},{4,6},{5,7},{6,0},{7,1},{8,10},{9,11},{10,... | collective-permute-start | bytes 4616 | tf_op jit(solution)/shard_map/ppermute | solution.py:40
  427.8 5.4 %collective-permute-done.57.refs_2_ = f32[48,1152]{1,0:T(8,128)S(1)} collective-permute-done((f32[48,1152]{1,0:T(8,128)S(1)}, f32[48,1152]{1,0:T(8,128)S(1)}, u32[]{:S(2)}, u32[]{:S(2)}) %collective-permute-start.57) | collective-permute-done | bytes 221216 | tf_op jit(solution)/shard_map/ppermute | solution.py:31
  (580 shorter events, 223.1 us)
Async XLA Ops:
  37.0 25.7 %collective-permute-start.11 = (bf16[4,592,128]{2,1,0:T(8,128)(2,1)S(1)}, bf16[4,592,128]{2,1,0:T(8,128)(2,1)S(1)}, u32[]{:S(2)}, u32[]{:S(2)}) collective-permute-start(bf16[4,592,128]{2,1,0:T(8,128)(2,1)S(1)} %hold.6.refs_3_), channel_id=1, source_target_pairs={{0,16},{8,24},{16,0},{24,8},{1,17},{9,25},{17,1},{25,9},{2,18},{10... | collective-permute-start | bytes 1818632 | tf_op jit(solution)/shard_map/ppermute | solution.py:31
  67.1 33.4 %collective-permute-start.17 = (bf16[4,576,128]{2,1,0:T(8,128)(2,1)}, bf16[4,576,128]{2,1,0:T(8,128)(2,1)}, u32[]{:S(2)}, u32[]{:S(2)}) collective-permute-start(bf16[4,576,128]{2,1,0:T(8,128)(2,1)} %stack.118.refs_1_), channel_id=1, source_target_pairs={{0,8},{8,0},{16,24},{24,16},{1,9},{9,1},{17,25},{25,17},{2,10},{10... | collective-permute-start | bytes 1769480 | tf_op jit(solution)/shard_map/ppermute | solution.py:31
  67.3 51.9 %collective-permute-start.23 = (bf16[4,1152,128]{2,1,0:T(8,128)(2,1)}, bf16[4,1152,128]{2,1,0:T(8,128)(2,1)}, u32[]{:S(2)}, u32[]{:S(2)}) collective-permute-start(bf16[4,1152,128]{2,1,0:T(8,128)(2,1)} %stack.119.refs_9_.refs_6_.refs_1_), channel_id=1, source_target_pairs={{0,1},{1,0},{2,3},{3,2},{4,5},{5,4},{6,7},{7,6},{8,9},{9,8},{10,11... | collective-permute-start | bytes 3538952 | tf_op jit(solution)/shard_map/ppermute | solution.py:35
  67.8 46.7 %collective-permute-start.26 = (bf16[4,1152,128]{2,1,0:T(8,128)(2,1)}, bf16[4,1152,128]{2,1,0:T(8,128)(2,1)}, u32[]{:S(2)}, u32[]{:S(2)}) collective-permute-start(bf16[4,1152,128]{2,1,0:T(8,128)(2,1)} %stack.119.refs_9_.refs_6_.refs_1_), channel_id=1, source_target_pairs={{0,16},{8,24},{16,0},{24,8},{1,17},{9,25},{17,1},{25,9},{2,18},{10... | collective-permute-start | bytes 3538952 | tf_op jit(solution)/shard_map/ppermute | solution.py:31
  68.3 45.6 %collective-permute-start.19 = (bf16[4,576,128]{2,1,0:T(8,128)(2,1)}, bf16[4,576,128]{2,1,0:T(8,128)(2,1)}, u32[]{:S(2)}, u32[]{:S(2)}) collective-permute-start(bf16[4,576,128]{2,1,0:T(8,128)(2,1)} %collective-permute-done.18.refs_3_), channel_id=1, source_target_pairs={{0,8},{8,0},{16,24},{24,16},{1,9},{9,1},{17,25},{25,17},{2,10},{10... | collective-permute-start | bytes 1769480 | tf_op jit(solution)/shard_map/ppermute | solution.py:31
  82.8 25.7 %collective-permute-start.21 = (bf16[4,576,128]{2,1,0:T(8,128)(2,1)}, bf16[4,576,128]{2,1,0:T(8,128)(2,1)}, u32[]{:S(2)}, u32[]{:S(2)}) collective-permute-start(bf16[4,576,128]{2,1,0:T(8,128)(2,1)} %hold.7.refs_5_), channel_id=1, source_target_pairs={{0,1},{1,0},{2,3},{3,2},{4,5},{5,4},{6,7},{7,6},{8,9},{9,8},{10,11... | collective-permute-start | bytes 1769480 | tf_op jit(solution)/shard_map/ppermute | solution.py:35
  114.0 45.9 %collective-permute-start.24 = (bf16[4,1152,128]{2,1,0:T(8,128)(2,1)}, bf16[4,1152,128]{2,1,0:T(8,128)(2,1)}, u32[]{:S(2)}, u32[]{:S(2)}) collective-permute-start(bf16[4,1152,128]{2,1,0:T(8,128)(2,1)} %stack.119.refs_9_.refs_6_.refs_1_), channel_id=1, source_target_pairs={{0,8},{8,0},{16,24},{24,16},{1,9},{9,1},{17,25},{25,17},{2,10},{10... | collective-permute-start | bytes 3538952 | tf_op jit(solution)/shard_map/ppermute | solution.py:31
  114.6 45.3 %collective-permute-start.27 = (bf16[4,1152,128]{2,1,0:T(8,128)(2,1)}, bf16[4,1152,128]{2,1,0:T(8,128)(2,1)}, u32[]{:S(2)}, u32[]{:S(2)}) collective-permute-start(bf16[4,1152,128]{2,1,0:T(8,128)(2,1)} %collective-permute-done.26.refs_5_), channel_id=1, source_target_pairs={{0,8},{8,0},{16,24},{24,16},{1,9},{9,1},{17,25},{25,17},{2,10},{10... | collective-permute-start | bytes 3538952 | tf_op jit(solution)/shard_map/ppermute | solution.py:31
  122.5 28.6 %collective-permute-start.28 = (bf16[4,1152,128]{2,1,0:T(8,128)(2,1)}, bf16[4,1152,128]{2,1,0:T(8,128)(2,1)}, u32[]{:S(2)}, u32[]{:S(2)}) collective-permute-start(bf16[4,1152,128]{2,1,0:T(8,128)(2,1)} %hold.8.refs_4_.refs_3_), channel_id=1, source_target_pairs={{0,16},{8,24},{16,0},{24,8},{1,17},{9,25},{17,1},{25,9},{2,18},{10... | collective-permute-start | bytes 3538952 | tf_op jit(solution)/shard_map/ppermute | solution.py:31
  123.0 36.9 %collective-permute-start.25 = (bf16[4,1152,128]{2,1,0:T(8,128)(2,1)}, bf16[4,1152,128]{2,1,0:T(8,128)(2,1)}, u32[]{:S(2)}, u32[]{:S(2)}) collective-permute-start(bf16[4,1152,128]{2,1,0:T(8,128)(2,1)} %hold.8.refs_4_.refs_3_), channel_id=1, source_target_pairs={{0,8},{8,0},{16,24},{24,16},{1,9},{9,1},{17,25},{25,17},{2,10},{10... | collective-permute-start | bytes 3538952 | tf_op jit(solution)/shard_map/ppermute | solution.py:31
  201.1 21.4 %collective-permute-start.30 = (bf16[8,2,128,384]{3,2,1,0:T(8,128)(2,1)S(1)}, bf16[8,2,128,384]{3,2,1,0:T(8,128)(2,1)S(1)}, u32[]{:S(2)}, u32[]{:S(2)}) collective-permute-start(bf16[8,2,128,384]{3,2,1,0:T(8,128)(2,1)S(1)} %bitcast.235), channel_id=1, source_target_pairs={{0,8},{8,0},{16,24},{24,16},{1,9},{9,1},{17,25},{25,17},{2,10},{10... | collective-permute-start | bytes 4718600 | tf_op jit(solution)/shard_map/ppermute | solution.py:31
  217.3 41.8 %collective-permute-start.33 = (bf16[4,2,48,2048]{3,2,1,0:T(8,128)(2,1)}, bf16[4,2,48,2048]{3,2,1,0:T(8,128)(2,1)}, u32[]{:S(2)}, u32[]{:S(2)}) collective-permute-start(bf16[4,2,48,2048]{3,2,1,0:T(8,128)(2,1)} %get-tuple-element.80.refs_3_.refs_4_.refs_7_), channel_id=1, source_target_pairs={{0,1},{1,0},{2,3},{3,2},{4,5},{5,4},{6,7},{7,6},{8,9},{9,8},{10,11... | collective-permute-start | bytes 4718600 | tf_op jit(solution)/shard_map/ppermute | solution.py:35
  224.8 38.1 %collective-permute-start.32 = (bf16[4,2,128,384]{3,2,1,0:T(8,128)(2,1)}, bf16[4,2,128,384]{3,2,1,0:T(8,128)(2,1)}, u32[]{:S(2)}, u32[]{:S(2)}) collective-permute-start(bf16[4,2,128,384]{3,2,1,0:T(8,128)(2,1)} %get-tuple-element.82.refs_6_), channel_id=1, source_target_pairs={{0,16},{8,24},{16,0},{24,8},{1,17},{9,25},{17,1},{25,9},{2,18},{10... | collective-permute-start | bytes 2359304 | tf_op jit(solution)/shard_map/ppermute | solution.py:31
  266.0 65.2 %collective-permute-start.34 = (bf16[4,128,384]{2,1,0:T(8,128)(2,1)}, bf16[4,128,384]{2,1,0:T(8,128)(2,1)}, u32[]{:S(2)}, u32[]{:S(2)}) collective-permute-start(bf16[4,128,384]{2,1,0:T(8,128)(2,1)} %get-tuple-element.88.refs_10_), channel_id=1, source_target_pairs={{0,1},{1,0},{2,3},{3,2},{4,5},{5,4},{6,7},{7,6},{8,9},{9,8},{10,11... | collective-permute-start | bytes 1179656 | tf_op jit(solution)/shard_map/ppermute | solution.py:35
  282.3 51.2 %collective-permute-start.44 = (bf16[48,2048]{1,0:T(8,128)(2,1)}, bf16[48,2048]{1,0:T(8,128)(2,1)}, u32[]{:S(2)}, u32[]{:S(2)}) collective-permute-start(bf16[48,2048]{1,0:T(8,128)(2,1)} %get-tuple-element.94.refs_2_.refs_8_), channel_id=1, source_target_pairs={{0,2},{1,3},{2,4},{3,5},{4,6},{5,7},{6,0},{7,1},{8,10},{9,11},{10,... | collective-permute-start | bytes 589832 | tf_op jit(solution)/shard_map/ppermute | solution.py:40
  289.1 46.1 %collective-permute-start.45 = (bf16[48,2048]{1,0:T(8,128)(2,1)}, bf16[48,2048]{1,0:T(8,128)(2,1)}, u32[]{:S(2)}, u32[]{:S(2)}) collective-permute-start(bf16[48,2048]{1,0:T(8,128)(2,1)} %get-tuple-element.95.refs_3_.refs_9_), channel_id=1, source_target_pairs={{0,4},{1,5},{2,6},{3,7},{4,0},{5,1},{6,2},{7,3},{8,12},{9,13},{10,... | collective-permute-start | bytes 589832 | tf_op jit(solution)/shard_map/ppermute | solution.py:40
  293.4 42.5 %collective-permute-start.46 = (bf16[48,2048]{1,0:T(8,128)(2,1)}, bf16[48,2048]{1,0:T(8,128)(2,1)}, u32[]{:S(2)}, u32[]{:S(2)}) collective-permute-start(bf16[48,2048]{1,0:T(8,128)(2,1)} %get-tuple-element.96.refs_4_.refs_10_), channel_id=1, source_target_pairs={{0,6},{1,7},{2,0},{3,1},{4,2},{5,3},{6,4},{7,5},{8,14},{9,15},{10,... | collective-permute-start | bytes 589832 | tf_op jit(solution)/shard_map/ppermute | solution.py:40
  295.3 33.3 %collective-permute-start.37 = (bf16[4,2,48,1920]{3,2,1,0:T(8,128)(2,1)}, bf16[4,2,48,1920]{3,2,1,0:T(8,128)(2,1)}, u32[]{:S(2)}, u32[]{:S(2)}) collective-permute-start(bf16[4,2,48,1920]{3,2,1,0:T(8,128)(2,1)} %get-tuple-element.98.refs_7_), channel_id=1, source_target_pairs={{0,16},{8,24},{16,0},{24,8},{1,17},{9,25},{17,1},{25,9},{2,18},{10... | collective-permute-start | bytes 4423688 | tf_op jit(solution)/shard_map/ppermute | solution.py:31
  331.2 26.8 %collective-permute-start.43 = (bf16[4,48,1920]{2,1,0:T(8,128)(2,1)}, bf16[4,48,1920]{2,1,0:T(8,128)(2,1)}, u32[]{:S(2)}, u32[]{:S(2)}) collective-permute-start(bf16[4,48,1920]{2,1,0:T(8,128)(2,1)} %get-tuple-element.104.refs_3_), channel_id=1, source_target_pairs={{0,1},{1,0},{2,3},{3,2},{4,5},{5,4},{6,7},{7,6},{8,9},{9,8},{10,11... | collective-permute-start | bytes 2211848 | tf_op jit(solution)/shard_map/ppermute | solution.py:35
  333.5 34.8 %collective-permute-start.38 = (bf16[128,384]{1,0:T(8,128)(2,1)}, bf16[128,384]{1,0:T(8,128)(2,1)}, u32[]{:S(2)}, u32[]{:S(2)}) collective-permute-start(bf16[128,384]{1,0:T(8,128)(2,1)} %get-tuple-element.106.refs_3_.refs_4_), channel_id=1, source_target_pairs={{0,2},{1,3},{2,4},{3,5},{4,6},{5,7},{6,0},{7,1},{8,10},{9,11},{10,... | collective-permute-start | bytes 294920 | tf_op jit(solution)/shard_map/ppermute | solution.py:40
  335.2 33.1 %collective-permute-start.39 = (bf16[128,384]{1,0:T(8,128)(2,1)}, bf16[128,384]{1,0:T(8,128)(2,1)}, u32[]{:S(2)}, u32[]{:S(2)}) collective-permute-start(bf16[128,384]{1,0:T(8,128)(2,1)} %get-tuple-element.107.refs_4_.refs_5_), channel_id=1, source_target_pairs={{0,4},{1,5},{2,6},{3,7},{4,0},{5,1},{6,2},{7,3},{8,12},{9,13},{10,... | collective-permute-start | bytes 294920 | tf_op jit(solution)/shard_map/ppermute | solution.py:40
  335.9 32.4 %collective-permute-start.40 = (bf16[128,384]{1,0:T(8,128)(2,1)}, bf16[128,384]{1,0:T(8,128)(2,1)}, u32[]{:S(2)}, u32[]{:S(2)}) collective-permute-start(bf16[128,384]{1,0:T(8,128)(2,1)} %get-tuple-element.108.refs_5_.refs_6_), channel_id=1, source_target_pairs={{0,6},{1,7},{2,0},{3,1},{4,2},{5,3},{6,4},{7,5},{8,14},{9,15},{10,... | collective-permute-start | bytes 294920 | tf_op jit(solution)/shard_map/ppermute | solution.py:40
  341.5 22.9 %collective-permute-start.42 = (bf16[4,2,48,1152]{3,2,1,0:T(8,128)(2,1)}, bf16[4,2,48,1152]{3,2,1,0:T(8,128)(2,1)}, u32[]{:S(2)}, u32[]{:S(2)}) collective-permute-start(bf16[4,2,48,1152]{3,2,1,0:T(8,128)(2,1)} %get-tuple-element.111.refs_4_), channel_id=1, source_target_pairs={{0,16},{8,24},{16,0},{24,8},{1,17},{9,25},{17,1},{25,9},{2,18},{10... | collective-permute-start | bytes 2654216 | tf_op jit(solution)/shard_map/ppermute | solution.py:31
  400.7 21.8 %collective-permute-start.60 = (f32[96,2048]{1,0:T(8,128)}, f32[96,2048]{1,0:T(8,128)S(1)}, u32[]{:S(2)}, u32[]{:S(2)}) collective-permute-start(f32[96,2048]{1,0:T(8,128)} %rows.4.refs_5_), channel_id=1, source_target_pairs={{0,8},{8,0},{16,24},{24,16},{1,9},{9,1},{17,25},{25,17},{2,10},{10... | collective-permute-start | bytes 2359304 | tf_op jit(solution)/shard_map/ppermute | solution.py:31
  (198 other events, 1457.5 us)
